TPU v7x, 32 devices: a whole 2x2x4 slice. The times are simulated.
32 devices in a mesh: dp: 32 (over z, y, x, core).
Axes of the slice: x: 2, y: 2, z: 4, core: 2. Of those that a mesh axis runs over, the one named last changes fastest.
Arguments:
- inputs: bfloat16 [2, 32, 64, 1152], P(None, 'dp'), may hold values from -32 to 32
- segment_ids: int32 [2, 32, 64], P(None, 'dp'), may hold values from 0 to 3, never falling along the last dimension, each value on 1 to 32 neighbouring positions
- valid_mask: int32 [2, 32, 64], P(None, 'dp'), may hold values from 0 to 1, as said below
- attn_in: bfloat16 [1536, 1152], P('dp'), may hold values from -0.1875 to 0.1875
- attn_out: bfloat16 [1024, 1152], P('dp'), may hold values from -0.1875 to 0.1875
- ffw_in: bfloat16 [13824, 1152], P('dp'), may hold values from -0.1875 to 0.1875
- ffw_out: bfloat16 [6912, 1152], P('dp'), may hold values from -0.078125 to 0.078125
- norm_gains: float32 [4, 1152], replicated, may hold values from 0.1 to 1.9
- head_gains: float32 [2, 256], replicated, may hold values from 0.1 to 1.9
- cotangent: bfloat16 [2, 32, 64, 1152], P(None, 'dp'), may hold values from -32 to 32
Outputs:
- layer_out: bfloat16 [2, 32, 64, 1152], P(None, 'dp')
- input_grad: float32 [2, 32, 64, 1152], P(None, 'dp')
- attn_in_grad: float32 [1536, 1152], P('dp')
- attn_out_grad: float32 [1024, 1152], P('dp')
- ffw_in_grad: float32 [13824, 1152], P('dp')
- ffw_out_grad: float32 [6912, 1152], P('dp')
- norm_grad: float32 [4, 1152], replicated
- head_grad: float32 [2, 256], replicated
- rms_values: float32 [4], replicated
Inputs may be any that keep to these rules, and one draw needn't show every extreme that they name: `segment_ids`: within a sequence the numbers never fall; each of the 4 documents holds 1 to 32 tokens. `valid_mask`: in each sequence the first tokens, 32 of them or more, are 1 and the rest 0.
All inputs are finite; a program needn't handle non-finite values.
Results may differ from a plain program's by a relative error of at most 0.015.
Values may be sent and summed in bfloat16 or wider, within the bound.
A program may use at most 320 MiB of HBM per device.

v0:
```python
import math

import jax
import jax.numpy as jnp
from jax import lax
from jax.sharding import PartitionSpec as P

D = 1152
HEADS = 4
HD = 256
FF = 6912
MICRO = 2


EPSILON = 1e-06
SCALE_FACTOR = 0.0625
THETA = 10000.0
NEGATIVE = -1e30


def shortened(x):

    def short(part):
        return part.astype(jnp.bfloat16) if part.dtype == jnp.float32 else part

    return jax.tree.map(short, x)


def swapped(block, axis, stride):
    count = lax.axis_size(axis)
    route = []
    for low in range(count):
        high = low | 1 << stride
        if high != low and high < count:
            route += [(low, high), (high, low)]
    return lax.ppermute(block, axis, route)


def norm_rows(values, gain):
    return values * lax.rsqrt(jnp.mean(values * values, -1, keepdims=True) + EPSILON) * gain


def rotate(values, cosine, sine):
    half = values.shape[-1] // 2
    first = values[..., :half]
    second = values[..., half:]
    return jnp.concatenate([first * cosine - second * sine, second * cosine + first * sine], -1)


def doc_tables(segments, validity, head_size):
    length = segments.shape[-1]
    places = jnp.arange(length, dtype=jnp.int32)
    same_doc = segments[..., :, None] == segments[..., None, :]
    earlier = places[None, :] < places[:, None]
    position = jnp.sum(jnp.logical_and(same_doc, earlier).astype(jnp.int32), -1)
    reach = places[None, :] <= places[:, None]
    usable = jnp.logical_or(validity[..., None, :] > 0, places[None, :] == places[:, None])
    allowed = jnp.logical_and(jnp.logical_and(same_doc, reach), usable)
    freqs = jnp.exp(
        jnp.arange(head_size // 2, dtype=jnp.float32) * (-2.0 * math.log(THETA) / head_size)
    )
    angles = position.astype(jnp.float32)[..., None] * freqs
    return (allowed, jnp.cos(angles), jnp.sin(angles))


def prepare(projected, head_gains, cosine, sine):
    width = HEADS * HD
    query = projected[..., :width].reshape(projected.shape[:-1] + (HEADS, HD))
    keys = projected[..., width : width + HD]
    values = projected[..., width + HD :]
    query = rotate(norm_rows(query, head_gains[0]), cosine[..., None, :], sine[..., None, :])
    keys = rotate(norm_rows(keys, head_gains[1]), cosine, sine)
    return (query, keys, values)


def across(left, piece):
    return lax.dot_general(
        left, piece, (((1,), (1,)), ((), ())), preferred_element_type=jnp.float32
    )


def over_rows(left, right):
    return lax.dot_general(
        left, right, (((0,), (0,)), ((), ())), preferred_element_type=jnp.float32
    )


def score_table(query_low, keys_low):
    return (
        jnp.einsum("qhd,kd->hqk", query_low, keys_low, preferred_element_type=jnp.float32)
        * SCALE_FACTOR
    )


def attend(query_low, keys_low, values_low, allowed):
    scores = score_table(query_low, keys_low)
    masked = jnp.where(allowed[None], scores, NEGATIVE)
    peak = jnp.max(masked, -1, keepdims=True)
    expo = jnp.where(allowed[None], jnp.exp(masked - peak), 0.0)
    totals = jnp.sum(expo, -1, keepdims=True)
    probs = expo / totals
    mixed = jnp.einsum(
        "hqk,kd->qhd", probs.astype(jnp.bfloat16), values_low, preferred_element_type=jnp.float32
    )
    return (mixed, peak + jnp.log(totals))


def attend_back(query_low, keys_low, values_low, allowed, log_sum, grad_low):
    scores = score_table(query_low, keys_low)
    probs = jnp.where(allowed[None], jnp.exp(scores - log_sum), 0.0)
    grad_probs = jnp.einsum("qhd,kd->hqk", grad_low, values_low, preferred_element_type=jnp.float32)
    grad_values = jnp.einsum(
        "hqk,qhd->kd", probs.astype(jnp.bfloat16), grad_low, preferred_element_type=jnp.float32
    )
    center = jnp.sum(grad_probs * probs, -1, keepdims=True)
    grad_scores = (probs * (grad_probs - center)).astype(jnp.bfloat16)
    grad_query = (
        jnp.einsum("hqk,kd->qhd", grad_scores, keys_low, preferred_element_type=jnp.float32)
        * SCALE_FACTOR
    )
    grad_keys = (
        jnp.einsum("hqk,qhd->kd", grad_scores, query_low, preferred_element_type=jnp.float32)
        * SCALE_FACTOR
    )
    return (grad_query, grad_keys, grad_values)


def gated(gate, upward):
    return jax.nn.gelu(gate, approximate=True) * upward


def shards(
    inputs,
    segment_ids,
    valid_mask,
    attn_in,
    attn_out,
    ffw_in,
    ffw_out,
    norm_gains,
    head_gains,
    cotangent,
):
    width = HEADS * HD
    kept_proj = []
    kept_normed_in = []
    kept_mixed = []
    kept_attn = []
    kept_gate = []
    kept_normed_mid = []
    kept_hidden = []
    kept_ffw = []
    gain_sums = jnp.zeros((4, D), jnp.float32)
    head_sums = jnp.zeros((2, HD), jnp.float32)
    stats = jnp.zeros((5,), jnp.float32)
    results = []
    input_grads = []
    for step in range(MICRO):
        full_in, full_out = (
            lax.all_gather(attn_in, "dp", axis=0, tiled=True),
            lax.all_gather(attn_out, "dp", axis=0, tiled=True),
        )
        full_ffin, full_ffout = (
            lax.all_gather(ffw_in, "dp", axis=0, tiled=True),
            lax.all_gather(ffw_out, "dp", axis=0, tiled=True),
        )
        stream = inputs[step, 0].astype(jnp.float32)
        length = stream.shape[0]
        allowed, cosine, sine = doc_tables(segment_ids[step, 0], valid_mask[step, 0], HD)
        normed_in = norm_rows(stream, norm_gains[0]).astype(jnp.bfloat16)
        projected = across(normed_in, full_in)
        query, keys, values = prepare(projected, head_gains, cosine, sine)
        query_low = query.astype(jnp.bfloat16)
        keys_low = keys.astype(jnp.bfloat16)
        values_low = values.astype(jnp.bfloat16)
        mixed, log_sum = attend(query_low, keys_low, values_low, allowed)
        mixed_low = mixed.reshape(length, width).astype(jnp.bfloat16)
        attn_proj = jnp.dot(mixed_low, full_out, preferred_element_type=jnp.float32)
        attn_branch = norm_rows(attn_proj, norm_gains[1])
        middle = stream + attn_branch
        normed_mid = norm_rows(middle, norm_gains[2]).astype(jnp.bfloat16)
        gate_up = across(normed_mid, full_ffin)
        gate = gate_up[:, :FF]
        upward = gate_up[:, FF:]
        hidden = gated(gate, upward).astype(jnp.bfloat16)
        ffw_proj = jnp.dot(hidden, full_ffout, preferred_element_type=jnp.float32)
        ffw_branch = norm_rows(ffw_proj, norm_gains[3])
        results.append((middle + ffw_branch).astype(jnp.bfloat16))
        weight = valid_mask[step, 0].astype(jnp.float32)
        sums = [
            jnp.sum(weight * jnp.sum(value * value, -1))
            for value in (stream, middle, attn_branch, ffw_branch)
        ]
        sums.append(jnp.sum(weight))
        stats = stats + jnp.stack(sums)
        upstream = cotangent[step, 0].astype(jnp.float32)
        _, back_ffw = jax.vjp(norm_rows, ffw_proj, norm_gains[3])
        grad_ffw_proj, gain_three = back_ffw(upstream)
        grad_ffw_low = grad_ffw_proj.astype(jnp.bfloat16)
        grad_hidden = across(grad_ffw_low, full_ffout)
        _, back_gated = jax.vjp(gated, gate, upward)
        grad_gate, grad_upward = back_gated(grad_hidden)
        grad_gate_up = jnp.concatenate([grad_gate, grad_upward], 1).astype(jnp.bfloat16)
        grad_normed_mid = jnp.dot(grad_gate_up, full_ffin, preferred_element_type=jnp.float32)
        _, back_mid = jax.vjp(norm_rows, middle, norm_gains[2])
        grad_mid_part, gain_two = back_mid(grad_normed_mid)
        grad_middle = upstream + grad_mid_part
        _, back_attn = jax.vjp(norm_rows, attn_proj, norm_gains[1])
        grad_attn_proj, gain_one = back_attn(grad_middle)
        grad_attn_low = grad_attn_proj.astype(jnp.bfloat16)
        grad_mixed = across(grad_attn_low, full_out)
        grad_mixed_low = grad_mixed.astype(jnp.bfloat16).reshape(length, HEADS, HD)
        grad_query, grad_keys, grad_values = attend_back(
            query_low, keys_low, values_low, allowed, log_sum, grad_mixed_low
        )
        _, back_prep = jax.vjp(
            lambda table, gains: prepare(table, gains, cosine, sine), projected, head_gains
        )
        grad_projected, grad_heads = back_prep((grad_query, grad_keys, grad_values))
        grad_proj_low = grad_projected.astype(jnp.bfloat16)
        grad_normed_in = jnp.dot(grad_proj_low, full_in, preferred_element_type=jnp.float32)
        _, back_in = jax.vjp(norm_rows, stream, norm_gains[0])
        grad_stream, gain_zero = back_in(grad_normed_in)
        input_grads.append(grad_middle + grad_stream)
        gain_sums = gain_sums + jnp.stack([gain_zero, gain_one, gain_two, gain_three])
        head_sums = head_sums + grad_heads
        kept_proj.append(grad_proj_low)
        kept_normed_in.append(normed_in)
        kept_mixed.append(mixed_low)
        kept_attn.append(grad_attn_low)
        kept_gate.append(grad_gate_up)
        kept_normed_mid.append(normed_mid)
        kept_hidden.append(hidden)
        kept_ffw.append(grad_ffw_low)
    pairs = [
        (jnp.concatenate(kept_proj, 0), jnp.concatenate(kept_normed_in, 0)),
        (jnp.concatenate(kept_mixed, 0), jnp.concatenate(kept_attn, 0)),
        (jnp.concatenate(kept_gate, 0), jnp.concatenate(kept_normed_mid, 0)),
        (jnp.concatenate(kept_hidden, 0), jnp.concatenate(kept_ffw, 0)),
    ]
    levels = lax.axis_size("dp").bit_length() - 1
    place = lax.axis_index("dp")
    top_bit = place >> levels - 1 & 1
    kept_parts = []
    sent_parts = []
    for left, right in pairs:
        half_cols = left.shape[1] // 2
        kept_parts.append(
            over_rows(lax.dynamic_slice_in_dim(left, top_bit * half_cols, half_cols, 1), right)
        )
        sent_parts.append(
            over_rows(
                lax.dynamic_slice_in_dim(left, (1 - top_bit) * half_cols, half_cols, 1), right
            )
        )
    current = tuple(kept_parts)
    outgoing = tuple(sent_parts)
    for level in range(levels):
        bit = levels - 1 - level
        arrived = jax.tree.map(
            lambda part, own: part.astype(own.dtype),
            swapped(shortened(outgoing), "dp", bit),
            outgoing,
        )
        current = tuple((mine + theirs for mine, theirs in zip(current, arrived)))
        if level + 1 < levels:
            next_bit = place >> bit - 1 & 1
            halves = [piece.shape[0] // 2 for piece in current]
            outgoing = tuple(
                (
                    lax.dynamic_slice_in_dim(piece, (1 - next_bit) * rows, rows, 0)
                    for piece, rows in zip(current, halves)
                )
            )
            current = tuple(
                (
                    lax.dynamic_slice_in_dim(piece, next_bit * rows, rows, 0)
                    for piece, rows in zip(current, halves)
                )
            )
    shard_in, shard_out, shard_ffin, shard_ffout = current
    gain_total, head_total, stat_total = lax.psum((gain_sums, head_sums, stats), "dp")
    rms_values = jnp.sqrt(stat_total[:4] / (stat_total[4] * D))
    layer_out = jnp.stack(results)[:, None]
    input_grad = jnp.stack(input_grads)[:, None]
    return (
        layer_out,
        input_grad,
        shard_in,
        shard_out,
        shard_ffin,
        shard_ffout,
        gain_total,
        head_total,
        rms_values,
    )


def solution(mesh):
    placed = (
        P(None, "dp", None, None),
        P(None, "dp", None),
        P(None, "dp", None),
        P("dp", None),
        P("dp", None),
        P("dp", None),
        P("dp", None),
        P(),
        P(),
        P(None, "dp", None, None),
    )
    return jax.shard_map(
        shards,
        mesh=mesh,
        in_specs=placed,
        out_specs=(
            P(None, "dp", None, None),
            P(None, "dp", None, None),
            P("dp", None),
            P("dp", None),
            P("dp", None),
            P("dp", None),
            P(),
            P(),
            P(),
        ),
        check_vma=False,
    )
```

profile of v0, /device:TPU:22, one launch (start us, length us, event | category | flops | bytes accessed | tf_op | source)
XLA Modules:
  0.0 2083.3 jit_solution(15166478304310422444)
XLA Ops:
  17.3 1.8 fusion.52
  19.2 50.6 %all-gather.5.cloned.1.call-done = bf16[1536,1152]{1,0:T(8,128)(2,1)} async-done(((bf16[48,1152]{1,0:T(8,128)(2,1)}), bf16[1536,1152]{1,0:T(8,128)(2,1)}) %all-gather.5.cloned.1.call-update) | async-done | bytes 3538960 | tf_op jit(solution)/shard_map/all_gather | solution.py:160
  69.8 3.4 fusion.207
  74.7 1.8 reshape.592
  76.4 1.7 multiply_reduce_fusion.21
  79.6 2.1 fusion.209
  83.1 1.8 reshape.593
  84.9 1.7 multiply_reduce_fusion.20
  100.2 28.3 %all-gather.7.cloned.1.call-done = bf16[1024,1152]{1,0:T(8,128)(2,1)} async-done(((bf16[32,1152]{1,0:T(8,128)(2,1)}), bf16[1024,1152]{1,0:T(8,128)(2,1)}) %all-gather.7.cloned.1.call-update) | async-done | bytes 2359312 | tf_op jit(solution)/shard_map/all_gather | solution.py:161
  128.5 2.5 multiply_reduce_fusion.14
  134.5 183.2 %all-gather.9.cloned.1.call-done = bf16[13824,1152]{1,0:T(8,128)(2,1)} async-done(((bf16[432,1152]{1,0:T(8,128)(2,1)}), bf16[13824,1152]{1,0:T(8,128)(2,1)}) %all-gather.9.cloned.1.call-update) | async-done | bytes 31850512 | tf_op jit(solution)/shard_map/all_gather | solution.py:164
  317.7 14.8 fusion.208
  332.5 1.8 copy-done.9
  335.9 93.8 %all-gather.11.cloned.1.call-done = bf16[6912,1152]{1,0:T(8,128)(2,1)} async-done(((bf16[216,1152]{1,0:T(8,128)(2,1)}), bf16[6912,1152]{1,0:T(8,128)(2,1)}) %all-gather.11.cloned.1.call-update) | async-done | bytes 15925264 | tf_op jit(solution)/shard_map/all_gather | solution.py:165
  429.7 8.8 multiply_reduce_fusion.15
  438.5 15.0 fusion.210
  454.1 9.4 multiply_reduce_fusion.12
  465.7 12.5 fusion.6
  478.2 12.5 fusion.13
  490.7 4.0 maximum_maximum_fusion
  494.7 9.4 convolution_convert_fusion
  510.2 22.4 %fusion.18 = f32[64,1152]{1,0:T(8,128)S(1)} fusion(bf16[13824,1152]{1,0:T(8,128)(2,1)} %all-gather.9.cloned.1.call-done, bf16[64,6912]{1,0:T(8,128)(2,1)} %get-tuple-element.115, bf16[64,6912]{1,0:T(8,128)(2,1)} %get-tuple-element.114), kind=kOutput, calls=%fused_computation.49 | convolution fusion | flops 2041970688 | bytes 33914880 | tf_op jit(solution)/shard_map/dot_general | solution.py:204
  532.8 13.7 multiply_reduce_fusion.6
  554.0 5.5 convolution_convert_fusion.1
  562.8 796.7 %collective-permute-done.10 = bf16[6912,1152]{1,0:T(8,128)(2,1)} collective-permute-done((bf16[6912,1152]{1,0:T(8,128)(2,1)}, bf16[6912,1152]{1,0:T(8,128)(2,1)}, u32[]{:S(2)}, u32[]{:S(2)}) %collective-permute-start.10) | collective-permute-done | bytes 15925280 | tf_op jit(solution)/shard_map/ppermute | solution.py:36
  1359.4 16.9 convert_add_fusion
  1376.4 8.7 dynamic-slice_convert_fusion
  1385.1 3.1 collective-permute-start.11
  1394.4 3.4 stack.81
  1397.9 3.3 stack.87
  1402.0 346.7 %all-reduce.18 = (f32[4,1152]{1,0:T(4,128)}, f32[2,256]{1,0:T(2,128)}, f32[5]{0:T(128)S(1)}) all-reduce(f32[4,1152]{1,0:T(4,128)S(1)} %maximum_add_fusion, f32[2,256]{1,0:T(2,128)S(1)} %add_add_fusion.12, f32[5]{0:T(128)S(1)} %add.525), channel_id=1, replica_groups=mesh['dp'=32] {'dp'}, use_global_device_ids=true, to_apply=%region_40.41 | all-reduce | flops 5125 | bytes 41000 | tf_op jit(solution)/shard_map/psum | solution.py:282
  1749.3 1.7 convolution_convert_fusion.2
  1751.0 2.2 collective-permute-start
  1754.2 1.8 convert_add_fusion.8
  1758.4 44.4 %collective-permute-done.6 = bf16[256,1152]{1,0:T(8,128)(2,1)S(1)} collective-permute-done((bf16[256,1152]{1,0:T(8,128)(2,1)S(1)}, bf16[256,1152]{1,0:T(8,128)(2,1)S(1)}, u32[]{:S(2)}, u32[]{:S(2)}) %collective-permute-start.6) | collective-permute-done | bytes 589856 | tf_op jit(solution)/shard_map/ppermute | solution.py:36
  1804.5 22.5 %collective-permute-done = bf16[768,1152]{1,0:T(8,128)(2,1)S(1)} collective-permute-done((bf16[768,1152]{1,0:T(8,128)(2,1)S(1)}, bf16[768,1152]{1,0:T(8,128)(2,1)S(1)}, u32[]{:S(2)}, u32[]{:S(2)}) %collective-permute-start) | collective-permute-done | bytes 1769504 | tf_op jit(solution)/shard_map/ppermute | solution.py:36
  1828.7 3.0 collective-permute-start.1
  1831.8 5.5 convert_add_fusion.1
  1837.7 1.7 collective-permute-start.16
  1840.4 13.9 convert_add_fusion.2
  1854.3 5.6 dynamic-slice_convert_fusion.2
  1861.3 75.9 %collective-permute-done.16 = bf16[1728,1152]{1,0:T(8,128)(2,1)} collective-permute-done((bf16[1728,1152]{1,0:T(8,128)(2,1)S(1)}, bf16[1728,1152]{1,0:T(8,128)(2,1)}, u32[]{:S(2)}, u32[]{:S(2)}) %collective-permute-start.16) | collective-permute-done | bytes 3981344 | tf_op jit(solution)/shard_map/ppermute | solution.py:36
  1937.2 6.2 convert_add_fusion.3
  1943.4 2.5 dynamic-slice_convert_fusion.3
  1950.1 2.1 collective-permute-start.2
  1953.7 46.5 %collective-permute-done.2 = bf16[192,1152]{1,0:T(8,128)(2,1)S(1)} collective-permute-done((bf16[192,1152]{1,0:T(8,128)(2,1)S(1)}, bf16[192,1152]{1,0:T(8,128)(2,1)S(1)}, u32[]{:S(2)}, u32[]{:S(2)}) %collective-permute-start.2) | collective-permute-done | bytes 442400 | tf_op jit(solution)/shard_map/ppermute | solution.py:36
  2002.3 5.1 convert_add_fusion.4
  2009.9 60.8 %collective-permute-done.3 = bf16[96,1152]{1,0:T(8,128)(2,1)S(1)} collective-permute-done((bf16[96,1152]{1,0:T(8,128)(2,1)S(1)}, bf16[96,1152]{1,0:T(8,128)(2,1)S(1)}, u32[]{:S(2)}, u32[]{:S(2)}) %collective-permute-start.3) | collective-permute-done | bytes 221216 | tf_op jit(solution)/shard_map/ppermute | solution.py:36
  (504 shorter events, 82.8 us)
Async XLA Ops:
  7.2 62.6 %all-gather.5.cloned.1.call-start = ((), (), s32[]{:S(2)}) async-start(), calls=%async_computation | async-start | bytes 3649536 | tf_op jit(solution)/shard_map/all_gather | solution.py:160
  7.9 120.6 %all-gather.7.cloned.1.call-start = ((), (), s32[]{:S(2)}) async-start(), calls=%async_computation.1 | async-start | bytes 2433024 | tf_op jit(solution)/shard_map/all_gather | solution.py:161
  8.7 309.0 %all-gather.9.cloned.1.call-start = ((), (), s32[]{:S(2)}) async-start(), calls=%async_computation.2 | async-start | bytes 32845824 | tf_op jit(solution)/shard_map/all_gather | solution.py:164
  9.4 420.3 %all-gather.11.cloned.1.call-start = ((), (), s32[]{:S(2)}) async-start(), calls=%async_computation.3 | async-start | bytes 16422912 | tf_op jit(solution)/shard_map/all_gather | solution.py:165
  15.8 54.0 %copy-start.122 = (f32[64]{0:T(128)}, f32[64]{0:T(128)S(1)}, u32[]{:S(2)}) copy-start(f32[64]{0:T(128)S(1)} %get-tuple-element.206) | copy-start | bytes 772
  15.8 54.0 %copy-start.124 = (f32[64]{0:T(128)}, f32[64]{0:T(128)S(1)}, u32[]{:S(2)}) copy-start(f32[64]{0:T(128)S(1)} %get-tuple-element.207) | copy-start | bytes 772
  504.2 855.3 %collective-permute-start.10 = (bf16[6912,1152]{1,0:T(8,128)(2,1)}, bf16[6912,1152]{1,0:T(8,128)(2,1)}, u32[]{:S(2)}, u32[]{:S(2)}) collective-permute-start(bf16[6912,1152]{1,0:T(8,128)(2,1)} %convolution_convert_fusion), channel_id=1, source_target_pairs={{0,16},{16,0},{1,17},{17,1},{2,18},{18,2},{3,19},{19,3},{4,20},{20... | collective-permute-start | bytes 47775752 | tf_op jit(solution)/shard_map/ppermute | solution.py:36
  510.2 22.5 %copy-start.28 = (bf16[64,6912]{1,0:T(8,128)(2,1)S(1)}, bf16[64,6912]{1,0:T(8,128)(2,1)}, u32[]{:S(2)}) copy-start(bf16[64,6912]{1,0:T(8,128)(2,1)} %get-tuple-element.112) | copy-start | bytes 2654212
  510.2 22.5 %copy-start.29 = (bf16[64,6912]{1,0:T(8,128)(2,1)S(1)}, bf16[64,6912]{1,0:T(8,128)(2,1)}, u32[]{:S(2)}) copy-start(bf16[64,6912]{1,0:T(8,128)(2,1)} %get-tuple-element.113) | copy-start | bytes 2654212
  510.2 22.5 %copy-start.89 = (f32[1152]{0:T(1024)S(1)}, f32[1152]{0:T(1024)}, u32[]{:S(2)}) copy-start(f32[1152]{0:T(1024)} %get-tuple-element.92) | copy-start | bytes 13828
  548.0 844.8 %copy-start.51 = (bf16[64,1152]{1,0:T(8,128)(2,1)}, bf16[64,1152]{1,0:T(8,128)(2,1)S(1)}, u32[]{:S(2)}) copy-start(bf16[64,1152]{1,0:T(8,128)(2,1)S(1)} %get-tuple-element.148) | copy-start | bytes 442372
  548.0 844.8 %copy-start.53 = (bf16[64,1152]{1,0:T(8,128)(2,1)}, bf16[64,1152]{1,0:T(8,128)(2,1)S(1)}, u32[]{:S(2)}) copy-start(bf16[64,1152]{1,0:T(8,128)(2,1)S(1)} %get-tuple-element.149) | copy-start | bytes 442372
  554.0 805.5 %copy-start.43 = (bf16[64,1152]{1,0:T(8,128)(2,1)S(1)}, bf16[64,1152]{1,0:T(8,128)(2,1)}, u32[]{:S(2)}) copy-start(bf16[64,1152]{1,0:T(8,128)(2,1)} %get-tuple-element.152) | copy-start | bytes 442372
  554.0 805.5 %copy-start.46 = (bf16[64,1152]{1,0:T(8,128)(2,1)S(1)}, bf16[64,1152]{1,0:T(8,128)(2,1)}, u32[]{:S(2)}) copy-start(bf16[64,1152]{1,0:T(8,128)(2,1)} %get-tuple-element.153) | copy-start | bytes 442372
  559.5 1272.3 %collective-permute-start.15 = (bf16[3456,1152]{1,0:T(8,128)(2,1)}, bf16[3456,1152]{1,0:T(8,128)(2,1)}, u32[]{:S(2)}, u32[]{:S(2)}) collective-permute-start(bf16[3456,1152]{1,0:T(8,128)(2,1)} %convolution_convert_fusion.1), channel_id=1, source_target_pairs={{0,16},{16,0},{1,17},{17,1},{2,18},{18,2},{3,19},{19,3},{4,20},{20... | collective-permute-start | bytes 23887880 | tf_op jit(solution)/shard_map/ppermute | solution.py:36
  1385.1 455.3 %collective-permute-start.11 = (bf16[3456,1152]{1,0:T(8,128)(2,1)}, bf16[3456,1152]{1,0:T(8,128)(2,1)}, u32[]{:S(2)}, u32[]{:S(2)}) collective-permute-start(bf16[3456,1152]{1,0:T(8,128)(2,1)} %dynamic-slice_convert_fusion), channel_id=1, source_target_pairs={{0,8},{8,0},{1,9},{9,1},{2,10},{10,2},{3,11},{11,3},{4,12},{12,4},... | collective-permute-start | bytes 23887880 | tf_op jit(solution)/shard_map/ppermute | solution.py:36
  1392.5 361.4 %copy-start.23 = (bf16[2,1,64,1152]{3,2,1,0:T(8,128)(2,1)S(1)}, bf16[2,1,64,1152]{3,2,1,0:T(8,128)(2,1)}, u32[]{:S(2)}) copy-start(bf16[2,1,64,1152]{3,2,1,0:T(8,128)(2,1)} %param.10) | copy-start | bytes 884740
  1392.5 361.4 %copy-start.37 = (f32[64,1152]{1,0:T(8,128)S(1)}, f32[64,1152]{1,0:T(8,128)}, u32[]{:S(2)}) copy-start(f32[64,1152]{1,0:T(8,128)} %copy-done.36) | copy-start | bytes 884740
  1392.5 361.4 %copy-start.39 = (f32[64,1152]{1,0:T(8,128)S(1)}, f32[64,1152]{1,0:T(8,128)}, u32[]{:S(2)}) copy-start(f32[64,1152]{1,0:T(8,128)} %copy-done.38) | copy-start | bytes 884740
  1392.5 361.4 %copy-start.66 = (f32[64,1152]{1,0:T(8,128)S(1)}, f32[64,1152]{1,0:T(8,128)}, u32[]{:S(2)}) copy-start(f32[64,1152]{1,0:T(8,128)} %get-tuple-element.201) | copy-start | bytes 884740
  1393.3 360.9 %copy-start.52 = (bf16[64,1152]{1,0:T(8,128)(2,1)S(1)}, bf16[64,1152]{1,0:T(8,128)(2,1)}, u32[]{:S(2)}) copy-start(bf16[64,1152]{1,0:T(8,128)(2,1)} %copy-done.51) | copy-start | bytes 442372
  1393.3 360.9 %copy-start.54 = (bf16[64,1152]{1,0:T(8,128)(2,1)S(1)}, bf16[64,1152]{1,0:T(8,128)(2,1)}, u32[]{:S(2)}) copy-start(bf16[64,1152]{1,0:T(8,128)(2,1)} %copy-done.53) | copy-start | bytes 442372
  1393.3 360.9 %copy-start.74 = (bf16[128,1024]{1,0:T(8,128)(2,1)S(1)}, bf16[128,1024]{1,0:T(8,128)(2,1)}, u32[]{:S(2)}) copy-start(bf16[128,1024]{1,0:T(8,128)(2,1)} %copy-done.72) | copy-start | bytes 786436
  1393.3 360.9 %collective-permute-start.5 = (bf16[512,1152]{1,0:T(8,128)(2,1)S(1)}, bf16[512,1152]{1,0:T(8,128)(2,1)}, u32[]{:S(2)}, u32[]{:S(2)}) collective-permute-start(bf16[512,1152]{1,0:T(8,128)(2,1)S(1)} %convolution_convert_fusion.3), channel_id=1, source_target_pairs={{0,16},{16,0},{1,17},{17,1},{2,18},{18,2},{3,19},{19,3},{4,20},{20... | collective-permute-start | bytes 3538952 | tf_op jit(solution)/shard_map/ppermute | solution.py:36
  1393.6 360.3 %copy-start.41 = (f32[64,1152]{1,0:T(8,128)S(1)}, f32[64,1152]{1,0:T(8,128)}, u32[]{:S(2)}) copy-start(f32[64,1152]{1,0:T(8,128)} %copy-done.40) | copy-start | bytes 884740
  1751.0 76.0 %collective-permute-start = (bf16[768,1152]{1,0:T(8,128)(2,1)S(1)}, bf16[768,1152]{1,0:T(8,128)(2,1)S(1)}, u32[]{:S(2)}, u32[]{:S(2)}) collective-permute-start(bf16[768,1152]{1,0:T(8,128)(2,1)S(1)} %convolution_convert_fusion.2), channel_id=1, source_target_pairs={{0,16},{16,0},{1,17},{17,1},{2,18},{18,2},{3,19},{19,3},{4,20},{20... | collective-permute-start | bytes 5308424 | tf_op jit(solution)/shard_map/ppermute | solution.py:36
  1756.1 46.6 %collective-permute-start.6 = (bf16[256,1152]{1,0:T(8,128)(2,1)S(1)}, bf16[256,1152]{1,0:T(8,128)(2,1)S(1)}, u32[]{:S(2)}, u32[]{:S(2)}) collective-permute-start(bf16[256,1152]{1,0:T(8,128)(2,1)S(1)} %dynamic-slice_convert_fusion.8), channel_id=1, source_target_pairs={{0,8},{8,0},{1,9},{9,1},{2,10},{10,2},{3,11},{11,3},{4,12},{12,4},... | collective-permute-start | bytes 1769480 | tf_op jit(solution)/shard_map/ppermute | solution.py:36
  1757.5 69.5 %copy-start.31 = (bf16[64,1536]{1,0:T(8,128)(2,1)S(1)}, bf16[64,1536]{1,0:T(8,128)(2,1)}, u32[]{:S(2)}) copy-start(bf16[64,1536]{1,0:T(8,128)(2,1)} %copy-done.30) | copy-start | bytes 589828
  1757.5 69.5 %copy-start.33 = (bf16[64,1536]{1,0:T(8,128)(2,1)S(1)}, bf16[64,1536]{1,0:T(8,128)(2,1)}, u32[]{:S(2)}) copy-start(bf16[64,1536]{1,0:T(8,128)(2,1)} %copy-done.32) | copy-start | bytes 589828
  1757.5 69.5 %copy-start.55 = (bf16[64,1152]{1,0:T(8,128)(2,1)S(1)}, bf16[64,1152]{1,0:T(8,128)(2,1)}, u32[]{:S(2)}) copy-start(bf16[64,1152]{1,0:T(8,128)(2,1)} %get-tuple-element.138) | copy-start | bytes 442372
  1757.5 69.5 %copy-start.56 = (bf16[64,1152]{1,0:T(8,128)(2,1)S(1)}, bf16[64,1152]{1,0:T(8,128)(2,1)}, u32[]{:S(2)}) copy-start(bf16[64,1152]{1,0:T(8,128)(2,1)} %get-tuple-element.139) | copy-start | bytes 442372
  1802.9 28.8 %copy-start.63 = (bf16[64,1152]{1,0:T(8,128)(2,1)S(1)}, bf16[64,1152]{1,0:T(8,128)(2,1)}, u32[]{:S(2)}) copy-start(bf16[64,1152]{1,0:T(8,128)(2,1)} %get-tuple-element.128) | copy-start | bytes 442372
  1803.0 28.8 %copy-start.65 = (bf16[64,1152]{1,0:T(8,128)(2,1)S(1)}, bf16[64,1152]{1,0:T(8,128)(2,1)}, u32[]{:S(2)}) copy-start(bf16[64,1152]{1,0:T(8,128)(2,1)} %get-tuple-element.135) | copy-start | bytes 442372
  1803.0 36.5 %collective-permute-start.7 = (bf16[128,1152]{1,0:T(8,128)(2,1)S(1)}, bf16[128,1152]{1,0:T(8,128)(2,1)S(1)}, u32[]{:S(2)}, u32[]{:S(2)}) collective-permute-start(bf16[128,1152]{1,0:T(8,128)(2,1)S(1)} %dynamic-slice_convert_fusion.11), channel_id=1, source_target_pairs={{0,4},{4,0},{1,5},{5,1},{2,6},{6,2},{3,7},{7,3},{8,12},{12,8},{9,1... | collective-permute-start | bytes 884744 | tf_op jit(solution)/shard_map/ppermute | solution.py:36
  1828.7 119.8 %collective-permute-start.1 = (bf16[384,1152]{1,0:T(8,128)(2,1)}, bf16[384,1152]{1,0:T(8,128)(2,1)}, u32[]{:S(2)}, u32[]{:S(2)}) collective-permute-start(bf16[384,1152]{1,0:T(8,128)(2,1)} %dynamic-slice_convert_fusion.7), channel_id=1, source_target_pairs={{0,8},{8,0},{1,9},{9,1},{2,10},{10,2},{3,11},{11,3},{4,12},{12,4},... | collective-permute-start | bytes 2654216 | tf_op jit(solution)/shard_map/ppermute | solution.py:36
  1837.7 99.5 %collective-permute-start.16 = (bf16[1728,1152]{1,0:T(8,128)(2,1)S(1)}, bf16[1728,1152]{1,0:T(8,128)(2,1)}, u32[]{:S(2)}, u32[]{:S(2)}) collective-permute-start(bf16[1728,1152]{1,0:T(8,128)(2,1)S(1)} %dynamic-slice_convert_fusion.1), channel_id=1, source_target_pairs={{0,8},{8,0},{1,9},{9,1},{2,10},{10,2},{3,11},{11,3},{4,12},{12,4},... | collective-permute-start | bytes 11943944 | tf_op jit(solution)/shard_map/ppermute | solution.py:36
  1859.9 142.4 %collective-permute-start.12 = (bf16[1728,1152]{1,0:T(8,128)(2,1)}, bf16[1728,1152]{1,0:T(8,128)(2,1)}, u32[]{:S(2)}, u32[]{:S(2)}) collective-permute-start(bf16[1728,1152]{1,0:T(8,128)(2,1)} %dynamic-slice_convert_fusion.2), channel_id=1, source_target_pairs={{0,4},{4,0},{1,5},{5,1},{2,6},{6,2},{3,7},{7,3},{8,12},{12,8},{9,1... | collective-permute-start | bytes 11943944 | tf_op jit(solution)/shard_map/ppermute | solution.py:36
  1945.9 54.4 %collective-permute-start.17 = (bf16[864,1152]{1,0:T(8,128)(2,1)S(1)}, bf16[864,1152]{1,0:T(8,128)(2,1)S(1)}, u32[]{:S(2)}, u32[]{:S(2)}) collective-permute-start(bf16[864,1152]{1,0:T(8,128)(2,1)S(1)} %dynamic-slice_convert_fusion.3), channel_id=1, source_target_pairs={{0,4},{4,0},{1,5},{5,1},{2,6},{6,2},{3,7},{7,3},{8,12},{12,8},{9,1... | collective-permute-start | bytes 5971976 | tf_op jit(solution)/shard_map/ppermute | solution.py:36
  1948.4 5.2 collective-permute-start.8
  1948.5 51.7 %copy-start.3 = (f32[1728,1152]{1,0:T(8,128)S(1)}, f32[1728,1152]{1,0:T(8,128)}, u32[]{:S(2)}) copy-start(f32[1728,1152]{1,0:T(8,128)} %convert_add_fusion.3) | copy-start | bytes 23887876
  1950.1 50.0 %collective-permute-start.2 = (bf16[192,1152]{1,0:T(8,128)(2,1)S(1)}, bf16[192,1152]{1,0:T(8,128)(2,1)S(1)}, u32[]{:S(2)}, u32[]{:S(2)}) collective-permute-start(bf16[192,1152]{1,0:T(8,128)(2,1)S(1)} %dynamic-slice_convert_fusion.10), channel_id=1, source_target_pairs={{0,4},{4,0},{1,5},{5,1},{2,6},{6,2},{3,7},{7,3},{8,12},{12,8},{9,1... | collective-permute-start | bytes 1327112 | tf_op jit(solution)/shard_map/ppermute | solution.py:36
  2000.7 70.1 %collective-permute-start.18 = (bf16[432,1152]{1,0:T(8,128)(2,1)S(1)}, bf16[432,1152]{1,0:T(8,128)(2,1)S(1)}, u32[]{:S(2)}, u32[]{:S(2)}) collective-permute-start(bf16[432,1152]{1,0:T(8,128)(2,1)S(1)} %dynamic-slice_convert_fusion.5), channel_id=1, source_target_pairs={{0,2},{2,0},{1,3},{3,1},{4,6},{6,4},{5,7},{7,5},{8,10},{10,8},{9,1... | collective-permute-start | bytes 2985992 | tf_op jit(solution)/shard_map/ppermute | solution.py:36
  2007.6 64.1 %collective-permute-start.13 = (bf16[864,1152]{1,0:T(8,128)(2,1)S(1)}, bf16[864,1152]{1,0:T(8,128)(2,1)S(1)}, u32[]{:S(2)}, u32[]{:S(2)}) collective-permute-start(bf16[864,1152]{1,0:T(8,128)(2,1)S(1)} %dynamic-slice_convert_fusion.4), channel_id=1, source_target_pairs={{0,2},{2,0},{1,3},{3,1},{4,6},{6,4},{5,7},{7,5},{8,10},{10,8},{9,1... | collective-permute-start | bytes 5971976 | tf_op jit(solution)/shard_map/ppermute | solution.py:36
  2008.3 62.4 %collective-permute-start.3 = (bf16[96,1152]{1,0:T(8,128)(2,1)S(1)}, bf16[96,1152]{1,0:T(8,128)(2,1)S(1)}, u32[]{:S(2)}, u32[]{:S(2)}) collective-permute-start(bf16[96,1152]{1,0:T(8,128)(2,1)S(1)} %dynamic-slice_convert_fusion.12), channel_id=1, source_target_pairs={{0,2},{2,0},{1,3},{3,1},{4,6},{6,4},{5,7},{7,5},{8,10},{10,8},{9,1... | collective-permute-start | bytes 663560 | tf_op jit(solution)/shard_map/ppermute | solution.py:36
  2009.8 62.5 %collective-permute-start.9 = (bf16[32,1152]{1,0:T(8,128)(2,1)S(1)}, bf16[32,1152]{1,0:T(8,128)(2,1)S(1)}, u32[]{:S(2)}, u32[]{:S(2)}) collective-permute-start(bf16[32,1152]{1,0:T(8,128)(2,1)S(1)} %dynamic-slice_convert_fusion.15), channel_id=1, source_target_pairs={{0,1},{1,0},{2,3},{3,2},{4,5},{5,4},{6,7},{7,6},{8,9},{9,8},{10,11... | collective-permute-start | bytes 221192 | tf_op jit(solution)/shard_map/ppermute | solution.py:36
  2070.8 2.2 collective-permute-start.4
  2071.2 2.5 collective-permute-start.19
  2072.2 2.6 collective-permute-start.14
  (143 other events, 710.1 us)
Sparse Core Ops, SparseCore 0:
  10.9 58.8 all-gather.4
  72.7 55.7 all-gather.6
  131.4 186.2 all-gather.8
  320.5 109.1 all-gather.10
where the time goes:
time: 2100 us; the launch traced here: 2080 us
  waiting for transfers between devices  1410 us (67%)
  blocking collectives  347 us (17%)
  matrix products  169 us (8%)
  other arithmetic  67.9 us (3%)
  local copies, waits for them, and re-layouts  50.9 us (2%)
  starting transfers between devices  24.7 us (1%)
    ppermute x20, waiting for transfers between devices, swapped(): return lax.ppermute(block, axis, route)  1050 us
    psum x1, blocking collectives, shards(): lax.psum((gain_sums, head_sums, stats), 'dp')  347 us
    all_gather x1, waiting for transfers between devices, shards(): lax.all_gather(ffw_in, 'dp', axis=0, tiled=True)  183 us
    all_gather x1, waiting for transfers between devices, shards(): lax.all_gather(ffw_out, 'dp', axis=0, tiled=True)  93.8 us
    dot_general x8, matrix products, across(): lax.dot_general(left, piece, (((1,), (1,)), ((), ())), preferred_element_...  62 us
    all_gather x1, waiting for transfers between devices, shards(): lax.all_gather(attn_in, 'dp', axis=0, tiled=True)  50.6 us
    dot_general x8, matrix products, over_rows(): lax.dot_general(left, right, (((0,), (0,)), ((), ())), preferred_element_...  42.1 us
  transfers between devices with their start and end apart: 24, of which 12 were waited for; matrix products, arithmetic and copies ran while one was open for 10% of the time, Pallas kernels for 0%

commit v1 on v0

--- a/solution.py
+++ b/solution.py
@@ -3,6 +3,8 @@
 import jax
 import jax.numpy as jnp
 from jax import lax
+from jax.experimental import pallas as pl
+from jax.experimental.pallas import tpu as pltpu
 from jax.sharding import PartitionSpec as P
 
 D = 1152
@@ -129,7 +131,7 @@
     return jax.nn.gelu(gate, approximate=True) * upward
 
 
-def shards(
+def general_shards(
     inputs,
     segment_ids,
     valid_mask,
@@ -296,6 +298,799 @@
     )
 
 
+BLOCK = 216
+PADDED = 224
+WIDE = 2 * PADDED
+MINE = 128
+VMEM_BYTES = 56 << 20
+SQRT_2_OVER_PI = math.sqrt(2.0 / math.pi)
+CUBIC = 0.044715
+MESH = pl.DeviceIdType.MESH
+
+
+def spots():
+    me = lax.axis_index("dp")
+    return me, me // 8, me // 4 % 2, me // 2 % 2, me % 2
+
+
+def at(z, y, x, c):
+    return z * 8 + y * 4 + x * 2 + c
+
+
+def z_peer(z, k):
+    if k == 0:
+        return z
+    if k == 1:
+        return z + 1 - 2 * (z % 2)
+    if k == 2:
+        return (z + 2) % 4
+    return 3 - z
+
+
+def remote(src, dst, send_sem, recv_sem, device):
+    return pltpu.make_async_remote_copy(
+        src_ref=src,
+        dst_ref=dst,
+        send_sem=send_sem,
+        recv_sem=recv_sem,
+        device_id=(device,),
+        device_id_type=MESH,
+    )
+
+
+def greet(devices):
+    barrier = pltpu.get_barrier_semaphore()
+    for device in devices:
+        pl.semaphore_signal(barrier, inc=1, device_id=(device,), device_id_type=MESH)
+    pl.semaphore_wait(barrier, len(devices))
+
+
+def greet_all(me):
+    barrier = pltpu.get_barrier_semaphore()
+
+    def one(step, carry):
+        pl.semaphore_signal(barrier, inc=1, device_id=((me + step) % 32,), device_id_type=MESH)
+        return carry
+
+    lax.fori_loop(1, 32, one, 0)
+    pl.semaphore_wait(barrier, 31)
+
+
+def weights_kernel(
+    ain, aout, gu, dn, all_in, all_out, all_gu, all_dn, local, sa, ra, sb, rb, sw, rw, sd, rd
+):
+    me, z, y, x, c = spots()
+    greet_all(me)
+    xp, yp, cp = at(z, y, 1 - x, c), at(z, 1 - y, x, c), at(z, y, x, 1 - c)
+    mine_in, mine_out = all_in.at[z, y, x, c], all_out.at[z, y, x, c]
+    keep_in = pltpu.make_async_copy(ain, mine_in, local.at[0])
+    keep_out = pltpu.make_async_copy(aout, mine_out, local.at[1])
+    keep_in.start()
+    keep_out.start()
+    sent = []
+
+    def send(src, dst, send_sem, recv_sem, device):
+        copy = remote(src, dst, send_sem, recv_sem, device)
+        copy.start()
+        sent.append(copy)
+
+    def got(block, send_sem, recv_sem):
+        remote(block, block, send_sem, recv_sem, cp).wait_recv()
+
+    for k in (1, 2, 3):
+        send(ain, mine_in, sa.at[k], ra.at[k], at(z_peer(z, k), y, x, c))
+    send(ain, mine_in, sa.at[4], ra.at[4], xp)
+    for k in (1, 2, 3):
+        send(aout, mine_out, sb.at[k], rb.at[k], at(z_peer(z, k), y, x, c))
+    send(aout, mine_out, sb.at[4], rb.at[4], yp)
+    kind, goal = z // 2, 2 * (z % 2) + x
+    down_z, down_y = 2 * (z // 2) + y, z % 2
+    moves = [
+        (
+            jnp.logical_and(goal == z, x == h),
+            gu.at[h],
+            all_gu.at[kind, h, c],
+            sw.at[h],
+            rw.at[kind],
+            at(goal, y, h, c),
+        )
+        for h in range(2)
+    ]
+    moves.append(
+        (down_y == y, dn, all_dn.at[c, x], sw.at[2], rw.at[2], at(down_z, down_y, x, c))
+    )
+    for stays, src, dst, send_sem, recv_sem, device in moves:
+
+        @pl.when(stays)
+        def _():
+            pltpu.make_async_copy(src, dst, recv_sem).start()
+
+        @pl.when(jnp.logical_not(stays))
+        def _():
+            remote(src, dst, send_sem, recv_sem, device).start()
+
+    for k in (1, 2, 3):
+        there = z_peer(z, k)
+        block = all_in.at[there, y, x, c]
+        got(block, sa.at[k], ra.at[k])
+        send(block, block, sa.at[4 + k], ra.at[4 + k], xp)
+        block = all_out.at[there, y, x, c]
+        got(block, sb.at[k], rb.at[k])
+        send(block, block, sb.at[4 + k], rb.at[4 + k], yp)
+    keep_in.wait()
+    keep_out.wait()
+    for k in range(4):
+        there = z_peer(z, k)
+        got(all_in.at[there, y, 1 - x, c], sa.at[4 + k], ra.at[4 + k])
+        pair = all_in.at[there, y, :, c]
+        send(pair, pair, sa.at[8 + k], ra.at[8 + k], yp)
+        got(all_out.at[there, 1 - y, x, c], sb.at[4 + k], rb.at[4 + k])
+        pair = all_out.at[there, :, x, c]
+        send(pair, pair, sb.at[8 + k], rb.at[8 + k], xp)
+    for t in range(2):
+        block = all_gu.at[t, x, c]
+        got(block, sw.at[t], rw.at[t])
+        send(block, block, sd.at[t], rd.at[t], xp)
+    block = all_dn.at[c, x]
+    got(block, sw.at[2], rw.at[2])
+    send(block, block, sd.at[2], rd.at[2], xp)
+    near = all_in.at[:, y, :, c]
+    send(near, near, sd.at[3], rd.at[3], cp)
+    near = all_out.at[:, :, x, c]
+    send(near, near, sd.at[4], rd.at[4], cp)
+    for k in range(4):
+        there = z_peer(z, k)
+        got(all_in.at[there, 1 - y, :, c], sa.at[8 + k], ra.at[8 + k])
+        got(all_out.at[there, :, 1 - x, c], sb.at[8 + k], rb.at[8 + k])
+    far = all_in.at[:, 1 - y, :, c]
+    send(far, far, sd.at[5], rd.at[5], cp)
+    far = all_out.at[:, :, 1 - x, c]
+    send(far, far, sd.at[6], rd.at[6], cp)
+    for t in range(2):
+        got(all_gu.at[t, 1 - x, c], sd.at[t], rd.at[t])
+    got(all_dn.at[c, 1 - x], sd.at[2], rd.at[2])
+    send(all_gu.at[:, :, c], all_gu.at[:, :, c], sd.at[7], rd.at[7], cp)
+    send(all_dn.at[c], all_dn.at[c], sd.at[8], rd.at[8], cp)
+    got(all_in.at[:, y, :, 1 - c], sd.at[3], rd.at[3])
+    got(all_out.at[:, :, x, 1 - c], sd.at[4], rd.at[4])
+    got(all_in.at[:, 1 - y, :, 1 - c], sd.at[5], rd.at[5])
+    got(all_out.at[:, :, 1 - x, 1 - c], sd.at[6], rd.at[6])
+    got(all_gu.at[:, :, 1 - c], sd.at[7], rd.at[7])
+    got(all_dn.at[1 - c], sd.at[8], rd.at[8])
+    for copy in sent:
+        copy.wait_send()
+    for stays, src, dst, send_sem, recv_sem, device in moves:
+
+        @pl.when(jnp.logical_not(stays))
+        def _():
+            remote(src, dst, send_sem, recv_sem, device).wait_send()
+
+
+def dma(count):
+    return pltpu.SemaphoreType.DMA((count,))
+
+
+def gather_weights(ain, aout, gu, dn):
+    low = jnp.bfloat16
+    any_place = pl.BlockSpec(memory_space=pl.ANY)
+    return pl.pallas_call(
+        weights_kernel,
+        out_shape=(
+            jax.ShapeDtypeStruct((4, 2, 2, 2) + ain.shape, low),
+            jax.ShapeDtypeStruct((4, 2, 2, 2) + aout.shape, low),
+            jax.ShapeDtypeStruct((2, 2, 2, PADDED, D), low),
+            jax.ShapeDtypeStruct((2, 2, PADDED, D), low),
+        ),
+        in_specs=[any_place] * 4,
+        out_specs=(any_place,) * 4,
+        scratch_shapes=[dma(2)] + [dma(12)] * 4 + [dma(3)] * 2 + [dma(9)] * 2,
+        compiler_params=pltpu.CompilerParams(
+            collective_id=1, has_side_effects=True, vmem_limit_bytes=VMEM_BYTES
+        ),
+        name="gather_weights",
+    )(ain, aout, gu, dn)
+
+
+def nt(left, right):
+    return lax.dot_general(
+        left, right, (((1,), (1,)), ((), ())), preferred_element_type=jnp.float32
+    )
+
+
+def nn(left, right):
+    return lax.dot_general(
+        left, right, (((1,), (0,)), ((), ())), preferred_element_type=jnp.float32
+    )
+
+
+def tn(left, right):
+    return lax.dot_general(
+        left, right, (((0,), (0,)), ((), ())), preferred_element_type=jnp.float32
+    )
+
+
+def moved(rows, got_all, total, pairs, buffers, sems):
+    acc, keep, send_y, recv_y, send_z, recv_z = buffers
+    gsz, grz, gsy, gry, ssy, sry, ssz, srz = sems
+    me, z, y, x, c = spots()
+    yp = at(z, 1 - y, x, c)
+    peers = [at(z_peer(z, k), y, x, c) for k in (1, 2, 3)]
+    greet(peers + [yp])
+    sent = []
+
+    def send(src, dst, send_sem, recv_sem, device):
+        copy = remote(src, dst, send_sem, recv_sem, device)
+        copy.start()
+        sent.append(copy)
+
+    for k in (1, 2, 3):
+        send(rows, got_all.at[z, y], gsz.at[k - 1], grz.at[k - 1], peers[k - 1])
+    send(rows, got_all.at[z, y], gsy.at[0], gry.at[0], yp)
+    got_all[z, y] = rows[...]
+
+    def finish(k):
+        there = z_peer(z, k)
+        remote(recv_y.at[k], recv_y.at[k], ssy.at[k], sry.at[k], yp).wait_recv()
+        if k == 0:
+            total[...] = keep[0] + recv_y[0].astype(jnp.float32)
+        else:
+            send_z[k - 1] = (keep[k] + recv_y[k].astype(jnp.float32)).astype(jnp.bfloat16)
+            send(
+                send_z.at[k - 1],
+                recv_z.at[k - 1],
+                ssz.at[k - 1],
+                srz.at[k - 1],
+                at(there, y, x, c),
+            )
+
+    for k in range(4):
+        there = z_peer(z, k)
+        if k < 3:
+            block = got_all.at[z_peer(z, k + 1), y]
+            remote(block, block, gsz.at[k], grz.at[k], yp).wait_recv()
+            send(block, block, gsy.at[k + 1], gry.at[k + 1], yp)
+        block = got_all.at[there, 1 - y]
+        remote(block, block, gsy.at[k], gry.at[k], yp).wait_recv()
+        pairs(there, acc)
+        keep[k] = acc[y]
+        send_y[k] = acc[1 - y].astype(jnp.bfloat16)
+        send(send_y.at[k], recv_y.at[k], ssy.at[k], sry.at[k], yp)
+        if k:
+            finish(k - 1)
+    return sent, finish
+
+
+def settle(total, recv_z, ssz, srz):
+    me, z, y, x, c = spots()
+    for k in (1, 2, 3):
+        block = recv_z.at[k - 1]
+        remote(block, block, ssz.at[k - 1], srz.at[k - 1], at(z, 1 - y, x, c)).wait_recv()
+        total[...] += recv_z[k - 1].astype(jnp.float32)
+
+
+def forward_kernel(
+    rows, w_gu, w_dn, total, got_all, hidden, slope_gate, slope_up, *scratch
+):
+    buffers, sems = scratch[:6], scratch[6:]
+
+    def pairs(there, acc):
+        def half(h, carry):
+            block = got_all[there].reshape(2 * MINE, D)
+            gate = nt(block, w_gu[0, h])
+            upward = nt(block, w_gu[1, h])
+            square = gate * gate
+            tanh = jnp.tanh(SQRT_2_OVER_PI * gate * (1.0 + CUBIC * square))
+            side = 0.5 * (1.0 + tanh)
+            gelu = gate * side
+            slope = side + 0.5 * gate * (1.0 - tanh * tanh) * (
+                SQRT_2_OVER_PI * (1.0 + 3.0 * CUBIC * square)
+            )
+            low = (gelu * upward).astype(jnp.bfloat16)
+            hidden[h, there] = low
+            slope_gate[h, there] = (upward * slope).astype(jnp.bfloat16)
+            slope_up[h, there] = gelu.astype(jnp.bfloat16)
+            part = nn(low, w_dn[h]).reshape(2, MINE, D)
+
+            @pl.when(h == 0)
+            def _():
+                acc[...] = part
+
+            @pl.when(h == 1)
+            def _():
+                acc[...] += part
+
+            return carry
+
+        lax.fori_loop(0, 2, half, 0)
+
+    sent, finish = moved(rows, got_all, total, pairs, buffers, sems)
+    finish(3)
+    settle(total, buffers[5], sems[6], sems[7])
+    for copy in sent:
+        copy.wait_send()
+
+
+def backward_kernel(
+    rows,
+    w_gu,
+    w_dn,
+    mids,
+    hidden,
+    slope_gate,
+    slope_up,
+    total,
+    d_gu,
+    d_dn,
+    got_all,
+    grad_gate,
+    grad_up,
+    *scratch,
+):
+    buffers, sems = scratch[:6], scratch[6:]
+
+    def pairs(there, acc):
+        def half(h, carry):
+            block = got_all[there].reshape(2 * MINE, D)
+            back = nt(block, w_dn[h])
+            gate = (back * slope_gate[h, there].astype(jnp.float32)).astype(jnp.bfloat16)
+            upward = (back * slope_up[h, there].astype(jnp.float32)).astype(jnp.bfloat16)
+            grad_gate[h, there] = gate
+            grad_up[h, there] = upward
+            part = (nn(gate, w_gu[0, h]) + nn(upward, w_gu[1, h])).reshape(2, MINE, D)
+
+            @pl.when(h == 0)
+            def _():
+                acc[...] = part
+
+            @pl.when(h == 1)
+            def _():
+                acc[...] += part
+
+            return carry
+
+        lax.fori_loop(0, 2, half, 0)
+
+    sent, finish = moved(rows, got_all, total, pairs, buffers, sems)
+    step = 128
+
+    def column(j, carry):
+        cols = pl.ds(pl.multiple_of(j * step, step), step)
+        ups = got_all[:, :, :, cols].reshape(8 * MINE, step)
+        mid = mids[:, :, :, cols].reshape(8 * MINE, step)
+        for h in range(2):
+            d_dn[h, :, cols] = tn(hidden[h].reshape(8 * MINE, WIDE), ups).astype(jnp.bfloat16)
+            d_gu[0, h, :, cols] = tn(grad_gate[h].reshape(8 * MINE, WIDE), mid).astype(jnp.bfloat16)
+            d_gu[1, h, :, cols] = tn(grad_up[h].reshape(8 * MINE, WIDE), mid).astype(jnp.bfloat16)
+        return carry
+
+    finish(3)
+    lax.fori_loop(0, D // step, column, 0)
+    settle(total, buffers[5], sems[6], sems[7])
+    for copy in sent:
+        copy.wait_send()
+
+
+def move_scratch():
+    low = jnp.bfloat16
+    return [
+        pltpu.VMEM((2, MINE, D), jnp.float32),
+        pltpu.VMEM((4, MINE, D), jnp.float32),
+        pltpu.VMEM((4, MINE, D), low),
+        pltpu.VMEM((4, MINE, D), low),
+        pltpu.VMEM((3, MINE, D), low),
+        pltpu.VMEM((3, MINE, D), low),
+    ] + [dma(3), dma(3), dma(4), dma(4), dma(4), dma(4), dma(3), dma(3)]
+
+
+def ffw_forward(rows, w_gu, w_dn):
+    low = jnp.bfloat16
+    wide = jax.ShapeDtypeStruct((2, 4, 2 * MINE, WIDE), low)
+    vmem = pl.BlockSpec(memory_space=pltpu.VMEM)
+    return pl.pallas_call(
+        forward_kernel,
+        out_shape=(
+            jax.ShapeDtypeStruct((MINE, D), jnp.float32),
+            jax.ShapeDtypeStruct((4, 2, MINE, D), low),
+            wide,
+            wide,
+            wide,
+        ),
+        in_specs=[vmem] * 3,
+        out_specs=(vmem,) * 5,
+        scratch_shapes=move_scratch(),
+        compiler_params=pltpu.CompilerParams(
+            collective_id=2, has_side_effects=True, vmem_limit_bytes=VMEM_BYTES
+        ),
+        name="ffw_forward",
+    )(rows, w_gu, w_dn)
+
+
+def ffw_backward(rows, w_gu, w_dn, mids, hidden, slope_gate, slope_up):
+    low = jnp.bfloat16
+    vmem = pl.BlockSpec(memory_space=pltpu.VMEM)
+    wide = pltpu.VMEM((2, 4, 2 * MINE, WIDE), low)
+    return pl.pallas_call(
+        backward_kernel,
+        out_shape=(
+            jax.ShapeDtypeStruct((MINE, D), jnp.float32),
+            jax.ShapeDtypeStruct((2, 2, WIDE, D), low),
+            jax.ShapeDtypeStruct((2, WIDE, D), low),
+        ),
+        in_specs=[vmem] * 7,
+        out_specs=(vmem,) * 3,
+        scratch_shapes=[pltpu.VMEM((4, 2, MINE, D), low), wide, wide] + move_scratch(),
+        compiler_params=pltpu.CompilerParams(
+            collective_id=3, has_side_effects=True, vmem_limit_bytes=VMEM_BYTES
+        ),
+        name="ffw_backward",
+    )(rows, w_gu, w_dn, mids, hidden, slope_gate, slope_up)
+
+
+def added(left, right):
+    return (left.astype(jnp.float32) + right.astype(jnp.float32)).astype(jnp.bfloat16)
+
+
+def return_kernel(
+    d_in,
+    d_out,
+    d_gu,
+    d_dn,
+    small,
+    o_in,
+    o_out,
+    o_gu,
+    o_dn,
+    o_small,
+    a0,
+    a1,
+    a2,
+    a3,
+    ta,
+    ta1,
+    ta2,
+    b0,
+    b1,
+    b2,
+    b3,
+    tb,
+    tb1,
+    tb2,
+    g0,
+    g1,
+    g2,
+    tg,
+    tg1,
+    n0,
+    n1,
+    n2,
+    tn0,
+    tn1,
+    sv,
+    ss,
+    rs,
+    sv_s,
+    sv_r,
+    so,
+    ro,
+):
+    me, z, y, x, c = spots()
+    greet_all(me)
+    xp, yp, cp = at(z, y, 1 - x, c), at(z, 1 - y, x, c), at(z, y, x, 1 - c)
+    sent = []
+
+    def send(src, dst, slot, device):
+        copy = remote(src, dst, ss.at[slot], rs.at[slot], device)
+        copy.start()
+        sent.append(copy)
+
+    def got(block, slot):
+        remote(block, block, ss.at[slot], rs.at[slot], cp).wait_recv()
+
+    def send_small(src, dst, slot, device):
+        copy = remote(src, dst, sv_s.at[slot], sv_r.at[slot], device)
+        copy.start()
+        sent.append(copy)
+
+    def got_small(slot):
+        remote(sv.at[slot], sv.at[slot], sv_s.at[slot], sv_r.at[slot], cp).wait_recv()
+
+    send_small(small, sv.at[0], 0, cp)
+    send(d_out.at[:, :, :, 1 - c], b0, 0, cp)
+    send(d_in.at[:, :, :, 1 - c], a0, 1, cp)
+    send(d_dn.at[1 - c], n0, 2, cp)
+    send(d_gu.at[:, :, 1 - c], g0, 3, cp)
+    got_small(0)
+    o_small[...] = small[...] + sv[0]
+    sv[6] = o_small[...]
+    send_small(sv.at[6], sv.at[1], 1, xp)
+
+    got(b0, 0)
+
+    def sum_out(i, carry):
+        p, q, r = i // 4, i // 2 % 2, i % 2
+        tb[p, q, r] = added(d_out[p, q, r, c], b0[p, q, r])
+        return carry
+
+    lax.fori_loop(0, 16, sum_out, 0)
+    send(tb.at[:, :, 1 - x], b1, 4, xp)
+    got(a0, 1)
+
+    def sum_in(i, carry):
+        p, q, r = i // 4, i // 2 % 2, i % 2
+        ta[p, q, r] = added(d_in[p, q, r, c], a0[p, q, r])
+        return carry
+
+    lax.fori_loop(0, 16, sum_in, 0)
+    send(ta.at[:, 1 - y], a1, 5, yp)
+    got(n0, 2)
+    for q in range(2):
+        tn0[q] = added(d_dn[c, q], n0[q])
+    send(tn0.at[1 - x], n1, 6, xp)
+    got(g0, 3)
+    for t in range(2):
+        for h in range(2):
+            tg[t, h] = added(d_gu[t, h, c], g0[t, h])
+    send(tg.at[:, 1 - x], g1, 7, xp)
+    got_small(1)
+    o_small[...] += sv[1]
+    sv[7] = o_small[...]
+    send_small(sv.at[7], sv.at[2], 2, yp)
+
+    got(b1, 4)
+
+    def sum_out1(i, carry):
+        p, q = i // 2, i % 2
+        tb1[p, q] = added(tb[p, q, x], b1[p, q])
+        return carry
+
+    lax.fori_loop(0, 8, sum_out1, 0)
+    send(tb1.at[:, 1 - y], b2, 8, yp)
+    got(a1, 5)
+
+    def sum_in1(i, carry):
+        p, q = i // 2, i % 2
+        ta1[p, q] = added(ta[p, y, q], a1[p, q])
+        return carry
+
+    lax.fori_loop(0, 8, sum_in1, 0)
+    send(ta1.at[:, 1 - x], a2, 9, xp)
+    got_small(2)
+    o_small[...] += sv[2]
+    sv[8] = o_small[...]
+    for k in (1, 2, 3):
+        send_small(sv.at[8], sv.at[2 + k], 2 + k, at(z_peer(z, k), y, x, c))
+
+    got(n1, 6)
+    tn1[...] = added(tn0[x], n1[...])
+    got(g1, 7)
+    for t in range(2):
+        tg1[t] = added(tg[t, x], g1[t])
+    home_z, home_y = 2 * (z // 2) + y, z % 2
+    source_z, source_x = z // 2, z % 2
+    moves = [
+        (home_y == y, tn1, n2, so.at[2], ro.at[2], at(home_z, home_y, x, c)),
+        (
+            jnp.logical_and(source_z == z, source_x == x),
+            tg1.at[0],
+            g2.at[x],
+            so.at[0],
+            ro.at[x],
+            at(source_z, y, source_x, c),
+        ),
+        (
+            jnp.logical_and(source_z + 2 == z, source_x == x),
+            tg1.at[1],
+            g2.at[x],
+            so.at[1],
+            ro.at[x],
+            at(source_z + 2, y, source_x, c),
+        ),
+    ]
+    for stays, src, dst, send_sem, recv_sem, device in moves:
+
+        @pl.when(stays)
+        def _():
+            pltpu.make_async_copy(src, dst, recv_sem).start()
+
+        @pl.when(jnp.logical_not(stays))
+        def _():
+            remote(src, dst, send_sem, recv_sem, device).start()
+
+    got(b2, 8)
+    for p in range(4):
+        tb2[p] = added(tb1[p, y], b2[p])
+    for k in (1, 2, 3):
+        there = z_peer(z, k)
+        send(tb2.at[there], b3.at[k - 1], 9 + k, at(there, y, x, c))
+    got(a2, 9)
+    for p in range(4):
+        ta2[p] = added(ta1[p, x], a2[p])
+    for k in (1, 2, 3):
+        there = z_peer(z, k)
+        send(ta2.at[there], a3.at[k - 1], 12 + k, at(there, y, x, c))
+    for k in (1, 2, 3):
+        got_small(2 + k)
+    first = sv[8] + sv[3]
+    second = sv[4] + sv[5]
+    o_small[...] = first + second
+
+    for k in (1, 2, 3):
+        got(b3.at[k - 1], 9 + k)
+    o_out[...] = (tb2[z].astype(jnp.float32) + b3[0].astype(jnp.float32)) + (
+        b3[1].astype(jnp.float32) + b3[2].astype(jnp.float32)
+    )
+    for k in (1, 2, 3):
+        got(a3.at[k - 1], 12 + k)
+    o_in[...] = (ta2[z].astype(jnp.float32) + a3[0].astype(jnp.float32)) + (
+        a3[1].astype(jnp.float32) + a3[2].astype(jnp.float32)
+    )
+    remote(n2, n2, so.at[2], ro.at[2], cp).wait_recv()
+    o_dn[...] = n2[...].astype(jnp.float32)
+    for h in range(2):
+        remote(g2.at[h], g2.at[h], so.at[h], ro.at[h], cp).wait_recv()
+        o_gu[h] = g2[h].astype(jnp.float32)
+    for copy in sent:
+        copy.wait_send()
+    for stays, src, dst, send_sem, recv_sem, device in moves:
+
+        @pl.when(jnp.logical_not(stays))
+        def _():
+            remote(src, dst, send_sem, recv_sem, device).wait_send()
+
+
+def return_grads(d_in, d_out, d_gu, d_dn, small):
+    low = jnp.bfloat16
+    f32 = jnp.float32
+    vmem = pl.BlockSpec(memory_space=pltpu.VMEM)
+
+    def leg(*lead):
+        return pltpu.VMEM(lead + (D,), low)
+
+    scratch = []
+    for rows in (48, 32):
+        scratch += [leg(4, 2, 2, rows), leg(4, 2, rows), leg(4, rows), leg(3, rows)]
+        scratch += [leg(4, 2, 2, rows), leg(4, 2, rows), leg(4, rows)]
+    scratch += [leg(2, 2, PADDED), leg(2, PADDED), leg(2, PADDED)]
+    scratch += [leg(2, 2, PADDED), leg(2, PADDED)]
+    scratch += [leg(2, PADDED), leg(PADDED), leg(PADDED)]
+    scratch += [leg(2, PADDED), leg(PADDED)]
+    scratch += [pltpu.VMEM((9,) + small.shape, f32)]
+    scratch += [dma(16), dma(16), dma(6), dma(6), dma(3), dma(3)]
+    return pl.pallas_call(
+        return_kernel,
+        out_shape=(
+            jax.ShapeDtypeStruct((48, D), f32),
+            jax.ShapeDtypeStruct((32, D), f32),
+            jax.ShapeDtypeStruct((2, PADDED, D), f32),
+            jax.ShapeDtypeStruct((PADDED, D), f32),
+            jax.ShapeDtypeStruct(small.shape, f32),
+        ),
+        in_specs=[vmem] * 5,
+        out_specs=(vmem,) * 5,
+        scratch_shapes=scratch,
+        compiler_params=pltpu.CompilerParams(
+            collective_id=4, has_side_effects=True, vmem_limit_bytes=VMEM_BYTES
+        ),
+        name="return_grads",
+    )(d_in, d_out, d_gu, d_dn, small)
+
+
+def padded_rows(rows):
+    return jnp.pad(rows, ((0, 0), (0, PADDED - BLOCK), (0, 0)))
+
+
+def split_shards(
+    inputs,
+    segment_ids,
+    valid_mask,
+    attn_in,
+    attn_out,
+    ffw_in,
+    ffw_out,
+    norm_gains,
+    head_gains,
+    cotangent,
+):
+    width = HEADS * HD
+    length = inputs.shape[2]
+    rows = MICRO * length
+    all_in, all_out, all_gu, all_dn = gather_weights(
+        attn_in,
+        attn_out,
+        padded_rows(ffw_in.reshape(2, BLOCK, D)),
+        padded_rows(ffw_out.reshape(1, BLOCK, D))[0],
+    )
+    full_in = all_in.reshape(width + 2 * HD, D)
+    full_out = all_out.reshape(width, D)
+    w_gu = all_gu.reshape(2, 2, WIDE, D)
+    w_dn = all_dn.reshape(2, WIDE, D)
+    stream = inputs.reshape(rows, D).astype(jnp.float32)
+    upstream = cotangent.reshape(rows, D).astype(jnp.float32)
+    allowed, cosine, sine = doc_tables(segment_ids[:, 0], valid_mask[:, 0], HD)
+    cosine, sine = cosine.reshape(rows, -1), sine.reshape(rows, -1)
+    normed_in = norm_rows(stream, norm_gains[0]).astype(jnp.bfloat16)
+    projected = across(normed_in, full_in)
+    query, keys, values = prepare(projected, head_gains, cosine, sine)
+    query_low = query.astype(jnp.bfloat16).reshape(MICRO, length, HEADS, HD)
+    keys_low = keys.astype(jnp.bfloat16).reshape(MICRO, length, HD)
+    values_low = values.astype(jnp.bfloat16).reshape(MICRO, length, HD)
+    mixed, log_sum = jax.vmap(attend)(query_low, keys_low, values_low, allowed)
+    mixed_low = mixed.reshape(rows, width).astype(jnp.bfloat16)
+    attn_proj = jnp.dot(mixed_low, full_out, preferred_element_type=jnp.float32)
+    attn_branch = norm_rows(attn_proj, norm_gains[1])
+    middle = stream + attn_branch
+    normed_mid = norm_rows(middle, norm_gains[2]).astype(jnp.bfloat16)
+    ffw_proj, mids, hidden, slope_gate, slope_up = ffw_forward(normed_mid, w_gu, w_dn)
+    ffw_branch = norm_rows(ffw_proj, norm_gains[3])
+    layer_out = (middle + ffw_branch).astype(jnp.bfloat16)
+    weight = valid_mask.reshape(rows).astype(jnp.float32)
+    sums = [
+        jnp.sum(weight * jnp.sum(value * value, -1))
+        for value in (stream, middle, attn_branch, ffw_branch)
+    ]
+    sums.append(jnp.sum(weight))
+    _, back_ffw = jax.vjp(norm_rows, ffw_proj, norm_gains[3])
+    grad_ffw_proj, gain_three = back_ffw(upstream)
+    grad_normed_mid, d_gu, d_dn = ffw_backward(
+        grad_ffw_proj.astype(jnp.bfloat16), w_gu, w_dn, mids, hidden, slope_gate, slope_up
+    )
+    _, back_mid = jax.vjp(norm_rows, middle, norm_gains[2])
+    grad_mid_part, gain_two = back_mid(grad_normed_mid)
+    grad_middle = upstream + grad_mid_part
+    _, back_attn = jax.vjp(norm_rows, attn_proj, norm_gains[1])
+    grad_attn_proj, gain_one = back_attn(grad_middle)
+    grad_attn_low = grad_attn_proj.astype(jnp.bfloat16)
+    grad_mixed = across(grad_attn_low, full_out)
+    grad_mixed_low = grad_mixed.astype(jnp.bfloat16).reshape(MICRO, length, HEADS, HD)
+    grad_query, grad_keys, grad_values = jax.vmap(attend_back)(
+        query_low, keys_low, values_low, allowed, log_sum, grad_mixed_low
+    )
+    _, back_prep = jax.vjp(
+        lambda table, gains: prepare(table, gains, cosine, sine), projected, head_gains
+    )
+    grad_projected, grad_heads = back_prep(
+        (
+            grad_query.reshape(rows, HEADS, HD),
+            grad_keys.reshape(rows, HD),
+            grad_values.reshape(rows, HD),
+        )
+    )
+    grad_proj_low = grad_projected.astype(jnp.bfloat16)
+    d_in = over_rows(grad_proj_low, normed_in).astype(jnp.bfloat16)
+    d_out = over_rows(mixed_low, grad_attn_low).astype(jnp.bfloat16)
+    grad_normed_in = jnp.dot(grad_proj_low, full_in, preferred_element_type=jnp.float32)
+    _, back_in = jax.vjp(norm_rows, stream, norm_gains[0])
+    grad_stream, gain_zero = back_in(grad_normed_in)
+    input_grad = grad_middle + grad_stream
+    flat = jnp.concatenate(
+        [gain_zero, gain_one, gain_two, gain_three, grad_heads.reshape(-1), jnp.stack(sums)]
+    )
+    small = jnp.pad(flat, (0, 48 * 128 - flat.shape[0])).reshape(48, 128)
+    shard_in, shard_out, shard_gu, shard_dn, small = return_grads(
+        d_in.reshape(4, 2, 2, 2, 48, D),
+        d_out.reshape(4, 2, 2, 2, 32, D),
+        d_gu.reshape(2, 2, 2, PADDED, D),
+        d_dn.reshape(2, 2, PADDED, D),
+        small,
+    )
+    flat = small.reshape(-1)
+    gain_total = flat[: 4 * D].reshape(4, D)
+    head_total = flat[4 * D : 4 * D + 2 * HD].reshape(2, HD)
+    stat_total = flat[4 * D + 2 * HD : 4 * D + 2 * HD + 5]
+    rms_values = jnp.sqrt(stat_total[:4] / (stat_total[4] * D))
+    return (
+        layer_out.reshape(inputs.shape),
+        input_grad.reshape(inputs.shape),
+        shard_in,
+        shard_out,
+        shard_gu[:, :BLOCK].reshape(2 * BLOCK, D),
+        shard_dn[:BLOCK],
+        gain_total,
+        head_total,
+        rms_values,
+    )
+
+
 def solution(mesh):
     placed = (
         P(None, "dp", None, None),
@@ -310,7 +1105,7 @@
         P(None, "dp", None, None),
     )
     return jax.shard_map(
-        shards,
+        split_shards if mesh.shape["dp"] == 32 else general_shards,
         mesh=mesh,
         in_specs=placed,
         out_specs=(

time: 2100 us -> 442 us (0.21)
  waiting for transfers between devices: 1410 us -> 0 us
  Pallas kernels: 0 us -> 366 us
  blocking collectives: 347 us -> 0 us
  matrix products: 169 us -> 14.6 us
  other arithmetic: 67.9 us -> 26.5 us
  starting transfers between devices: 24.7 us -> 0 us
  local copies, waits for them, and re-layouts: 50.9 us -> 29.2 us
    ppermute x20 -> x0, waiting for transfers between devices: 1050 us -> none  [swapped(): return lax.ppermute(block, axis, route)]
    pallas_call x0 -> x4, Pallas kernels: none -> 366 us  [the longest x1 104 us: return_grads(): pl.pallas_call(return_kernel, out_shape=(jax.ShapeDtypeStruct((48, D), f3...]
    all_gather x4 -> x0, waiting for transfers between devices: 356 us -> none  [the longest x1 183 us: shards(): lax.all_gather(ffw_in, 'dp', axis=0, tiled=True)]
    psum x1 -> x0, blocking collectives: 347 us -> none  [shards(): lax.psum((gain_sums, head_sums, stats), 'dp')]
    dot_general x8 -> x2, matrix products: 59.7 us -> 1.43 us  [the longest x1 0.83 us: split_shards(): jnp.dot(grad_proj_low, full_in, preferred_element_type=jnp.float32)]
    dot_general x8 -> x2, matrix products: 62 us -> 4.84 us  [across(): lax.dot_general(left, piece, (((1,), (1,)), ((), ())), preferred_element_...]
    dot_general x8 -> x2, matrix products: 42.1 us -> 5.21 us  [over_rows(): lax.dot_general(left, right, (((0,), (0,)), ((), ())), preferred_element_...]
    add x19 -> x1, other arithmetic: 33.6 us -> 0.01 us  [norm_rows(): jnp.mean(values * values, -1, keepdims=True) + EPSILON]
  transfers between devices with their start and end apart: 24 -> 0, of which waited for: 12 -> 0; matrix products, arithmetic and copies ran while one was open for 10% -> 0% of each run, Pallas kernels for 0% -> 0%
where the time goes in v1:
time: 442 us; the launch traced here: 438 us
  Pallas kernels  366 us (83%)
  local copies, waits for them, and re-layouts  29.2 us (7%)
  other arithmetic  26.5 us (6%)
  matrix products  14.6 us (3%)
    pallas_call x1, Pallas kernels, return_grads(): pl.pallas_call(return_kernel, out_shape=(jax.ShapeDtypeStruct((48, D), f3...  104 us
    pallas_call x1, Pallas kernels, gather_weights(): pl.pallas_call(weights_kernel, out_shape=(jax.ShapeDtypeStruct((4, 2, 2,...  96.7 us
    pallas_call x1, Pallas kernels, ffw_forward(): pl.pallas_call(forward_kernel, out_shape=(jax.ShapeDtypeStruct((MINE, D),...  82.7 us
    pallas_call x1, Pallas kernels, ffw_backward(): pl.pallas_call(backward_kernel, out_shape=(jax.ShapeDtypeStruct((MINE, D)...  82.4 us

profile of v1, /device:TPU:22, one launch (start us, length us, event | category | flops | bytes accessed | tf_op | source)
XLA Modules:
  0.0 438.4 jit_solution(12551145144185464222)
XLA Ops:
  0.7 1.2 fusion.15
  1.9 0.7 broadcast_compare_fusion
  3.2 0.8 fusion.67
  4.0 0.9 convert_reduce_fusion
  5.0 0.9 fusion.52
  5.8 1.5 slice_reduce_fusion
  7.3 1.1 fusion.17
  8.5 1.9 pad_bitcast_fusion.dn
  10.3 1.0 pad.39.gu
  11.4 96.7 %gather_weights.1 = (bf16[4,2,2,2,48,1152]{5,4,3,2,1,0:T(8,128)(2,1)}, bf16[4,2,2,2,32,1152]{5,4,3,2,1,0:T(8,128)(2,1)}, bf16[2,2,2,224,1152]{4,3,2,1,0:T(8,128)(2,1)}, bf16[2,2,224,1152]{3,2,1,0:T(8,128)(2,1)}) custom-call(bf16[48,1152]{1,0:T(8,128)(2,1)} %ain.1, bf16[32,1152]{1,0:T(8,128)(2,1)} %aout.1, bf16[2,224,1152]{2,1,0:T(8,128)(2,1)} %pad.39.gu, ...), custom_call_target="tpu_custom_call" | custom-call | tf_op jit(solution)/shard_map/gather_weights/pallas_call | solution.py:476
  108.1 3.2 fusion.68
  118.7 1.2 reduce_sum.300
  119.9 1.5 multiply_convert_fusion.rows
  121.5 82.7 %ffw_forward.1 = (f32[128,1152]{1,0:T(8,128)}, bf16[4,2,128,1152]{3,2,1,0:T(8,128)(2,1)}, bf16[2,4,256,448]{3,2,1,0:T(8,128)(2,1)}, bf16[2,4,256,448]{3,2,1,0:T(8,128)(2,1)}, bf16[2,4,256,448]{3,2,1,0:T(8,128)(2,1)}) custom-call(bf16[128,1152]{1,0:T(8,128)(2,1)} %multiply_convert_fusion.rows, bf16[2,2,448,1152]{3,2,1,0:T(8,128)(2,1)} %bitcast.142, ...), custom_call_target="tpu_custom_call" | custom-call | tf_op jit(solution)/shard_map/ffw_forward/pallas_call | solution.py:689
  204.2 1.2 multiply_reduce_fusion.6
  205.4 2.0 fusion.10
  207.4 2.2 fusion.7
  209.5 82.4 %ffw_backward.1 = (f32[128,1152]{1,0:T(8,128)}, bf16[2,2,448,1152]{3,2,1,0:T(8,128)(2,1)}, bf16[2,448,1152]{2,1,0:T(8,128)(2,1)}) custom-call(bf16[128,1152]{1,0:T(8,128)(2,1)} %get-tuple-element.118.rows, bf16[2,2,448,1152]{3,2,1,0:T(8,128)(2,1)} %bitcast.143, bf16[2,448,1152]{2,1,0:T(8,128)(2,1)} %bitcast.152, ...), custom_call_target="tpu_custom_call" | custom-call | tf_op jit(solution)/shard_map/ffw_backward/pallas_call | solution.py:712
  292.0 1.3 reduce_sum.309
  293.3 1.9 multiply_reduce_fusion.2
  295.2 0.6 multiply_multiply_fusion.5
  295.8 2.4 multiply_reduce_fusion.3
  298.3 0.8 copy-done.3
  299.2 1.6 convolution_convert_fusion.2
  300.9 1.2 reshape.368
  302.1 0.7 reduce_sum.303
  302.8 1.4 convert_reduce_fusion.1
  304.2 0.9 fusion.25
  305.1 1.2 multiply_reduce_fusion.11
  306.3 0.8 multiply_convert_fusion.1
  307.7 1.0 multiply_reduce_fusion.12
  308.8 1.0 add_add_fusion.5
  311.1 1.1 copy-done.8
  312.3 0.8 fusion.14
  313.2 3.3 concatenate.27
  317.1 1.1 fusion.13
  318.2 2.3 convolution_convert_fusion.1
  320.5 2.9 convolution_convert_fusion
  323.4 104.2 %return_grads.1 = (f32[48,1152]{1,0:T(8,128)}, f32[32,1152]{1,0:T(8,128)}, f32[2,224,1152]{2,1,0:T(8,128)}, f32[224,1152]{1,0:T(8,128)}, f32[48,128]{1,0:T(8,128)}) custom-call(bf16[4,2,2,2,48,1152]{5,4,3,2,1,0:T(8,128)(2,1)} %bitcast.144, bf16[4,2,2,2,32,1152]{5,4,3,2,1,0:T(8,128)(2,1)} %bitcast.150, bf16[2,2,2,224,1152]{4,3,2,1,0:T(8,128)(2,1)} %bitcast.153, ...), custom_call_target="tpu_custom_call" | custom-call | tf_op jit(solution)/shard_map/return_grads/pallas_call | solution.py:959
  427.6 1.4 slice.98
  429.6 1.2 fusion.55
  430.8 0.7 slice.87
  431.5 0.7 slice.86
  432.2 0.6 reshape.382
  433.4 2.2 slice.85
  435.7 1.4 slice.84
  437.1 0.7 copy.125
  437.8 0.7 copy.126
  (176 shorter events, 11.1 us)
Async XLA Ops:
  0.6 9.7 %copy-start.15 = (bf16[432,1152]{1,0:T(8,128)(2,1)S(1)}, bf16[432,1152]{1,0:T(8,128)(2,1)}, u32[]{:S(2)}) copy-start(bf16[432,1152]{1,0:T(8,128)(2,1)} %param.15) | copy-start | bytes 2985988
  0.7 110.9 %copy-start.52 = (f32[128]{0:T(128)}, f32[128]{0:T(128)S(1)}, u32[]{:S(2)}) copy-start(f32[128]{0:T(128)S(1)} %multiply_exponential_fusion) | copy-start | bytes 1540
  1.9 2.1 copy-start.47
  2.6 105.4 %copy-start.62 = (f32[128]{0:T(128)}, f32[128]{0:T(128)S(1)}, u32[]{:S(2)}) copy-start(f32[128]{0:T(128)S(1)} %add.132) | copy-start | bytes 1540
  4.0 107.5 %copy-start.43 = (f32[1,256]{1,0:T(1,128)}, f32[1,256]{1,0:T(1,128)S(1)}, u32[]{:S(2)}) copy-start(f32[1,256]{1,0:T(1,128)S(1)} %get-tuple-element.126) | copy-start | bytes 3076
  4.0 108.8 %copy-start.45 = (f32[1,256]{1,0:T(1,128)}, f32[1,256]{1,0:T(1,128)S(1)}, u32[]{:S(2)}) copy-start(f32[1,256]{1,0:T(1,128)S(1)} %get-tuple-element.127) | copy-start | bytes 3076
  4.9 106.7 %copy-start.54 = (f32[128]{0:T(128)}, f32[128]{0:T(128)S(1)}, u32[]{:S(2)}) copy-start(f32[128]{0:T(128)S(1)} %convert_element_type.107) | copy-start | bytes 1540
  7.3 100.7 %copy-start.33 = (f32[1152]{0:T(1024)}, f32[1152]{0:T(1024)S(1)}, u32[]{:S(2)}) copy-start(f32[1152]{0:T(1024)S(1)} %get-tuple-element.104) | copy-start | bytes 13828
  111.5 3.7 copy-start.18
  111.9 2.2 copy-start.16
  112.0 2.2 copy-start.29
  112.0 2.2 copy-start.31
  114.1 1.9 copy-start
  114.2 2.3 copy-start.25
  115.5 1.9 copy-start.5
  115.5 1.9 copy-start.21
  115.7 1.9 copy-start.12
  121.5 83.9 %copy-start.9 = (bf16[2,1,64,1152]{3,2,1,0:T(8,128)(2,1)S(1)}, bf16[2,1,64,1152]{3,2,1,0:T(8,128)(2,1)}, u32[]{:S(2)}) copy-start(bf16[2,1,64,1152]{3,2,1,0:T(8,128)(2,1)} %param.19) | copy-start | bytes 884740
  121.5 83.9 %copy-start.35 = (f32[1152]{0:T(1024)S(1)}, f32[1152]{0:T(1024)}, u32[]{:S(2)}) copy-start(f32[1152]{0:T(1024)} %get-tuple-element.102) | copy-start | bytes 13828
  293.3 5.0 %copy-start.61 = (f32[128]{0:T(128)S(1)}, f32[128]{0:T(128)}, u32[]{:S(2)}) copy-start(f32[128]{0:T(128)} %copy-done.60) | copy-start | bytes 1540
  293.3 5.8 %copy-start.2 = (f32[128,1152]{1,0:T(8,128)S(1)}, f32[128,1152]{1,0:T(8,128)}, u32[]{:S(2)}) copy-start(f32[128,1152]{1,0:T(8,128)} %copy-done.1) | copy-start | bytes 1769476
  293.3 5.8 %copy-start.22 = (f32[1152]{0:T(1024)S(1)}, f32[1152]{0:T(1024)}, u32[]{:S(2)}) copy-start(f32[1152]{0:T(1024)} %get-tuple-element.103) | copy-start | bytes 13828
  293.3 5.8 %copy-start.49 = (f32[128]{0:T(128)S(1)}, f32[128]{0:T(128)}, u32[]{:S(2)}) copy-start(f32[128]{0:T(128)} %copy-done.48) | copy-start | bytes 1540
  299.1 5.2 %copy-start.11 = (f32[2,4,64,64]{2,3,1,0:T(8,128)S(1)}, f32[2,4,64,64]{2,3,1,0:T(8,128)}, u32[]{:S(2)}) copy-start(f32[2,4,64,64]{2,3,1,0:T(8,128)} %copy-done.10) | copy-start | bytes 393220
  300.8 6.2 %copy-start.24 = (bf16[128,4,128]{2,0,1:T(8,128)(2,1)S(1)}, bf16[128,4,128]{2,0,1:T(8,128)(2,1)}, u32[]{:S(2)}) copy-start(bf16[128,4,128]{2,0,1:T(8,128)(2,1)} %copy-done.23) | copy-start | bytes 393220
  300.8 6.3 %copy-start.26 = (bf16[128,4,128]{2,0,1:T(8,128)(2,1)S(1)}, bf16[128,4,128]{2,0,1:T(8,128)(2,1)}, u32[]{:S(2)}) copy-start(bf16[128,4,128]{2,0,1:T(8,128)(2,1)} %copy-done.25) | copy-start | bytes 393220
  300.8 6.5 %copy-start.53 = (f32[128]{0:T(128)S(1)}, f32[128]{0:T(128)}, u32[]{:S(2)}) copy-start(f32[128]{0:T(128)} %copy-done.52) | copy-start | bytes 1540
  300.8 6.5 %copy-start.55 = (f32[128]{0:T(128)S(1)}, f32[128]{0:T(128)}, u32[]{:S(2)}) copy-start(f32[128]{0:T(128)} %copy-done.54) | copy-start | bytes 1540
  300.8 6.8 %copy-start.44 = (f32[1,256]{1,0:T(1,128)S(1)}, f32[1,256]{1,0:T(1,128)}, u32[]{:S(2)}) copy-start(f32[1,256]{1,0:T(1,128)} %copy-done.43) | copy-start | bytes 3076
  300.9 6.8 %copy-start.51 = (f32[128]{0:T(128)S(1)}, f32[128]{0:T(128)}, u32[]{:S(2)}) copy-start(f32[128]{0:T(128)} %copy-done.50) | copy-start | bytes 1540
  300.9 7.9 %copy-start.59 = (f32[128]{0:T(128)S(1)}, f32[128]{0:T(128)}, u32[]{:S(2)}) copy-start(f32[128]{0:T(128)} %copy-done.58) | copy-start | bytes 1540
  300.9 8.9 %copy-start.30 = (bf16[128,128]{1,0:T(8,128)(2,1)S(1)}, bf16[128,128]{1,0:T(8,128)(2,1)}, u32[]{:S(2)}) copy-start(bf16[128,128]{1,0:T(8,128)(2,1)} %copy-done.29) | copy-start | bytes 98308
  300.9 8.9 %copy-start.32 = (bf16[128,128]{1,0:T(8,128)(2,1)S(1)}, bf16[128,128]{1,0:T(8,128)(2,1)}, u32[]{:S(2)}) copy-start(bf16[128,128]{1,0:T(8,128)(2,1)} %copy-done.31) | copy-start | bytes 98308
  305.1 5.7 %copy-start.27 = (f32[2,64,256,1]{2,1,3,0:T(8,128)}, f32[2,64,256,1]{2,1,3,0:T(8,128)S(1)}, u32[]{:S(2)}) copy-start(f32[2,64,256,1]{2,1,3,0:T(8,128)S(1)} %fusion.25) | copy-start | bytes 393220
  305.1 5.0 %copy-start.17 = (f32[128,128]{1,0:T(8,128)S(1)}, f32[128,128]{1,0:T(8,128)}, u32[]{:S(2)}) copy-start(f32[128,128]{1,0:T(8,128)} %copy-done.16) | copy-start | bytes 196612
  307.1 3.2 copy-start.37
  307.1 3.2 copy-start.46
  307.7 2.9 copy-start.42
  310.2 2.1 copy-start.8
  310.2 2.1 copy-start.34
  310.2 2.1 copy-start.57
  312.3 4.8 %copy-start.63 = (f32[128]{0:T(128)S(1)}, f32[128]{0:T(128)}, u32[]{:S(2)}) copy-start(f32[128]{0:T(128)} %copy-done.62) | copy-start | bytes 1540
  312.3 4.8 %copy-start.4 = (f32[128,1152]{1,0:T(8,128)S(1)}, f32[128,1152]{1,0:T(8,128)}, u32[]{:S(2)}) copy-start(f32[128,1152]{1,0:T(8,128)} %copy-done.3) | copy-start | bytes 1769476
  313.1 5.1 %copy-start.13 = (bf16[16,8,4,256]{3,1,2,0:T(8,128)(2,1)S(1)}, bf16[16,8,4,256]{3,1,2,0:T(8,128)(2,1)}, u32[]{:S(2)}) copy-start(bf16[16,8,4,256]{3,1,2,0:T(8,128)(2,1)} %copy-done.12) | copy-start | bytes 786436
  317.1 3.4 copy-start.28
  427.6 8.1 %copy-start.14 = (f32[2,224,1152]{2,1,0:T(8,128)S(1)}, f32[2,224,1152]{2,1,0:T(8,128)}, u32[]{:S(2)}) copy-start(f32[2,224,1152]{2,1,0:T(8,128)} %get-tuple-element.40) | copy-start | bytes 6193156
  435.6 1.4 copy-start.19
  435.7 2.1 copy-start.20
  (16 other events, 13.1 us)

commit v2 on v0

--- a/solution.py
+++ b/solution.py
@@ -3,6 +3,8 @@
 import jax
 import jax.numpy as jnp
 from jax import lax
+from jax.experimental import pallas as pl
+from jax.experimental.pallas import tpu as pltpu
 from jax.sharding import PartitionSpec as P
 
 D = 1152
@@ -129,7 +131,7 @@
     return jax.nn.gelu(gate, approximate=True) * upward
 
 
-def shards(
+def general_shards(
     inputs,
     segment_ids,
     valid_mask,
@@ -296,6 +298,804 @@
     )
 
 
+BLOCK = 216
+PADDED = 224
+WIDE = 2 * PADDED
+MINE = 128
+PAIR = 2 * MINE
+VMEM_BYTES = 62 << 20
+SQRT_2_OVER_PI = math.sqrt(2.0 / math.pi)
+CUBIC = 0.044715
+MESH = pl.DeviceIdType.MESH
+LOW = jnp.bfloat16
+F32 = jnp.float32
+
+
+def spots():
+    me = lax.axis_index("dp")
+    return me, me // 8, me // 4 % 2, me // 2 % 2, me % 2
+
+
+def at(z, y, x, c):
+    return z * 8 + y * 4 + x * 2 + c
+
+
+def z_peer(z, k):
+    if k == 0:
+        return z
+    if k == 1:
+        return z + 1 - 2 * (z % 2)
+    if k == 2:
+        return (z + 2) % 4
+    return 3 - z
+
+
+def greet_all(me):
+    barrier = pltpu.get_barrier_semaphore()
+
+    def one(step, carry):
+        pl.semaphore_signal(barrier, inc=1, device_id=((me + step) % 32,), device_id_type=MESH)
+        return carry
+
+    lax.fori_loop(1, 32, one, 0)
+    pl.semaphore_wait(barrier, 31)
+
+
+def nt(left, right):
+    return lax.dot_general(left, right, (((1,), (1,)), ((), ())), preferred_element_type=F32)
+
+
+def nn(left, right):
+    return lax.dot_general(left, right, (((1,), (0,)), ((), ())), preferred_element_type=F32)
+
+
+def tn(left, right):
+    return lax.dot_general(left, right, (((0,), (0,)), ((), ())), preferred_element_type=F32)
+
+
+def norm_back(values, gain, upstream):
+    scale = lax.rsqrt(jnp.mean(values * values, -1, keepdims=True) + EPSILON)
+    normed = values * scale
+    gain_grad = jnp.sum(upstream * normed, 0, keepdims=True)
+    inner = upstream * gain
+    grad = scale * (inner - normed * jnp.mean(inner * normed, -1, keepdims=True))
+    return grad, gain_grad
+
+
+def added(left, right):
+    return (left.astype(F32) + right.astype(F32)).astype(LOW)
+
+
+class Net:
+    def __init__(self, send_sems, recv_sems, anyone):
+        self.send_sems, self.recv_sems, self.anyone = send_sems, recv_sems, anyone
+        self.used, self.sent, self.maybe = 0, [], []
+
+    def slots(self, count):
+        first = self.used
+        self.used += count
+        return first
+
+    def copy(self, src, dst, send_slot, recv_slot, device):
+        return pltpu.make_async_remote_copy(
+            src_ref=src,
+            dst_ref=dst,
+            send_sem=self.send_sems.at[send_slot],
+            recv_sem=self.recv_sems.at[recv_slot],
+            device_id=(device,),
+            device_id_type=MESH,
+        )
+
+    def send(self, src, dst, slot, device):
+        copy = self.copy(src, dst, slot, slot, device)
+        copy.start()
+        self.sent.append(copy)
+
+    def move(self, stays, src, dst, send_slot, recv_slot, device):
+        copy = self.copy(src, dst, send_slot, recv_slot, device)
+
+        @pl.when(stays)
+        def _():
+            pltpu.make_async_copy(src, dst, self.recv_sems.at[recv_slot]).start()
+
+        @pl.when(jnp.logical_not(stays))
+        def _():
+            copy.start()
+
+        self.maybe.append((stays, copy))
+
+    def got(self, block, slot):
+        self.copy(block, block, slot, slot, self.anyone).wait_recv()
+
+    def flush(self, gone):
+        for copy in gone:
+            copy.wait_send()
+        names = {id(copy) for copy in gone}
+        self.sent = [copy for copy in self.sent if id(copy) not in names]
+
+    def drain(self):
+        self.flush(list(self.sent))
+        for stays, copy in self.maybe:
+
+            @pl.when(jnp.logical_not(stays))
+            def _():
+                copy.wait_send()
+
+        self.maybe = []
+
+
+def layer_kernel(*refs):
+    (
+        x_ref,
+        seg_ref,
+        valid_ref,
+        ain,
+        aout,
+        gu,
+        dn,
+        gains,
+        head_gains,
+        cot,
+        layer_out,
+        input_grad,
+        o_in,
+        o_out,
+        o_gu,
+        o_dn,
+        o_small,
+        all_in,
+        all_out,
+        all_gu,
+        all_dn,
+        allow,
+        cosine,
+        sine,
+        weight,
+        normed_in,
+        proj,
+        heads,
+        probs,
+        mixed,
+        attn_proj,
+        middle,
+        rows,
+        total,
+        got_mid,
+        got_up,
+        hidden_t,
+        slope_gate,
+        slope_up,
+        gate_t,
+        up_t,
+        acc,
+        keep,
+        send_y,
+        recv_y,
+        send_z,
+        recv_z,
+        grad_middle,
+        grad_attn,
+        grad_heads,
+        grad_proj,
+        key_acc,
+        d_in,
+        a1,
+        a2,
+        a3,
+        b1,
+        b2,
+        b3,
+        g0,
+        g1,
+        g2,
+        n0,
+        n1,
+        n2,
+        small,
+        local,
+        send_sems,
+        recv_sems,
+    ) = refs
+    me, z, y, x, c = spots()
+    xp, yp, cp = at(z, y, 1 - x, c), at(z, 1 - y, x, c), at(z, y, x, 1 - c)
+    z_peers = [at(z_peer(z, k), y, x, c) for k in range(4)]
+    net = Net(send_sems, recv_sems, cp)
+    keep_in = pltpu.make_async_copy(ain, all_in.at[z, y, x, c], local.at[0])
+    keep_out = pltpu.make_async_copy(aout, all_out.at[z, y, x, c], local.at[1])
+    keep_in.start()
+    keep_out.start()
+    greet_all(me)
+
+    a_z, a_x, a_y, a_c = net.slots(4), net.slots(4), net.slots(4), net.slots(2)
+    b_z, b_y, b_x, b_c = net.slots(4), net.slots(4), net.slots(4), net.slots(2)
+    mine_in, mine_out = all_in.at[z, y, x, c], all_out.at[z, y, x, c]
+    for k in (1, 2, 3):
+        net.send(ain, mine_in, a_z + k, z_peers[k])
+    net.send(ain, mine_in, a_x, xp)
+    for k in (1, 2, 3):
+        net.send(aout, mine_out, b_z + k, z_peers[k])
+    net.send(aout, mine_out, b_y, yp)
+    w_one, w_two, w_c = net.slots(3), net.slots(3), net.slots(2)
+    kind, goal = z // 2, 2 * (z % 2) + x
+    for h in range(2):
+        net.move(
+            jnp.logical_and(goal == z, x == h),
+            gu.at[h],
+            all_gu.at[kind, h, c],
+            w_one + h,
+            w_one + kind,
+            at(goal, y, h, c),
+        )
+    net.move(
+        z % 2 == y,
+        dn,
+        all_dn.at[c, x],
+        w_one + 2,
+        w_one + 2,
+        at(2 * (z // 2) + y, z % 2, x, c),
+    )
+
+    seg = jnp.broadcast_to(seg_ref[...].astype(F32), (MINE, MINE))
+    valid = jnp.broadcast_to(valid_ref[...].astype(F32), (MINE, MINE))
+    row = lax.broadcasted_iota(jnp.int32, (MINE, MINE), 0)
+    col = lax.broadcasted_iota(jnp.int32, (MINE, MINE), 1)
+    length = MINE // MICRO
+    same = jnp.logical_and(seg == seg.T, row // length == col // length)
+    position = jnp.sum(jnp.where(jnp.logical_and(same, col < row), 1.0, 0.0), -1, keepdims=True)
+    usable = jnp.logical_or(valid > 0.0, row == col)
+    allow[...] = jnp.where(
+        jnp.logical_and(jnp.logical_and(same, col <= row), usable), 1.0, 0.0
+    )
+    weight[...] = valid.T
+    freqs = jnp.exp(col.astype(F32) * (-2.0 * math.log(THETA) / HD))
+    angles = position * freqs
+    cosine[...] = jnp.cos(angles)
+    sine[...] = jnp.sin(angles)
+    stream = x_ref[...].astype(F32)
+    normed_in[...] = norm_rows(stream, gains[0:1, :]).astype(LOW)
+
+    for k in (1, 2, 3):
+        block = all_in.at[z_peer(z, k), y, x, c]
+        net.got(block, a_z + k)
+        net.send(block, block, a_x + k, xp)
+        block = all_out.at[z_peer(z, k), y, x, c]
+        net.got(block, b_z + k)
+        net.send(block, block, b_y + k, yp)
+    keep_in.wait()
+    keep_out.wait()
+    for k in range(4):
+        there = z_peer(z, k)
+        net.got(all_in.at[there, y, 1 - x, c], a_x + k)
+        pair = all_in.at[there, y, :, c]
+        net.send(pair, pair, a_y + k, yp)
+        net.got(all_out.at[there, 1 - y, x, c], b_y + k)
+        pair = all_out.at[there, :, x, c]
+        net.send(pair, pair, b_x + k, xp)
+    near = all_in.at[:, y, :, c]
+    net.send(near, near, a_c, cp)
+    near = all_out.at[:, :, x, c]
+    net.send(near, near, b_c, cp)
+    for t in range(2):
+        block = all_gu.at[t, x, c]
+        net.got(block, w_one + t)
+        net.send(block, block, w_two + t, xp)
+    block = all_dn.at[c, x]
+    net.got(block, w_one + 2)
+    net.send(block, block, w_two + 2, xp)
+    for k in range(4):
+        net.got(all_in.at[z_peer(z, k), 1 - y, :, c], a_y + k)
+    far = all_in.at[:, 1 - y, :, c]
+    net.send(far, far, a_c + 1, cp)
+    net.got(all_in.at[:, y, :, 1 - c], a_c)
+    net.got(all_in.at[:, 1 - y, :, 1 - c], a_c + 1)
+
+    flat_in = all_in.reshape(HEADS * HD + 2 * HD, D)
+    flat_out = all_out.reshape(HEADS * HD, D)
+    half = HD // 2
+
+    def rows_of(j):
+        return pl.ds(pl.multiple_of(j * HD, HD), HD)
+
+    def project(j, carry):
+        table = nt(normed_in[...], flat_in[rows_of(j), :])
+        proj[j] = table
+
+        @pl.when(j < HEADS + 1)
+        def _():
+            turned = norm_rows(table, head_gains[pl.ds(j // HEADS, 1), :])
+            first, second = turned[:, :half], turned[:, half:]
+            heads[j, :, :half] = (first * cosine[...] - second * sine[...]).astype(LOW)
+            heads[j, :, half:] = (second * cosine[...] + first * sine[...]).astype(LOW)
+
+        @pl.when(j == HEADS + 1)
+        def _():
+            heads[j] = table.astype(LOW)
+
+        return carry
+
+    lax.fori_loop(0, HEADS + 2, project, 0)
+    for k in range(4):
+        net.got(all_out.at[z_peer(z, k), :, 1 - x, c], b_x + k)
+    far = all_out.at[:, :, 1 - x, c]
+    net.send(far, far, b_c + 1, cp)
+
+    def attend_head(j, carry):
+        seen = allow[...] > 0.0
+        scores = nt(heads[j], heads[HEADS]) * SCALE_FACTOR
+        masked = jnp.where(seen, scores, NEGATIVE)
+        peak = jnp.max(masked, -1, keepdims=True)
+        expo = jnp.where(seen, jnp.exp(masked - peak), 0.0)
+        prob = expo / jnp.sum(expo, -1, keepdims=True)
+        probs[j] = prob
+        mixed[j] = nn(prob.astype(LOW), heads[HEADS + 1]).astype(LOW)
+        return carry
+
+    lax.fori_loop(0, HEADS, attend_head, 0)
+    net.got(all_out.at[:, :, x, 1 - c], b_c)
+    net.got(all_out.at[:, :, 1 - x, 1 - c], b_c + 1)
+
+    attn_proj[...] = jnp.zeros((MINE, D), F32)
+
+    def attn_out_head(j, carry):
+        attn_proj[...] += nn(mixed[j], flat_out[rows_of(j), :])
+        return carry
+
+    lax.fori_loop(0, HEADS, attn_out_head, 0)
+    branch = norm_rows(attn_proj[...], gains[1:2, :])
+    mid = x_ref[...].astype(F32) + branch
+    middle[...] = mid
+    rows[0] = norm_rows(mid, gains[2:3, :]).astype(LOW)
+
+    def counted(values):
+        return jnp.sum(weight[:, 0:1] * jnp.sum(values * values, -1, keepdims=True))
+
+    spot = lax.broadcasted_iota(jnp.int32, (1, D), 1)
+    stats = jnp.where(spot == 4, jnp.sum(weight[:, 0:1]), 0.0)
+    first_values = x_ref[...].astype(F32)
+    stats += jnp.where(spot == 0, counted(first_values), 0.0)
+    stats += jnp.where(spot == 1, counted(mid), 0.0)
+    stats += jnp.where(spot == 2, counted(branch), 0.0)
+    small[0] = jnp.zeros((8, D), F32)
+    small[0, 5:6, :] = stats
+
+    def moved(which, got_all, pairs, before_pairs):
+        mine = rows.at[which]
+        gz, gy, sy, sz = net.slots(4), net.slots(4), net.slots(4), net.slots(4)
+        for k in (1, 2, 3):
+            net.send(mine, got_all.at[z, y], gz + k, z_peers[k])
+        net.send(mine, got_all.at[z, y], gy, yp)
+        got_all[z, y] = rows[which]
+        gathered = net.sent[-4:]
+
+        def finish(k):
+            net.got(recv_y.at[k], sy + k)
+            if k == 0:
+                total[...] = keep[0] + recv_y[0].astype(F32)
+            else:
+                send_z[k - 1] = (keep[k % 2] + recv_y[k].astype(F32)).astype(LOW)
+                net.send(send_z.at[k - 1], recv_z.at[k - 1], sz + k, z_peers[k])
+
+        for k in range(4):
+            there = z_peer(z, k)
+            if k < 3:
+                block = got_all.at[z_peer(z, k + 1), y]
+                net.got(block, gz + k + 1)
+                net.send(block, block, gy + k + 1, yp)
+                gathered.append(net.sent[-1])
+            net.got(got_all.at[there, 1 - y], gy + k)
+            if k == 0:
+                before_pairs()
+            pairs(there)
+            if k:
+                finish(k - 1)
+            keep[k % 2] = acc[y]
+            send_y[k] = acc[1 - y].astype(LOW)
+            net.send(send_y.at[k], recv_y.at[k], sy + k, yp)
+
+        def settle():
+            for k in (1, 2, 3):
+                net.got(recv_z.at[k - 1], sz + k)
+                total[...] += recv_z[k - 1].astype(F32)
+
+        return finish, settle, gathered
+
+    w_gu, w_dn = all_gu.reshape(2, 2, WIDE, D), all_dn.reshape(2, WIDE, D)
+
+    def columns(there):
+        return pl.ds(pl.multiple_of(there * PAIR, PAIR), PAIR)
+
+    def put(h, part):
+        part = part.reshape(2, MINE, D)
+
+        @pl.when(h == 0)
+        def _():
+            acc[...] = part
+
+        @pl.when(h == 1)
+        def _():
+            acc[...] += part
+
+    def forward_pairs(there):
+        def one(h, carry):
+            block = got_mid[there].reshape(PAIR, D)
+            gate = nt(block, w_gu[0, h])
+            upward = nt(block, w_gu[1, h])
+            square = gate * gate
+            tanh = jnp.tanh(SQRT_2_OVER_PI * gate * (1.0 + CUBIC * square))
+            side = 0.5 * (1.0 + tanh)
+            gelu = gate * side
+            slope = side + 0.5 * gate * (1.0 - tanh * tanh) * (
+                SQRT_2_OVER_PI * (1.0 + 3.0 * CUBIC * square)
+            )
+            low = (gelu * upward).astype(LOW)
+            slope_gate[h, there] = (upward * slope).astype(LOW)
+            slope_up[h, there] = gelu.astype(LOW)
+            put(h, nn(low, w_dn[h]))
+            hidden_t[h, :, columns(there)] = low.T
+            return carry
+
+        lax.fori_loop(0, 2, one, 0)
+
+    def weights_here():
+        for t in range(2):
+            net.got(all_gu.at[t, 1 - x, c], w_two + t)
+        net.got(all_dn.at[c, 1 - x], w_two + 2)
+        net.send(all_gu.at[:, :, c], all_gu.at[:, :, c], w_c, cp)
+        net.send(all_dn.at[c], all_dn.at[c], w_c + 1, cp)
+        net.got(all_gu.at[:, :, 1 - c], w_c)
+        net.got(all_dn.at[1 - c], w_c + 1)
+
+    finish, settle, _ = moved(0, got_mid, forward_pairs, weights_here)
+    finish(3)
+    settle()
+    net.drain()
+
+    ffw_proj = total[...]
+    branch = norm_rows(ffw_proj, gains[3:4, :])
+    layer_out[...] = (middle[...] + branch).astype(LOW)
+    small[0, 5:6, :] += jnp.where(spot == 3, counted(branch), 0.0)
+    grad, gain_grad = norm_back(ffw_proj, gains[3:4, :], cot[...].astype(F32))
+    small[0, 3:4, :] = gain_grad
+    rows[1] = grad.astype(LOW)
+
+    def backward_pairs(there):
+        def one(h, carry):
+            block = got_up[there].reshape(PAIR, D)
+            back = nt(block, w_dn[h])
+            gate = (back * slope_gate[h, there].astype(F32)).astype(LOW)
+            upward = (back * slope_up[h, there].astype(F32)).astype(LOW)
+            put(h, nn(gate, w_gu[0, h]) + nn(upward, w_gu[1, h]))
+            gate_t[h, :, columns(there)] = gate.T
+            up_t[h, :, columns(there)] = upward.T
+            return carry
+
+        lax.fori_loop(0, 2, one, 0)
+
+    finish, settle, gathered = moved(1, got_up, backward_pairs, lambda: None)
+    finish(3)
+
+    step = 384
+    flat_mid, flat_up = got_mid.reshape(8 * MINE, D), got_up.reshape(8 * MINE, D)
+
+    def down_grads(i, carry):
+        h, cols = i // 3, pl.ds(pl.multiple_of(i % 3 * step, 128), step)
+        w_dn[h, :, cols] = nn(hidden_t[h], flat_up[:, cols]).astype(LOW)
+        return carry
+
+    lax.fori_loop(0, 6, down_grads, 0)
+    d_c, d_x, d_home = net.slots(4), net.slots(4), net.slots(3)
+    net.send(all_dn.at[1 - c], n0, d_c, cp)
+
+    def gate_up_grads(i, carry):
+        h, cols = i // 3, pl.ds(pl.multiple_of(i % 3 * step, 128), step)
+        w_gu[0, h, :, cols] = nn(gate_t[h], flat_mid[:, cols]).astype(LOW)
+        w_gu[1, h, :, cols] = nn(up_t[h], flat_mid[:, cols]).astype(LOW)
+        return carry
+
+    lax.fori_loop(0, 6, gate_up_grads, 0)
+    net.send(all_gu.at[:, :, 1 - c], g0, d_c + 1, cp)
+    settle()
+
+    mid = middle[...]
+    grad, gain_grad = norm_back(mid, gains[2:3, :], total[...])
+    small[0, 2:3, :] = gain_grad
+    grad_mid = cot[...].astype(F32) + grad
+    grad_middle[...] = grad_mid
+    grad, gain_grad = norm_back(attn_proj[...], gains[1:2, :], grad_mid)
+    small[0, 1:2, :] = gain_grad
+    grad_attn[...] = grad.astype(LOW)
+    net.flush(gathered)
+    d_out = got_up.reshape(4, 2, 2, 2, 32, D)
+    a0 = got_mid.reshape(8 * MINE, D).at[pl.ds(0, 16 * 48)].reshape(4, 2, 2, 48, D)
+    b0 = recv_y.reshape(4, 2, 2, 32, D)
+    flat_d_out, flat_d_in = got_up.reshape(HEADS * HD, D), d_in.reshape(HEADS * HD + 2 * HD, D)
+
+    def out_grads(j, carry):
+        flat_d_out[rows_of(j), :] = tn(mixed[j], grad_attn[...]).astype(LOW)
+        return carry
+
+    lax.fori_loop(0, HEADS, out_grads, 0)
+    net.got(n0, d_c)
+    net.got(g0, d_c + 1)
+    net.send(d_out.at[:, :, :, 1 - c], b0, d_c + 2, cp)
+
+    for q in range(2):
+        all_dn[c, q] = added(all_dn[c, q], n0[q])
+    net.send(all_dn.at[c, 1 - x], n1, d_x, xp)
+    for t in range(2):
+        for h in range(2):
+            all_gu[t, h, c] = added(all_gu[t, h, c], g0[t, h])
+    net.send(all_gu.at[:, 1 - x, c], g1, d_x + 1, xp)
+
+    grad_heads[...] = jnp.zeros((6, MINE, HD), F32)
+
+    def head_back(j, carry):
+        up = nt(grad_attn[...], flat_out[rows_of(j), :]).astype(LOW)
+        prob = probs[j]
+        grad_prob = nt(up, heads[HEADS + 1])
+        grad_heads[HEADS + 1] += tn(prob.astype(LOW), up)
+        center = jnp.sum(grad_prob * prob, -1, keepdims=True)
+        grad_score = (prob * (grad_prob - center)).astype(LOW)
+        grad_heads[j] = nn(grad_score, heads[HEADS]) * SCALE_FACTOR
+        grad_heads[HEADS] += tn(grad_score, heads[j]) * SCALE_FACTOR
+        return carry
+
+    lax.fori_loop(0, HEADS, head_back, 0)
+    key_acc[...] = jnp.zeros((2, HD), F32)
+
+    def turn_back(j, carry):
+        first, second = grad_heads[j, :, :half], grad_heads[j, :, half:]
+        turned = jnp.concatenate(
+            [
+                first * cosine[...] + second * sine[...],
+                second * cosine[...] - first * sine[...],
+            ],
+            -1,
+        )
+        which = pl.ds(j // HEADS, 1)
+        grad, gain_grad = norm_back(proj[j], head_gains[which, :], turned)
+        key_acc[which, :] += gain_grad
+        grad_proj[j] = grad.astype(LOW)
+        return carry
+
+    lax.fori_loop(0, HEADS + 1, turn_back, 0)
+    grad_proj[HEADS + 1] = grad_heads[HEADS + 1].astype(LOW)
+    small[0, 4:5, 0:HD] = key_acc[0:1, :]
+    small[0, 4:5, HD : 2 * HD] = key_acc[1:2, :]
+
+    r_a, r_b, r_s = net.slots(8), net.slots(8), net.slots(8)
+    net.got(b0, d_c + 2)
+
+    def sum_out(i, carry):
+        p, q, r = i // 4, i // 2 % 2, i % 2
+        d_out[p, q, r, c] = added(d_out[p, q, r, c], b0[p, q, r])
+        return carry
+
+    lax.fori_loop(0, 16, sum_out, 0)
+    net.send(d_out.at[:, :, 1 - x, c], b1, r_b, xp)
+
+    def in_grads(j, carry):
+        flat_d_in[rows_of(j), :] = tn(grad_proj[j], normed_in[...]).astype(LOW)
+        return carry
+
+    lax.fori_loop(0, HEADS + 2, in_grads, 0)
+    net.send(d_in.at[:, :, :, 1 - c], a0, d_c + 3, cp)
+    total[...] = jnp.zeros((MINE, D), F32)
+
+    def in_back(j, carry):
+        total[...] += nn(grad_proj[j], flat_in[rows_of(j), :])
+        return carry
+
+    lax.fori_loop(0, HEADS + 2, in_back, 0)
+    grad, gain_grad = norm_back(x_ref[...].astype(F32), gains[0:1, :], total[...])
+    small[0, 0:1, :] = gain_grad
+    input_grad[...] = grad_middle[...] + grad
+    net.send(small.at[0], small.at[1], r_s, cp)
+
+    net.got(a0, d_c + 3)
+
+    def sum_in(i, carry):
+        p, q, r = i // 4, i // 2 % 2, i % 2
+        d_in[p, q, r, c] = added(d_in[p, q, r, c], a0[p, q, r])
+        return carry
+
+    lax.fori_loop(0, 16, sum_in, 0)
+    net.send(d_in.at[:, 1 - y, :, c], a1, r_a, yp)
+    net.got(small.at[1], r_s)
+    small[2] = small[0] + small[1]
+    net.send(small.at[2], small.at[3], r_s + 1, xp)
+    net.got(b1, r_b)
+
+    def sum_out_two(i, carry):
+        p, q = i // 2, i % 2
+        d_out[p, q, x, c] = added(d_out[p, q, x, c], b1[p, q])
+        return carry
+
+    lax.fori_loop(0, 8, sum_out_two, 0)
+    net.send(d_out.at[:, 1 - y, x, c], b2, r_b + 1, yp)
+
+    net.got(n1, d_x)
+    all_dn[c, x] = added(all_dn[c, x], n1[...])
+    net.move(
+        z % 2 == y, all_dn.at[c, x], n2, d_home + 2, d_home + 2, at(2 * (z // 2) + y, z % 2, x, c)
+    )
+    net.got(g1, d_x + 1)
+    for t in range(2):
+        all_gu[t, x, c] = added(all_gu[t, x, c], g1[t])
+        source = z // 2 + 2 * t
+        net.move(
+            jnp.logical_and(source == z, z % 2 == x),
+            all_gu.at[t, x, c],
+            g2.at[x],
+            d_home + t,
+            d_home + x,
+            at(source, y, z % 2, c),
+        )
+
+    net.got(a1, r_a)
+
+    def sum_in_two(i, carry):
+        p, q = i // 2, i % 2
+        d_in[p, y, q, c] = added(d_in[p, y, q, c], a1[p, q])
+        return carry
+
+    lax.fori_loop(0, 8, sum_in_two, 0)
+    net.send(d_in.at[:, y, 1 - x, c], a2, r_a + 1, xp)
+    net.got(small.at[3], r_s + 1)
+    small[4] = small[2] + small[3]
+    net.send(small.at[4], small.at[5], r_s + 2, yp)
+    net.got(b2, r_b + 1)
+    for p in range(4):
+        d_out[p, y, x, c] = added(d_out[p, y, x, c], b2[p])
+    for k in (1, 2, 3):
+        net.send(d_out.at[z_peer(z, k), y, x, c], b3.at[k - 1], r_b + 1 + k, z_peers[k])
+    net.got(a2, r_a + 1)
+    for p in range(4):
+        d_in[p, y, x, c] = added(d_in[p, y, x, c], a2[p])
+    for k in (1, 2, 3):
+        net.send(d_in.at[z_peer(z, k), y, x, c], a3.at[k - 1], r_a + 1 + k, z_peers[k])
+    net.got(small.at[5], r_s + 2)
+    small[6] = small[4] + small[5]
+    for k in (1, 2, 3):
+        net.send(small.at[6], small.at[6 + k], r_s + 2 + k, z_peers[k])
+
+    for k in (1, 2, 3):
+        net.got(b3.at[k - 1], r_b + 1 + k)
+    o_out[...] = (d_out[z, y, x, c].astype(F32) + b3[0].astype(F32)) + (
+        b3[1].astype(F32) + b3[2].astype(F32)
+    )
+    net.got(n2, d_home + 2)
+    o_dn[...] = n2[...].astype(F32)[:BLOCK]
+    for k in (1, 2, 3):
+        net.got(a3.at[k - 1], r_a + 1 + k)
+    o_in[...] = (d_in[z, y, x, c].astype(F32) + a3[0].astype(F32)) + (
+        a3[1].astype(F32) + a3[2].astype(F32)
+    )
+    for k in (1, 2, 3):
+        net.got(small.at[6 + k], r_s + 2 + k)
+    o_small[...] = (small[6] + small[7]) + (small[8] + small[9])
+    for h in range(2):
+        net.got(g2.at[h], d_home + h)
+        o_gu[pl.ds(h * BLOCK, BLOCK), :] = g2[h].astype(F32)[:BLOCK]
+    net.drain()
+
+
+def vm(*shape):
+    return pltpu.VMEM(shape, LOW)
+
+
+def vf(*shape):
+    return pltpu.VMEM(shape, F32)
+
+
+def whole_layer(x, seg, valid, ain, aout, gu, dn, gains, head_gains, cot):
+    vmem = pl.BlockSpec(memory_space=pltpu.VMEM)
+    scratch = [
+        vm(4, 2, 2, 2, 48, D),
+        vm(4, 2, 2, 2, 32, D),
+        vm(2, 2, 2, PADDED, D),
+        vm(2, 2, PADDED, D),
+        vf(MINE, MINE),
+        vf(MINE, MINE),
+        vf(MINE, MINE),
+        vf(MINE, MINE),
+        vm(MINE, D),
+        vf(6, MINE, HD),
+        vm(6, MINE, HD),
+        vf(4, MINE, MINE),
+        vm(4, MINE, HD),
+        vf(MINE, D),
+        vf(MINE, D),
+        vm(2, MINE, D),
+        vf(MINE, D),
+        vm(4, 2, MINE, D),
+        vm(4, 2, MINE, D),
+        vm(2, WIDE, 8 * MINE),
+        vm(2, 4, PAIR, WIDE),
+        vm(2, 4, PAIR, WIDE),
+        vm(2, WIDE, 8 * MINE),
+        vm(2, WIDE, 8 * MINE),
+        vf(2, MINE, D),
+        vf(2, MINE, D),
+        vm(4, MINE, D),
+        vm(4, MINE, D),
+        vm(3, MINE, D),
+        vm(3, MINE, D),
+        vf(MINE, D),
+        vm(MINE, D),
+        vf(6, MINE, HD),
+        vm(6, MINE, HD),
+        vf(2, HD),
+        vm(4, 2, 2, 2, 48, D),
+    ]
+    for count in (48, 32):
+        scratch += [vm(4, 2, count, D), vm(4, count, D), vm(3, count, D)]
+    scratch += [vm(2, 2, PADDED, D), vm(2, PADDED, D), vm(2, PADDED, D)]
+    scratch += [vm(2, PADDED, D), vm(PADDED, D), vm(PADDED, D)]
+    scratch += [vf(10, 8, D)]
+    scratch += [pltpu.SemaphoreType.DMA((2,))] + [pltpu.SemaphoreType.DMA((112,))] * 2
+    return pl.pallas_call(
+        layer_kernel,
+        out_shape=(
+            jax.ShapeDtypeStruct((MINE, D), LOW),
+            jax.ShapeDtypeStruct((MINE, D), F32),
+            jax.ShapeDtypeStruct((48, D), F32),
+            jax.ShapeDtypeStruct((32, D), F32),
+            jax.ShapeDtypeStruct((2 * BLOCK, D), F32),
+            jax.ShapeDtypeStruct((BLOCK, D), F32),
+            jax.ShapeDtypeStruct((8, D), F32),
+        ),
+        in_specs=[vmem] * 10,
+        out_specs=(vmem,) * 7,
+        scratch_shapes=scratch,
+        compiler_params=pltpu.CompilerParams(
+            collective_id=1, has_side_effects=True, vmem_limit_bytes=VMEM_BYTES
+        ),
+        name="layer",
+    )(x, seg, valid, ain, aout, gu, dn, gains, head_gains, cot)
+
+
+def padded_rows(rows):
+    return jnp.pad(rows, ((0, 0), (0, PADDED - BLOCK), (0, 0)))
+
+
+def split_shards(
+    inputs,
+    segment_ids,
+    valid_mask,
+    attn_in,
+    attn_out,
+    ffw_in,
+    ffw_out,
+    norm_gains,
+    head_gains,
+    cotangent,
+):
+    layer_out, input_grad, shard_in, shard_out, shard_gu, shard_dn, small = whole_layer(
+        inputs.reshape(MINE, D),
+        segment_ids.reshape(1, MINE),
+        valid_mask.reshape(1, MINE),
+        attn_in,
+        attn_out,
+        padded_rows(ffw_in.reshape(2, BLOCK, D)),
+        padded_rows(ffw_out.reshape(1, BLOCK, D))[0],
+        norm_gains,
+        head_gains,
+        cotangent.reshape(MINE, D),
+    )
+    return (
+        layer_out.reshape(inputs.shape),
+        input_grad.reshape(inputs.shape),
+        shard_in,
+        shard_out,
+        shard_gu,
+        shard_dn,
+        small[:4],
+        small[4, : 2 * HD].reshape(2, HD),
+        jnp.sqrt(small[5, :4] / (small[5, 4] * D)),
+    )
+
+
 def solution(mesh):
     placed = (
         P(None, "dp", None, None),
@@ -310,7 +1110,7 @@
         P(None, "dp", None, None),
     )
     return jax.shard_map(
-        shards,
+        split_shards if mesh.shape["dp"] == 32 else general_shards,
         mesh=mesh,
         in_specs=placed,
         out_specs=(

time: 2100 us -> 369 us (0.18)
  waiting for transfers between devices: 1410 us -> 0 us
  blocking collectives: 347 us -> 0 us
  Pallas kernels: 0 us -> 340 us
  matrix products: 169 us -> 0 us
  other arithmetic: 67.9 us -> 3.88 us
  local copies, waits for them, and re-layouts: 50.9 us -> 18.7 us
  starting transfers between devices: 24.7 us -> 0 us
    ppermute x20 -> x0, waiting for transfers between devices: 1050 us -> none  [swapped(): return lax.ppermute(block, axis, route)]
    all_gather x4 -> x0, waiting for transfers between devices: 356 us -> none  [the longest x1 183 us: shards(): lax.all_gather(ffw_in, 'dp', axis=0, tiled=True)]
    psum x1 -> x0, blocking collectives: 347 us -> none  [shards(): lax.psum((gain_sums, head_sums, stats), 'dp')]
    pallas_call x0 -> x1, Pallas kernels: none -> 340 us  [whole_layer(): pl.pallas_call(layer_kernel, out_shape=(jax.ShapeDtypeStruct((MINE, D), L...]
    dot_general x36 -> x0, matrix products: 169 us -> none  [the longest x8 62 us: across(): lax.dot_general(left, piece, (((1,), (1,)), ((), ())), preferred_element_...]
    add x21 -> x0, other arithmetic: 35 us -> none  [the longest x16 32.8 us: shards(): current = tuple((mine + theirs for mine, theirs in zip(current, arrived)))]
    ppermute x20 -> x0, starting transfers between devices: 24.5 us -> none  [swapped(): return lax.ppermute(block, axis, route)]
    convert_element_type x18 -> x0, local copies, waits for them, and re-layouts: 21.3 us -> none  [the longest x16 20 us: short(): return part.astype(jnp.bfloat16) if part.dtype == jnp.float32 else part]
  transfers between devices with their start and end apart: 24 -> 0, of which waited for: 12 -> 0; matrix products, arithmetic and copies ran while one was open for 10% -> 0% of each run, Pallas kernels for 0% -> 0%
where the time goes in v2:
time: 369 us; the launch traced here: 364 us
  Pallas kernels  340 us (92%)
  local copies, waits for them, and re-layouts  18.7 us (5%)
  other arithmetic  3.88 us (1%)
    pallas_call x1, Pallas kernels, whole_layer(): pl.pallas_call(layer_kernel, out_shape=(jax.ShapeDtypeStruct((MINE, D), L...  340 us
    unnamed x13, local copies, waits for them, and re-layouts  9.29 us

profile of v2, /device:TPU:22, one launch (start us, length us, event | category | flops | bytes accessed | tf_op | source)
XLA Modules:
  0.0 364.2 jit_solution(4999474128236532205)
XLA Ops:
  0.6 0.5 broadcast.15
  1.2 1.3 reduce.10
  2.5 0.6 reshape.48.refs_1_
  3.1 1.3 reduce.11
  4.4 0.6 reshape.49.refs_2_
  5.0 1.9 pad_bitcast_fusion.refs_6_
  6.9 2.2 pad.8.refs_5_
  9.1 340.3 %layer.1 = (bf16[128,1152]{1,0:T(8,128)(2,1)}, f32[128,1152]{1,0:T(8,128)}, f32[48,1152]{1,0:T(8,128)}, f32[32,1152]{1,0:T(8,128)}, f32[432,1152]{1,0:T(8,128)}, /*index=5*/f32[216,1152]{1,0:T(8,128)}, f32[8,1152]{1,0:T(8,128)}) custom-call(bf16[128,1152]{1,0:T(8,128)(2,1)} %bitcast.19, s32[1,128]{1,0:T(1,128)} %reshape.48.refs_1_, ...), custom_call_target="tpu_custom_call" | custom-call | tf_op jit(solution)/shard_map/layer/pallas_call | solution.py:1037
  349.5 0.0 copy-start.2
  349.5 0.0 copy-start
  349.5 1.4 slice.15
  351.6 1.2 sqrt_bitcast_fusion
  352.8 0.7 slice_reduce_fusion
  353.5 1.4 slice.12
  354.9 0.6 reshape_squeeze.3
  355.5 1.7 copy.27
  357.2 1.9 copy.28
  359.1 1.6 copy.29
  360.7 0.0 copy-done.2
  360.7 0.7 copy.30
  361.4 0.0 copy-done
  361.4 0.0 copy-start.1
  361.4 1.3 copy.31
  362.7 0.6 copy-done.1
  363.3 0.9 copy.32
Async XLA Ops:
  349.5 11.2 %copy-start.2 = (f32[32,1152]{1,0:T(8,128)S(1)}, f32[32,1152]{1,0:T(8,128)}, u32[]{:S(2)}) copy-start(f32[32,1152]{1,0:T(8,128)} %get-tuple-element.44) | copy-start | bytes 442372
  349.5 11.9 %copy-start = (f32[432,1152]{1,0:T(8,128)S(1)}, f32[432,1152]{1,0:T(8,128)}, u32[]{:S(2)}) copy-start(f32[432,1152]{1,0:T(8,128)} %get-tuple-element.45) | copy-start | bytes 5971972
  361.4 1.9 copy-start.1

commit v3 on v2

--- a/solution.py
+++ b/solution.py
@@ -302,6 +302,7 @@
 PADDED = 224
 WIDE = 2 * PADDED
 MINE = 128
+PART = 64
 PAIR = 2 * MINE
 VMEM_BYTES = 62 << 20
 SQRT_2_OVER_PI = math.sqrt(2.0 / math.pi)
@@ -364,6 +365,10 @@
 
 def added(left, right):
     return (left.astype(F32) + right.astype(F32)).astype(LOW)
+
+
+def stream_of(ref):
+    return ref[...].reshape(MINE, D).astype(F32)
 
 
 class Net:
@@ -415,6 +420,9 @@
 
     def drain(self):
         self.flush(list(self.sent))
+        self.settle_moves()
+
+    def settle_moves(self):
         for stays, copy in self.maybe:
 
             @pl.when(jnp.logical_not(stays))
@@ -442,7 +450,9 @@
         o_out,
         o_gu,
         o_dn,
-        o_small,
+        o_gains,
+        o_heads,
+        o_rms,
         all_in,
         all_out,
         all_gu,
@@ -465,8 +475,6 @@
         hidden_t,
         slope_gate,
         slope_up,
-        gate_t,
-        up_t,
         acc,
         keep,
         send_y,
@@ -506,37 +514,90 @@
     keep_out.start()
     greet_all(me)
 
-    a_z, a_x, a_y, a_c = net.slots(4), net.slots(4), net.slots(4), net.slots(2)
-    b_z, b_y, b_x, b_c = net.slots(4), net.slots(4), net.slots(4), net.slots(2)
-    mine_in, mine_out = all_in.at[z, y, x, c], all_out.at[z, y, x, c]
-    for k in (1, 2, 3):
-        net.send(ain, mine_in, a_z + k, z_peers[k])
-    net.send(ain, mine_in, a_x, xp)
-    for k in (1, 2, 3):
-        net.send(aout, mine_out, b_z + k, z_peers[k])
-    net.send(aout, mine_out, b_y, yp)
+    class Spread:
+        def __init__(self, own, full):
+            self.own, self.full = own, full
+            self.az, self.ax, self.ay, self.ac = (net.slots(4) for _ in range(4))
+
+        def block(self, k):
+            return self.full.at[z_peer(z, k), y, x, c]
+
+        def start(self):
+            net.send(self.own, self.block(0), self.az + 1, z_peers[1])
+            net.send(self.own, self.block(0), self.ax, xp)
+            net.send(self.own, self.block(0), self.az + 2, z_peers[2])
+
+        def hop(self, k):
+            block = self.block(k)
+            net.got(block, self.az + k)
+            if k == 2:
+                net.send(block, block, self.az + 3, z_peers[1])
+            net.send(block, block, self.ax + k, xp)
+
+        def turn(self, k):
+            there = z_peer(z, k)
+            net.got(self.full.at[there, y, 1 - x, c], self.ax + k)
+            pair = self.full.at[there, y, :, c]
+            net.send(pair, pair, self.ay + k, yp)
+
+        def near(self):
+            part = self.full.at[:, y, :, c]
+            net.send(part, part, self.ac, cp)
+
+        def far(self):
+            for k in range(4):
+                net.got(self.full.at[z_peer(z, k), 1 - y, :, c], self.ay + k)
+            part = self.full.at[:, 1 - y, :, c]
+            net.send(part, part, self.ac + 1, cp)
+
+        def whole(self):
+            net.got(self.full.at[:, y, :, 1 - c], self.ac)
+            net.got(self.full.at[:, 1 - y, :, 1 - c], self.ac + 1)
+
+    into, outof = Spread(ain, all_in), Spread(aout, all_out)
+    into.start()
     w_one, w_two, w_c = net.slots(3), net.slots(3), net.slots(2)
     kind, goal = z // 2, 2 * (z % 2) + x
+    blank = jnp.zeros((PADDED - BLOCK, D), F32)
     for h in range(2):
+        part = gu[pl.ds(h * BLOCK, BLOCK), :].astype(F32)
+        g0[0, h] = jnp.concatenate([part, blank], 0).astype(LOW)
+    n0[0] = jnp.concatenate([dn[...].astype(F32), blank], 0).astype(LOW)
+
+    def rows_out():
+        for h in range(2):
+            net.move(
+                jnp.logical_and(goal == z, x == h),
+                g0.at[0, h],
+                all_gu.at[kind, h, c],
+                w_one + h,
+                w_one + kind,
+                at(goal, y, h, c),
+            )
         net.move(
-            jnp.logical_and(goal == z, x == h),
-            gu.at[h],
-            all_gu.at[kind, h, c],
-            w_one + h,
-            w_one + kind,
-            at(goal, y, h, c),
+            z % 2 == y,
+            n0.at[0],
+            all_dn.at[c, x],
+            w_one + 2,
+            w_one + 2,
+            at(2 * (z // 2) + y, z % 2, x, c),
         )
-    net.move(
-        z % 2 == y,
-        dn,
-        all_dn.at[c, x],
-        w_one + 2,
-        w_one + 2,
-        at(2 * (z // 2) + y, z % 2, x, c),
-    )
-
-    seg = jnp.broadcast_to(seg_ref[...].astype(F32), (MINE, MINE))
-    valid = jnp.broadcast_to(valid_ref[...].astype(F32), (MINE, MINE))
+
+    into.hop(1)
+    into.hop(2)
+    outof.start()
+    keep_in.wait()
+    keep_out.wait()
+    into.turn(0)
+    into.turn(1)
+    into.hop(3)
+    rows_out()
+
+    def along_lanes(ref):
+        return jnp.concatenate([ref[0].astype(F32), ref[1].astype(F32)], 1)
+
+    seg = jnp.broadcast_to(along_lanes(seg_ref), (MINE, MINE))
+    valid = jnp.broadcast_to(along_lanes(valid_ref), (MINE, MINE))
     row = lax.broadcasted_iota(jnp.int32, (MINE, MINE), 0)
     col = lax.broadcasted_iota(jnp.int32, (MINE, MINE), 1)
     length = MINE // MICRO
@@ -551,43 +612,22 @@
     angles = position * freqs
     cosine[...] = jnp.cos(angles)
     sine[...] = jnp.sin(angles)
-    stream = x_ref[...].astype(F32)
+    stream = stream_of(x_ref)
     normed_in[...] = norm_rows(stream, gains[0:1, :]).astype(LOW)
 
-    for k in (1, 2, 3):
-        block = all_in.at[z_peer(z, k), y, x, c]
-        net.got(block, a_z + k)
-        net.send(block, block, a_x + k, xp)
-        block = all_out.at[z_peer(z, k), y, x, c]
-        net.got(block, b_z + k)
-        net.send(block, block, b_y + k, yp)
-    keep_in.wait()
-    keep_out.wait()
-    for k in range(4):
-        there = z_peer(z, k)
-        net.got(all_in.at[there, y, 1 - x, c], a_x + k)
-        pair = all_in.at[there, y, :, c]
-        net.send(pair, pair, a_y + k, yp)
-        net.got(all_out.at[there, 1 - y, x, c], b_y + k)
-        pair = all_out.at[there, :, x, c]
-        net.send(pair, pair, b_x + k, xp)
-    near = all_in.at[:, y, :, c]
-    net.send(near, near, a_c, cp)
-    near = all_out.at[:, :, x, c]
-    net.send(near, near, b_c, cp)
-    for t in range(2):
-        block = all_gu.at[t, x, c]
-        net.got(block, w_one + t)
-        net.send(block, block, w_two + t, xp)
-    block = all_dn.at[c, x]
-    net.got(block, w_one + 2)
-    net.send(block, block, w_two + 2, xp)
-    for k in range(4):
-        net.got(all_in.at[z_peer(z, k), 1 - y, :, c], a_y + k)
-    far = all_in.at[:, 1 - y, :, c]
-    net.send(far, far, a_c + 1, cp)
-    net.got(all_in.at[:, y, :, 1 - c], a_c)
-    net.got(all_in.at[:, 1 - y, :, 1 - c], a_c + 1)
+    into.turn(2)
+    outof.hop(1)
+    outof.hop(2)
+    into.turn(3)
+    into.near()
+    outof.turn(0)
+    outof.turn(1)
+    outof.hop(3)
+    into.far()
+    outof.turn(2)
+    outof.turn(3)
+    outof.near()
+    into.whole()
 
     flat_in = all_in.reshape(HEADS * HD + 2 * HD, D)
     flat_out = all_out.reshape(HEADS * HD, D)
@@ -614,10 +654,7 @@
         return carry
 
     lax.fori_loop(0, HEADS + 2, project, 0)
-    for k in range(4):
-        net.got(all_out.at[z_peer(z, k), :, 1 - x, c], b_x + k)
-    far = all_out.at[:, :, 1 - x, c]
-    net.send(far, far, b_c + 1, cp)
+    outof.far()
 
     def attend_head(j, carry):
         seen = allow[...] > 0.0
@@ -631,8 +668,15 @@
         return carry
 
     lax.fori_loop(0, HEADS, attend_head, 0)
-    net.got(all_out.at[:, :, x, 1 - c], b_c)
-    net.got(all_out.at[:, :, 1 - x, 1 - c], b_c + 1)
+    for t in range(2):
+        block = all_gu.at[t, x, c]
+        net.got(block, w_one + t)
+        net.send(block, block, w_two + t, xp)
+    block = all_dn.at[c, x]
+    net.got(block, w_one + 2)
+    net.send(block, block, w_two + 2, xp)
+
+    outof.whole()
 
     attn_proj[...] = jnp.zeros((MINE, D), F32)
 
@@ -642,70 +686,91 @@
 
     lax.fori_loop(0, HEADS, attn_out_head, 0)
     branch = norm_rows(attn_proj[...], gains[1:2, :])
-    mid = x_ref[...].astype(F32) + branch
+    mid = stream_of(x_ref) + branch
     middle[...] = mid
-    rows[0] = norm_rows(mid, gains[2:3, :]).astype(LOW)
+    rows[0] = norm_rows(mid, gains[2:3, :]).astype(LOW).reshape(2, PART, D)
 
     def counted(values):
         return jnp.sum(weight[:, 0:1] * jnp.sum(values * values, -1, keepdims=True))
 
     spot = lax.broadcasted_iota(jnp.int32, (1, D), 1)
     stats = jnp.where(spot == 4, jnp.sum(weight[:, 0:1]), 0.0)
-    first_values = x_ref[...].astype(F32)
+    first_values = stream_of(x_ref)
     stats += jnp.where(spot == 0, counted(first_values), 0.0)
     stats += jnp.where(spot == 1, counted(mid), 0.0)
     stats += jnp.where(spot == 2, counted(branch), 0.0)
     small[0] = jnp.zeros((8, D), F32)
     small[0, 5:6, :] = stats
 
-    def moved(which, got_all, pairs, before_pairs):
-        mine = rows.at[which]
-        gz, gy, sy, sz = net.slots(4), net.slots(4), net.slots(4), net.slots(4)
-        for k in (1, 2, 3):
-            net.send(mine, got_all.at[z, y], gz + k, z_peers[k])
-        net.send(mine, got_all.at[z, y], gy, yp)
-        got_all[z, y] = rows[which]
-        gathered = net.sent[-4:]
-
-        def finish(k):
-            net.got(recv_y.at[k], sy + k)
-            if k == 0:
-                total[...] = keep[0] + recv_y[0].astype(F32)
-            else:
-                send_z[k - 1] = (keep[k % 2] + recv_y[k].astype(F32)).astype(LOW)
-                net.send(send_z.at[k - 1], recv_z.at[k - 1], sz + k, z_peers[k])
-
-        for k in range(4):
+    zh, zl = z // 2, z % 2
+    w_gu, w_dn = all_gu.reshape(2, 2, WIDE, D), all_dn.reshape(2, WIDE, D)
+
+    class Half:
+        def __init__(self, which, half, got_all, compute):
+            self.which, self.half, self.got_all, self.compute = which, half, got_all, compute
+            self.az, self.ay, self.ry, self.rz = (net.slots(4) for _ in range(4))
+            self.gathered = []
+
+        def block(self, k, yy):
             there = z_peer(z, k)
-            if k < 3:
-                block = got_all.at[z_peer(z, k + 1), y]
-                net.got(block, gz + k + 1)
-                net.send(block, block, gy + k + 1, yp)
-                gathered.append(net.sent[-1])
-            net.got(got_all.at[there, 1 - y], gy + k)
-            if k == 0:
-                before_pairs()
-            pairs(there)
-            if k:
-                finish(k - 1)
-            keep[k % 2] = acc[y]
-            send_y[k] = acc[1 - y].astype(LOW)
-            net.send(send_y.at[k], recv_y.at[k], sy + k, yp)
-
-        def settle():
-            for k in (1, 2, 3):
-                net.got(recv_z.at[k - 1], sz + k)
-                total[...] += recv_z[k - 1].astype(F32)
-
-        return finish, settle, gathered
-
-    w_gu, w_dn = all_gu.reshape(2, 2, WIDE, D), all_dn.reshape(2, WIDE, D)
-
-    def columns(there):
-        return pl.ds(pl.multiple_of(there * PAIR, PAIR), PAIR)
+            return self.got_all.at[self.half, there // 2, there % 2, yy]
+
+        def pass_on(self, block, slot, device):
+            net.send(block, block, slot, device)
+            self.gathered.append(net.sent[-1])
+
+        def start(self):
+            own = rows.at[self.which, self.half]
+            net.send(own, self.block(0, y), self.az + 1, z_peers[1])
+            self.gathered.append(net.sent[-1])
+            net.send(own, self.block(0, y), self.az + 2, z_peers[2])
+            self.gathered.append(net.sent[-1])
+            net.send(own, self.block(0, y), self.ay, yp)
+            self.gathered.append(net.sent[-1])
+            self.got_all[self.half, zh, zl, y] = rows[self.which, self.half]
+
+        def hop(self, k):
+            block = self.block(k, y)
+            net.got(block, self.az + k)
+            if k == 2:
+                self.pass_on(block, self.az + 3, z_peers[1])
+            self.pass_on(block, self.ay + k, yp)
+
+        def group(self, g):
+            for k in (2 * g, 2 * g + 1):
+                net.got(self.block(k, 1 - y), self.ay + k)
+            self.compute(self.half, zh if g == 0 else 1 - zh)
+            keep[self.half, g] = acc[:, y]
+            send_y[self.half, g] = acc[:, 1 - y].astype(LOW)
+            net.send(send_y.at[self.half, g], recv_y.at[self.half, g], self.ry + g, yp)
+
+        def fold(self, g):
+            net.got(recv_y.at[self.half, g], self.ry + g)
+            keep[self.half, g] += recv_y[self.half, g].astype(F32)
+            send_z[self.half, g] = keep[self.half, g, 1 - zl].astype(LOW)
+            net.send(send_z.at[self.half, g], recv_z.at[self.half, g], self.rz + g, z_peers[1])
+
+        def cross(self):
+            net.got(recv_z.at[self.half, 1], self.rz + 1)
+            send_z[self.half, 2] = (
+                keep[self.half, 1, zl] + recv_z[self.half, 1].astype(F32)
+            ).astype(LOW)
+            net.send(send_z.at[self.half, 2], recv_z.at[self.half, 2], self.rz + 2, z_peers[2])
+
+        def done(self):
+            net.got(recv_z.at[self.half, 0], self.rz)
+            net.got(recv_z.at[self.half, 2], self.rz + 2)
+            total[self.half] = (
+                keep[self.half, 0, zl]
+                + recv_z[self.half, 0].astype(F32)
+                + recv_z[self.half, 2].astype(F32)
+            )
+
+    def columns(half, pair):
+        return pl.ds(pl.multiple_of((half * 2 + pair) * PAIR, PAIR), PAIR)
 
     def put(h, part):
-        part = part.reshape(2, MINE, D)
+        part = part.reshape(2, 2, PART, D)
 
         @pl.when(h == 0)
         def _():
@@ -715,9 +780,9 @@
         def _():
             acc[...] += part
 
-    def forward_pairs(there):
+    def forward_pairs(half, pair):
         def one(h, carry):
-            block = got_mid[there].reshape(PAIR, D)
+            block = got_mid[half, pair].reshape(PAIR, D)
             gate = nt(block, w_gu[0, h])
             upward = nt(block, w_gu[1, h])
             square = gate * gate
@@ -728,10 +793,10 @@
                 SQRT_2_OVER_PI * (1.0 + 3.0 * CUBIC * square)
             )
             low = (gelu * upward).astype(LOW)
-            slope_gate[h, there] = (upward * slope).astype(LOW)
-            slope_up[h, there] = gelu.astype(LOW)
+            slope_gate[h, half, pair] = (upward * slope).astype(LOW)
+            slope_up[h, half, pair] = gelu.astype(LOW)
             put(h, nn(low, w_dn[h]))
-            hidden_t[h, :, columns(there)] = low.T
+            hidden_t[h, :, columns(half, pair)] = low.T
             return carry
 
         lax.fori_loop(0, 2, one, 0)
@@ -740,42 +805,82 @@
         for t in range(2):
             net.got(all_gu.at[t, 1 - x, c], w_two + t)
         net.got(all_dn.at[c, 1 - x], w_two + 2)
+        net.settle_moves()
         net.send(all_gu.at[:, :, c], all_gu.at[:, :, c], w_c, cp)
         net.send(all_dn.at[c], all_dn.at[c], w_c + 1, cp)
         net.got(all_gu.at[:, :, 1 - c], w_c)
         net.got(all_dn.at[1 - c], w_c + 1)
 
-    finish, settle, _ = moved(0, got_mid, forward_pairs, weights_here)
-    finish(3)
-    settle()
-    net.drain()
-
-    ffw_proj = total[...]
-    branch = norm_rows(ffw_proj, gains[3:4, :])
-    layer_out[...] = (middle[...] + branch).astype(LOW)
-    small[0, 5:6, :] += jnp.where(spot == 3, counted(branch), 0.0)
-    grad, gain_grad = norm_back(ffw_proj, gains[3:4, :], cot[...].astype(F32))
-    small[0, 3:4, :] = gain_grad
-    rows[1] = grad.astype(LOW)
-
-    def backward_pairs(there):
+    def forward_end(half):
+        span = pl.ds(half * PART, PART)
+        ffw_proj = total[half]
+        branch = norm_rows(ffw_proj, gains[3:4, :])
+        layer_out[half, 0] = (middle[span, :] + branch).astype(LOW)
+        counts = jnp.sum(weight[span, 0:1] * jnp.sum(branch * branch, -1, keepdims=True))
+        small[0, 5:6, :] += jnp.where(spot == 3, counts, 0.0)
+        grad, gain_grad = norm_back(ffw_proj, gains[3:4, :], cot[half, 0].astype(F32))
+        small[0, 3:4, :] += gain_grad
+        rows[1, half] = grad.astype(LOW)
+
+    def backward_pairs(half, pair):
         def one(h, carry):
-            block = got_up[there].reshape(PAIR, D)
+            block = got_up[half, pair].reshape(PAIR, D)
             back = nt(block, w_dn[h])
-            gate = (back * slope_gate[h, there].astype(F32)).astype(LOW)
-            upward = (back * slope_up[h, there].astype(F32)).astype(LOW)
+            gate = (back * slope_gate[h, half, pair].astype(F32)).astype(LOW)
+            upward = (back * slope_up[h, half, pair].astype(F32)).astype(LOW)
             put(h, nn(gate, w_gu[0, h]) + nn(upward, w_gu[1, h]))
-            gate_t[h, :, columns(there)] = gate.T
-            up_t[h, :, columns(there)] = upward.T
+            slope_gate[h, half, pair] = gate
+            slope_up[h, half, pair] = upward
             return carry
 
         lax.fori_loop(0, 2, one, 0)
 
-    finish, settle, gathered = moved(1, got_up, backward_pairs, lambda: None)
-    finish(3)
+    one, two = Half(0, 0, got_mid, forward_pairs), Half(0, 1, got_mid, forward_pairs)
+    one.start()
+    one.hop(1)
+    two.start()
+    one.hop(2)
+    weights_here()
+    one.group(0)
+    two.hop(1)
+    one.hop(3)
+    two.hop(2)
+    one.group(1)
+    one.fold(0)
+    two.hop(3)
+    two.group(0)
+    one.fold(1)
+    two.group(1)
+    one.cross()
+    two.fold(0)
+    one.done()
+    forward_end(0)
+    three, four = Half(1, 0, got_up, backward_pairs), Half(1, 1, got_up, backward_pairs)
+    three.start()
+    two.fold(1)
+    three.hop(1)
+    two.cross()
+    three.hop(2)
+    two.done()
+    forward_end(1)
+    four.start()
+    net.flush([copy for copy in net.sent if not any(copy is other for other in three.gathered + four.gathered)])
+    three.group(0)
+    four.hop(1)
+    three.hop(3)
+    four.hop(2)
+    three.group(1)
+    three.fold(0)
+    four.hop(3)
+    four.group(0)
+    three.fold(1)
 
     step = 384
     flat_mid, flat_up = got_mid.reshape(8 * MINE, D), got_up.reshape(8 * MINE, D)
+
+    four.group(1)
+    three.cross()
+    four.fold(0)
 
     def down_grads(i, carry):
         h, cols = i // 3, pl.ds(pl.multiple_of(i % 3 * step, 128), step)
@@ -783,28 +888,52 @@
         return carry
 
     lax.fori_loop(0, 6, down_grads, 0)
-    d_c, d_x, d_home = net.slots(4), net.slots(4), net.slots(3)
+    d_c, d_x, d_home = net.slots(5), net.slots(4), net.slots(3)
     net.send(all_dn.at[1 - c], n0, d_c, cp)
-
-    def gate_up_grads(i, carry):
-        h, cols = i // 3, pl.ds(pl.multiple_of(i % 3 * step, 128), step)
-        w_gu[0, h, :, cols] = nn(gate_t[h], flat_mid[:, cols]).astype(LOW)
-        w_gu[1, h, :, cols] = nn(up_t[h], flat_mid[:, cols]).astype(LOW)
-        return carry
-
-    lax.fori_loop(0, 6, gate_up_grads, 0)
-    net.send(all_gu.at[:, :, 1 - c], g0, d_c + 1, cp)
-    settle()
+    four.fold(1)
+    three.done()
+
+    def gate_up_grads(t, h, slopes):
+        hidden_t[h] = slopes[h].reshape(8 * MINE, WIDE).T
+
+        def part(i, carry):
+            cols = pl.ds(pl.multiple_of(i * step, 128), step)
+            w_gu[t, h, :, cols] = nn(hidden_t[h], flat_mid[:, cols]).astype(LOW)
+            return carry
+
+        lax.fori_loop(0, 3, part, 0)
+
+    for h in range(2):
+        gate_up_grads(0, h, slope_gate)
+    net.send(all_gu.at[0, :, 1 - c], g0.at[0], d_c + 1, cp)
+    net.got(n0, d_c)
+    for q in range(2):
+        all_dn[c, q] = added(all_dn[c, q], n0[q])
+    net.send(all_dn.at[c, 1 - x], n1, d_x, xp)
+    four.cross()
+    for h in range(2):
+        gate_up_grads(1, h, slope_up)
+    net.send(all_gu.at[1, :, 1 - c], g0.at[1], d_c + 2, cp)
+
+    def share(t):
+        net.got(g0.at[t], d_c + 1 + t)
+        for h in range(2):
+            all_gu[t, h, c] = added(all_gu[t, h, c], g0[t, h])
+        net.send(all_gu.at[t, 1 - x, c], g1.at[t], d_x + 1 + t, xp)
+
+    share(0)
+    share(1)
+    four.done()
 
     mid = middle[...]
-    grad, gain_grad = norm_back(mid, gains[2:3, :], total[...])
+    grad, gain_grad = norm_back(mid, gains[2:3, :], total[...].reshape(MINE, D))
     small[0, 2:3, :] = gain_grad
-    grad_mid = cot[...].astype(F32) + grad
+    grad_mid = stream_of(cot) + grad
     grad_middle[...] = grad_mid
     grad, gain_grad = norm_back(attn_proj[...], gains[1:2, :], grad_mid)
     small[0, 1:2, :] = gain_grad
     grad_attn[...] = grad.astype(LOW)
-    net.flush(gathered)
+    net.flush(three.gathered + four.gathered)
     d_out = got_up.reshape(4, 2, 2, 2, 32, D)
     a0 = got_mid.reshape(8 * MINE, D).at[pl.ds(0, 16 * 48)].reshape(4, 2, 2, 48, D)
     b0 = recv_y.reshape(4, 2, 2, 32, D)
@@ -815,17 +944,112 @@
         return carry
 
     lax.fori_loop(0, HEADS, out_grads, 0)
-    net.got(n0, d_c)
-    net.got(g0, d_c + 1)
-    net.send(d_out.at[:, :, :, 1 - c], b0, d_c + 2, cp)
-
-    for q in range(2):
-        all_dn[c, q] = added(all_dn[c, q], n0[q])
-    net.send(all_dn.at[c, 1 - x], n1, d_x, xp)
-    for t in range(2):
-        for h in range(2):
-            all_gu[t, h, c] = added(all_gu[t, h, c], g0[t, h])
-    net.send(all_gu.at[:, 1 - x, c], g1, d_x + 1, xp)
+    net.send(d_out.at[:, :, :, 1 - c], b0, d_c + 3, cp)
+
+    def home_down():
+        net.got(n1, d_x)
+        all_dn[c, x] = added(all_dn[c, x], n1[...])
+        net.move(
+            z % 2 == y,
+            all_dn.at[c, x],
+            n2,
+            d_home + 2,
+            d_home + 2,
+            at(2 * (z // 2) + y, z % 2, x, c),
+        )
+
+    def home_gate_up(t):
+        net.got(g1.at[t], d_x + 1 + t)
+        all_gu[t, x, c] = added(all_gu[t, x, c], g1[t])
+        source = z // 2 + 2 * t
+        net.move(
+            jnp.logical_and(source == z, z % 2 == x),
+            all_gu.at[t, x, c],
+            g2.at[x],
+            d_home + t,
+            d_home + x,
+            at(source, y, z % 2, c),
+        )
+
+    class Collect:
+        def __init__(self, grads, core_in, y_in, x_in, z_in, core_slot):
+            self.grads, self.core_in, self.y_in, self.x_in, self.z_in = (
+                grads,
+                core_in,
+                y_in,
+                x_in,
+                z_in,
+            )
+            self.cs, self.ys, self.xs, self.zs = core_slot, net.slots(2), net.slots(2), net.slots(2)
+
+        def cores(self):
+            net.got(self.core_in, self.cs)
+            for part, pair in enumerate((1 - zh, zh)):
+
+                def one(i, carry):
+                    p, q, r = 2 * pair + i // 4, i // 2 % 2, i % 2
+                    self.grads[p, q, r, c] = added(self.grads[p, q, r, c], self.core_in[p, q, r])
+                    return carry
+
+                lax.fori_loop(0, 8, one, 0)
+                both = pl.ds(2 * pair, 2)
+                net.send(
+                    self.grads.at[both, 1 - y, :, c], self.y_in.at[part], self.ys + part, yp
+                )
+
+        def ys_in(self, part):
+            pair = (1 - zh, zh)[part]
+            net.got(self.y_in.at[part], self.ys + part)
+
+            def one(i, carry):
+                p, q = i // 2, i % 2
+                there = 2 * pair + p
+                self.grads[there, y, q, c] = added(
+                    self.grads[there, y, q, c], self.y_in[part, p, q]
+                )
+                return carry
+
+            lax.fori_loop(0, 4, one, 0)
+            net.send(
+                self.grads.at[pl.ds(2 * pair, 2), y, 1 - x, c],
+                self.x_in.at[part],
+                self.xs + part,
+                xp,
+            )
+
+        def xs_in(self, part):
+            pair = (1 - zh, zh)[part]
+            net.got(self.x_in.at[part], self.xs + part)
+            for p in range(2):
+                there = 2 * pair + p
+                self.grads[there, y, x, c] = added(
+                    self.grads[there, y, x, c], self.x_in[part, p]
+                )
+            net.send(
+                self.grads.at[2 * pair + 1 - zl, y, x, c],
+                self.z_in.at[part],
+                self.zs + part,
+                z_peers[1],
+            )
+
+        def cross(self, slot):
+            net.got(self.z_in.at[0], self.zs)
+            there = 2 * (1 - zh) + zl
+            self.grads[there, y, x, c] = added(self.grads[there, y, x, c], self.z_in[0])
+            net.send(self.grads.at[there, y, x, c], self.z_in.at[2], slot, z_peers[2])
+
+        def done(self, slot, result):
+            net.got(self.z_in.at[1], self.zs + 1)
+            net.got(self.z_in.at[2], slot)
+            result[...] = (
+                self.grads[z, y, x, c].astype(F32)
+                + self.z_in[1].astype(F32)
+                + self.z_in[2].astype(F32)
+            )
+
+    r_s, r_z = net.slots(8), net.slots(2)
+    outs = Collect(d_out, b0, b1, b2, b3, d_c + 3)
+    ins = Collect(d_in, a0, a1, a2, a3, d_c + 4)
 
     grad_heads[...] = jnp.zeros((6, MINE, HD), F32)
 
@@ -863,117 +1087,63 @@
     small[0, 4:5, 0:HD] = key_acc[0:1, :]
     small[0, 4:5, HD : 2 * HD] = key_acc[1:2, :]
 
-    r_a, r_b, r_s = net.slots(8), net.slots(8), net.slots(8)
-    net.got(b0, d_c + 2)
-
-    def sum_out(i, carry):
-        p, q, r = i // 4, i // 2 % 2, i % 2
-        d_out[p, q, r, c] = added(d_out[p, q, r, c], b0[p, q, r])
-        return carry
-
-    lax.fori_loop(0, 16, sum_out, 0)
-    net.send(d_out.at[:, :, 1 - x, c], b1, r_b, xp)
+    outs.cores()
 
     def in_grads(j, carry):
         flat_d_in[rows_of(j), :] = tn(grad_proj[j], normed_in[...]).astype(LOW)
         return carry
 
     lax.fori_loop(0, HEADS + 2, in_grads, 0)
-    net.send(d_in.at[:, :, :, 1 - c], a0, d_c + 3, cp)
-    total[...] = jnp.zeros((MINE, D), F32)
+    net.send(d_in.at[:, :, :, 1 - c], a0, d_c + 4, cp)
+    home_down()
+    total[...] = jnp.zeros((2, PART, D), F32)
 
     def in_back(j, carry):
-        total[...] += nn(grad_proj[j], flat_in[rows_of(j), :])
+        total[...] += nn(grad_proj[j], flat_in[rows_of(j), :]).reshape(2, PART, D)
         return carry
 
     lax.fori_loop(0, HEADS + 2, in_back, 0)
-    grad, gain_grad = norm_back(x_ref[...].astype(F32), gains[0:1, :], total[...])
+    ins.cores()
+    grad, gain_grad = norm_back(stream_of(x_ref), gains[0:1, :], total[...].reshape(MINE, D))
     small[0, 0:1, :] = gain_grad
-    input_grad[...] = grad_middle[...] + grad
+    input_grad[...] = (grad_middle[...] + grad).reshape(2, 1, PART, D)
     net.send(small.at[0], small.at[1], r_s, cp)
-
-    net.got(a0, d_c + 3)
-
-    def sum_in(i, carry):
-        p, q, r = i // 4, i // 2 % 2, i % 2
-        d_in[p, q, r, c] = added(d_in[p, q, r, c], a0[p, q, r])
-        return carry
-
-    lax.fori_loop(0, 16, sum_in, 0)
-    net.send(d_in.at[:, 1 - y, :, c], a1, r_a, yp)
+    home_gate_up(0)
+    outs.ys_in(0)
+    outs.ys_in(1)
     net.got(small.at[1], r_s)
     small[2] = small[0] + small[1]
     net.send(small.at[2], small.at[3], r_s + 1, xp)
-    net.got(b1, r_b)
-
-    def sum_out_two(i, carry):
-        p, q = i // 2, i % 2
-        d_out[p, q, x, c] = added(d_out[p, q, x, c], b1[p, q])
-        return carry
-
-    lax.fori_loop(0, 8, sum_out_two, 0)
-    net.send(d_out.at[:, 1 - y, x, c], b2, r_b + 1, yp)
-
-    net.got(n1, d_x)
-    all_dn[c, x] = added(all_dn[c, x], n1[...])
-    net.move(
-        z % 2 == y, all_dn.at[c, x], n2, d_home + 2, d_home + 2, at(2 * (z // 2) + y, z % 2, x, c)
-    )
-    net.got(g1, d_x + 1)
-    for t in range(2):
-        all_gu[t, x, c] = added(all_gu[t, x, c], g1[t])
-        source = z // 2 + 2 * t
-        net.move(
-            jnp.logical_and(source == z, z % 2 == x),
-            all_gu.at[t, x, c],
-            g2.at[x],
-            d_home + t,
-            d_home + x,
-            at(source, y, z % 2, c),
-        )
-
-    net.got(a1, r_a)
-
-    def sum_in_two(i, carry):
-        p, q = i // 2, i % 2
-        d_in[p, y, q, c] = added(d_in[p, y, q, c], a1[p, q])
-        return carry
-
-    lax.fori_loop(0, 8, sum_in_two, 0)
-    net.send(d_in.at[:, y, 1 - x, c], a2, r_a + 1, xp)
+    ins.ys_in(0)
+    home_gate_up(1)
+    outs.xs_in(0)
+    outs.xs_in(1)
     net.got(small.at[3], r_s + 1)
     small[4] = small[2] + small[3]
     net.send(small.at[4], small.at[5], r_s + 2, yp)
-    net.got(b2, r_b + 1)
-    for p in range(4):
-        d_out[p, y, x, c] = added(d_out[p, y, x, c], b2[p])
-    for k in (1, 2, 3):
-        net.send(d_out.at[z_peer(z, k), y, x, c], b3.at[k - 1], r_b + 1 + k, z_peers[k])
-    net.got(a2, r_a + 1)
-    for p in range(4):
-        d_in[p, y, x, c] = added(d_in[p, y, x, c], a2[p])
-    for k in (1, 2, 3):
-        net.send(d_in.at[z_peer(z, k), y, x, c], a3.at[k - 1], r_a + 1 + k, z_peers[k])
+    ins.ys_in(1)
+    outs.cross(r_z)
+    ins.xs_in(0)
+    ins.xs_in(1)
     net.got(small.at[5], r_s + 2)
     small[6] = small[4] + small[5]
     for k in (1, 2, 3):
         net.send(small.at[6], small.at[6 + k], r_s + 2 + k, z_peers[k])
-
-    for k in (1, 2, 3):
-        net.got(b3.at[k - 1], r_b + 1 + k)
-    o_out[...] = (d_out[z, y, x, c].astype(F32) + b3[0].astype(F32)) + (
-        b3[1].astype(F32) + b3[2].astype(F32)
-    )
+    ins.cross(r_z + 1)
+    outs.done(r_z, o_out)
     net.got(n2, d_home + 2)
     o_dn[...] = n2[...].astype(F32)[:BLOCK]
     for k in (1, 2, 3):
-        net.got(a3.at[k - 1], r_a + 1 + k)
-    o_in[...] = (d_in[z, y, x, c].astype(F32) + a3[0].astype(F32)) + (
-        a3[1].astype(F32) + a3[2].astype(F32)
-    )
-    for k in (1, 2, 3):
         net.got(small.at[6 + k], r_s + 2 + k)
-    o_small[...] = (small[6] + small[7]) + (small[8] + small[9])
+    sums = (small[6] + small[7]) + (small[8] + small[9])
+    o_gains[...] = sums[0:4, :]
+    o_heads[...] = jnp.concatenate([sums[4:5, 0:HD], sums[4:5, HD : 2 * HD]], 0)
+    scaled = sums[5:6, :]
+    tokens = jnp.sum(jnp.where(spot == 4, scaled, 0.0), -1, keepdims=True)
+    means = jnp.sqrt(scaled / (tokens * D))
+    for i in range(4):
+        o_rms[i] = jnp.sum(jnp.where(spot == i, means, 0.0))
+    ins.done(r_z + 1, o_in)
     for h in range(2):
         net.got(g2.at[h], d_home + h)
         o_gu[pl.ds(h * BLOCK, BLOCK), :] = g2[h].astype(F32)[:BLOCK]
@@ -1006,21 +1176,19 @@
         vm(4, MINE, HD),
         vf(MINE, D),
         vf(MINE, D),
-        vm(2, MINE, D),
-        vf(MINE, D),
-        vm(4, 2, MINE, D),
-        vm(4, 2, MINE, D),
+        vm(2, 2, PART, D),
+        vf(2, PART, D),
+        vm(2, 2, 2, 2, PART, D),
+        vm(2, 2, 2, 2, PART, D),
         vm(2, WIDE, 8 * MINE),
-        vm(2, 4, PAIR, WIDE),
-        vm(2, 4, PAIR, WIDE),
-        vm(2, WIDE, 8 * MINE),
-        vm(2, WIDE, 8 * MINE),
-        vf(2, MINE, D),
-        vf(2, MINE, D),
-        vm(4, MINE, D),
-        vm(4, MINE, D),
-        vm(3, MINE, D),
-        vm(3, MINE, D),
+        vm(2, 2, 2, PAIR, WIDE),
+        vm(2, 2, 2, PAIR, WIDE),
+        vf(2, 2, PART, D),
+        vf(2, 2, 2, PART, D),
+        vm(2, 2, 2, PART, D),
+        vm(2, 2, 2, PART, D),
+        vm(2, 3, PART, D),
+        vm(2, 3, PART, D),
         vf(MINE, D),
         vm(MINE, D),
         vf(6, MINE, HD),
@@ -1029,24 +1197,26 @@
         vm(4, 2, 2, 2, 48, D),
     ]
     for count in (48, 32):
-        scratch += [vm(4, 2, count, D), vm(4, count, D), vm(3, count, D)]
+        scratch += [vm(2, 2, 2, count, D), vm(2, 2, count, D), vm(3, count, D)]
     scratch += [vm(2, 2, PADDED, D), vm(2, PADDED, D), vm(2, PADDED, D)]
     scratch += [vm(2, PADDED, D), vm(PADDED, D), vm(PADDED, D)]
     scratch += [vf(10, 8, D)]
-    scratch += [pltpu.SemaphoreType.DMA((2,))] + [pltpu.SemaphoreType.DMA((112,))] * 2
+    scratch += [pltpu.SemaphoreType.DMA((2,))] + [pltpu.SemaphoreType.DMA((144,))] * 2
     return pl.pallas_call(
         layer_kernel,
         out_shape=(
-            jax.ShapeDtypeStruct((MINE, D), LOW),
-            jax.ShapeDtypeStruct((MINE, D), F32),
+            jax.ShapeDtypeStruct((2, 1, PART, D), LOW),
+            jax.ShapeDtypeStruct((2, 1, PART, D), F32),
             jax.ShapeDtypeStruct((48, D), F32),
             jax.ShapeDtypeStruct((32, D), F32),
             jax.ShapeDtypeStruct((2 * BLOCK, D), F32),
             jax.ShapeDtypeStruct((BLOCK, D), F32),
-            jax.ShapeDtypeStruct((8, D), F32),
+            jax.ShapeDtypeStruct((4, D), F32),
+            jax.ShapeDtypeStruct((2, HD), F32),
+            jax.ShapeDtypeStruct((4,), F32),
         ),
         in_specs=[vmem] * 10,
-        out_specs=(vmem,) * 7,
+        out_specs=(vmem,) * 8 + (pl.BlockSpec(memory_space=pltpu.SMEM),),
         scratch_shapes=scratch,
         compiler_params=pltpu.CompilerParams(
             collective_id=1, has_side_effects=True, vmem_limit_bytes=VMEM_BYTES
@@ -1055,8 +1225,31 @@
     )(x, seg, valid, ain, aout, gu, dn, gains, head_gains, cot)
 
 
-def padded_rows(rows):
-    return jnp.pad(rows, ((0, 0), (0, PADDED - BLOCK), (0, 0)))
+def copy_kernel(*refs):
+    count = (len(refs) - 2) // 3
+    given, made, held = refs[:count], refs[count : 2 * count], refs[2 * count : 3 * count]
+    into = [pltpu.make_async_copy(a, b, refs[-2].at[i]) for i, (a, b) in enumerate(zip(given, held))]
+    out = [pltpu.make_async_copy(a, b, refs[-1].at[i]) for i, (a, b) in enumerate(zip(held, made))]
+    for copy in into:
+        copy.start()
+    for first, second in zip(into, out):
+        first.wait()
+        second.start()
+    for copy in out:
+        copy.wait()
+
+
+def copied(arrays):
+    place = pl.BlockSpec(memory_space=pl.ANY)
+    return pl.pallas_call(
+        copy_kernel,
+        out_shape=tuple(jax.ShapeDtypeStruct(array.shape, array.dtype) for array in arrays),
+        in_specs=[place] * len(arrays),
+        out_specs=(place,) * len(arrays),
+        scratch_shapes=[pltpu.VMEM(array.shape, array.dtype) for array in arrays]
+        + [pltpu.SemaphoreType.DMA((len(arrays),))] * 2,
+        name="results",
+    )(*arrays)
 
 
 def split_shards(
@@ -1071,29 +1264,19 @@
     head_gains,
     cotangent,
 ):
-    layer_out, input_grad, shard_in, shard_out, shard_gu, shard_dn, small = whole_layer(
-        inputs.reshape(MINE, D),
-        segment_ids.reshape(1, MINE),
-        valid_mask.reshape(1, MINE),
+    results = whole_layer(
+        inputs,
+        segment_ids,
+        valid_mask,
         attn_in,
         attn_out,
-        padded_rows(ffw_in.reshape(2, BLOCK, D)),
-        padded_rows(ffw_out.reshape(1, BLOCK, D))[0],
+        ffw_in,
+        ffw_out,
         norm_gains,
         head_gains,
-        cotangent.reshape(MINE, D),
+        cotangent,
     )
-    return (
-        layer_out.reshape(inputs.shape),
-        input_grad.reshape(inputs.shape),
-        shard_in,
-        shard_out,
-        shard_gu,
-        shard_dn,
-        small[:4],
-        small[4, : 2 * HD].reshape(2, HD),
-        jnp.sqrt(small[5, :4] / (small[5, 4] * D)),
-    )
+    return copied(results[:-1]) + results[-1:]
 
 
 def solution(mesh):

time: 369 us -> 310 us (0.84)
  Pallas kernels: 340 us -> 303 us
  local copies, waits for them, and re-layouts: 18.7 us -> 0.52 us
  other arithmetic: 3.88 us -> 0 us
    pallas_call x1 -> x2, Pallas kernels: 340 us -> 303 us  [the longest x1 299 us: whole_layer(): pl.pallas_call(layer_kernel, out_shape=(jax.ShapeDtypeStruct((2, 1, PART,...]
    unnamed x13 -> x3, local copies, waits for them, and re-layouts: 9.29 us -> 0.52 us
where the time goes in v3:
time: 310 us; the launch traced here: 304 us
  Pallas kernels  303 us (98%)
    pallas_call x1, Pallas kernels, whole_layer(): pl.pallas_call(layer_kernel, out_shape=(jax.ShapeDtypeStruct((2, 1, PART,...  299 us

profile of v3, /device:TPU:22, one launch (start us, length us, event | category | flops | bytes accessed | tf_op | source)
XLA Modules:
  0.0 304.3 jit_solution(9642540796509873772)
XLA Ops:
  0.6 299.3 %layer.1 = (bf16[2,1,64,1152]{3,2,1,0:T(8,128)(2,1)}, f32[2,1,64,1152]{3,2,1,0:T(8,128)}, f32[48,1152]{1,0:T(8,128)}, f32[32,1152]{1,0:T(8,128)}, f32[432,1152]{...) custom-call(bf16[2,1,64,1152]{3,2,1,0:T(8,128)(2,1)} %refs_0_.1, ...), custom_call_target="tpu_custom_call" | custom-call | tf_op jit(solution)/shard_map/layer/pallas_call | solution.py:1205
  300.0 0.0 copy-start
  300.0 3.7 %results.1 = (bf16[2,1,64,1152]{3,2,1,0:T(8,128)(2,1)}, f32[2,1,64,1152]{3,2,1,0:T(8,128)}, f32[48,1152]{1,0:T(8,128)}, f32[32,1152]{1,0:T(8,128)}, f32[432,1152...) custom-call(bf16[2,1,64,1152]{3,2,1,0:T(8,128)(2,1)} %get-tuple-element.26.refs_0_, ...), custom_call_target="tpu_custom_call" | custom-call | tf_op jit(solution)/shard_map/results/pallas_call | solution.py:1244
  303.7 0.0 copy-done
  303.8 0.5 copy.20
Async XLA Ops:
  300.0 3.8 %copy-start = (f32[4]{0:T(128)S(1)}, f32[4]{0:T(128)}, u32[]{:S(2)}) copy-start(f32[4]{0:T(128)} %get-tuple-element.60) | copy-start | bytes 52

commit v4 on v3

--- a/solution.py
+++ b/solution.py
@@ -496,6 +496,7 @@
         g0,
         g1,
         g2,
+        d_dn,
         n0,
         n1,
         n2,
@@ -515,16 +516,26 @@
     greet_all(me)
 
     class Spread:
-        def __init__(self, own, full):
-            self.own, self.full = own, full
+        def __init__(self, own, full, x_first):
+            self.own, self.full, self.x_first = own, full, x_first
+            self.first, self.second = (xp, yp) if x_first else (yp, xp)
             self.az, self.ax, self.ay, self.ac = (net.slots(4) for _ in range(4))
 
         def block(self, k):
             return self.full.at[z_peer(z, k), y, x, c]
 
+        def crossed(self, k):
+            there = z_peer(z, k)
+            return self.full.at[there, y, 1 - x, c] if self.x_first else self.full.at[there, 1 - y, x, c]
+
+        def pair(self, there, own, core):
+            if self.x_first:
+                return self.full.at[there, y if own else 1 - y, :, core]
+            return self.full.at[there, :, x if own else 1 - x, core]
+
         def start(self):
             net.send(self.own, self.block(0), self.az + 1, z_peers[1])
-            net.send(self.own, self.block(0), self.ax, xp)
+            net.send(self.own, self.block(0), self.ax, self.first)
             net.send(self.own, self.block(0), self.az + 2, z_peers[2])
 
         def hop(self, k):
@@ -532,32 +543,32 @@
             net.got(block, self.az + k)
             if k == 2:
                 net.send(block, block, self.az + 3, z_peers[1])
-            net.send(block, block, self.ax + k, xp)
+            net.send(block, block, self.ax + k, self.first)
 
         def turn(self, k):
-            there = z_peer(z, k)
-            net.got(self.full.at[there, y, 1 - x, c], self.ax + k)
-            pair = self.full.at[there, y, :, c]
-            net.send(pair, pair, self.ay + k, yp)
+            net.got(self.crossed(k), self.ax + k)
+            pair = self.pair(z_peer(z, k), True, c)
+            net.send(pair, pair, self.ay + k, self.second)
 
         def near(self):
-            part = self.full.at[:, y, :, c]
+            part = self.pair(slice(None), True, c)
             net.send(part, part, self.ac, cp)
 
         def far(self):
             for k in range(4):
-                net.got(self.full.at[z_peer(z, k), 1 - y, :, c], self.ay + k)
-            part = self.full.at[:, 1 - y, :, c]
+                net.got(self.pair(z_peer(z, k), False, c), self.ay + k)
+            part = self.pair(slice(None), False, c)
             net.send(part, part, self.ac + 1, cp)
 
         def whole(self):
-            net.got(self.full.at[:, y, :, 1 - c], self.ac)
-            net.got(self.full.at[:, 1 - y, :, 1 - c], self.ac + 1)
-
-    into, outof = Spread(ain, all_in), Spread(aout, all_out)
+            net.got(self.pair(slice(None), True, 1 - c), self.ac)
+            net.got(self.pair(slice(None), False, 1 - c), self.ac + 1)
+
+    into, outof = Spread(ain, all_in, True), Spread(aout, all_out, False)
     into.start()
-    w_one, w_two, w_c = net.slots(3), net.slots(3), net.slots(2)
-    kind, goal = z // 2, 2 * (z % 2) + x
+    w_one, w_two, w_c, w_d = net.slots(2), net.slots(2), net.slots(2), net.slots(2)
+    v_x, v_one, v_c = net.slots(1), net.slots(2), net.slots(1)
+    kind, goal = z // 2, 2 * (z % 2) + c
     blank = jnp.zeros((PADDED - BLOCK, D), F32)
     for h in range(2):
         part = gu[pl.ds(h * BLOCK, BLOCK), :].astype(F32)
@@ -567,22 +578,55 @@
     def rows_out():
         for h in range(2):
             net.move(
-                jnp.logical_and(goal == z, x == h),
+                jnp.logical_and(goal == z, c == h),
                 g0.at[0, h],
-                all_gu.at[kind, h, c],
+                all_gu.at[kind, h, x],
                 w_one + h,
                 w_one + kind,
-                at(goal, y, h, c),
+                at(goal, y, x, h),
             )
-        net.move(
-            z % 2 == y,
-            n0.at[0],
-            all_dn.at[c, x],
-            w_one + 2,
-            w_one + 2,
-            at(2 * (z // 2) + y, z % 2, x, c),
-        )
-
+
+    def rows_on(which):
+        t = (kind, 1 - kind)[which]
+        block = all_gu.at[t, c, x]
+        net.got(block, w_one + t)
+        net.send(block, block, w_two + which, xp)
+        net.send(block, block, w_c + which, cp)
+
+    def rows_across(which):
+        block = all_gu.at[(kind, 1 - kind)[which], c, 1 - x]
+        net.got(block, w_two + which)
+        net.send(block, block, w_d + which, cp)
+
+    def rows_whole():
+        for which in range(2):
+            t = (kind, 1 - kind)[which]
+            net.got(all_gu.at[t, 1 - c, x], w_c + which)
+            net.got(all_gu.at[t, 1 - c, 1 - x], w_d + which)
+        net.got(all_dn.at[1 - c], v_c)
+
+    net.send(n0.at[0], n0.at[1], v_x, xp)
+    across_x = net.sent[-1]
+
+    def down_out():
+        net.got(n0.at[1], v_x)
+        for other in range(2):
+            block_x = 1 - x if other else x
+            net.move(
+                jnp.logical_and(z % 2 == block_x, z % 2 == y),
+                n0.at[other],
+                all_dn.at[c, y],
+                v_one + other,
+                v_one + y,
+                at(2 * (z // 2) + block_x, z % 2, x, c),
+            )
+
+    def down_on():
+        for q in range(2):
+            net.got(all_dn.at[c, q], v_one + q)
+        net.send(all_dn.at[c], all_dn.at[c], v_c, cp)
+
+    rows_out()
     into.hop(1)
     into.hop(2)
     outof.start()
@@ -591,7 +635,6 @@
     into.turn(0)
     into.turn(1)
     into.hop(3)
-    rows_out()
 
     def along_lanes(ref):
         return jnp.concatenate([ref[0].astype(F32), ref[1].astype(F32)], 1)
@@ -619,14 +662,17 @@
     outof.hop(1)
     outof.hop(2)
     into.turn(3)
+    down_out()
     into.near()
     outof.turn(0)
     outof.turn(1)
     outof.hop(3)
+    rows_on(0)
     into.far()
     outof.turn(2)
     outof.turn(3)
     outof.near()
+    rows_on(1)
     into.whole()
 
     flat_in = all_in.reshape(HEADS * HD + 2 * HD, D)
@@ -654,6 +700,7 @@
         return carry
 
     lax.fori_loop(0, HEADS + 2, project, 0)
+    down_on()
     outof.far()
 
     def attend_head(j, carry):
@@ -668,14 +715,7 @@
         return carry
 
     lax.fori_loop(0, HEADS, attend_head, 0)
-    for t in range(2):
-        block = all_gu.at[t, x, c]
-        net.got(block, w_one + t)
-        net.send(block, block, w_two + t, xp)
-    block = all_dn.at[c, x]
-    net.got(block, w_one + 2)
-    net.send(block, block, w_two + 2, xp)
-
+    rows_across(0)
     outof.whole()
 
     attn_proj[...] = jnp.zeros((MINE, D), F32)
@@ -709,7 +749,7 @@
         def __init__(self, which, half, got_all, compute):
             self.which, self.half, self.got_all, self.compute = which, half, got_all, compute
             self.az, self.ay, self.ry, self.rz = (net.slots(4) for _ in range(4))
-            self.gathered = []
+            self.gathered, self.here = [], set()
 
         def block(self, k, yy):
             there = z_peer(z, k)
@@ -736,9 +776,14 @@
                 self.pass_on(block, self.az + 3, z_peers[1])
             self.pass_on(block, self.ay + k, yp)
 
+        def arrive(self, g):
+            if g not in self.here:
+                for k in (2 * g, 2 * g + 1):
+                    net.got(self.block(k, 1 - y), self.ay + k)
+            self.here.add(g)
+
         def group(self, g):
-            for k in (2 * g, 2 * g + 1):
-                net.got(self.block(k, 1 - y), self.ay + k)
+            self.arrive(g)
             self.compute(self.half, zh if g == 0 else 1 - zh)
             keep[self.half, g] = acc[:, y]
             send_y[self.half, g] = acc[:, 1 - y].astype(LOW)
@@ -802,14 +847,10 @@
         lax.fori_loop(0, 2, one, 0)
 
     def weights_here():
-        for t in range(2):
-            net.got(all_gu.at[t, 1 - x, c], w_two + t)
-        net.got(all_dn.at[c, 1 - x], w_two + 2)
         net.settle_moves()
-        net.send(all_gu.at[:, :, c], all_gu.at[:, :, c], w_c, cp)
-        net.send(all_dn.at[c], all_dn.at[c], w_c + 1, cp)
-        net.got(all_gu.at[:, :, 1 - c], w_c)
-        net.got(all_dn.at[1 - c], w_c + 1)
+        net.flush([across_x])
+        rows_across(1)
+        rows_whole()
 
     def forward_end(half):
         span = pl.ds(half * PART, PART)
@@ -878,20 +919,20 @@
     step = 384
     flat_mid, flat_up = got_mid.reshape(8 * MINE, D), got_up.reshape(8 * MINE, D)
 
+    four.arrive(1)
+
+    def down_grads(i, carry):
+        h, cols = i // 3, pl.ds(pl.multiple_of(i % 3 * step, 128), step)
+        d_dn.reshape(2, WIDE, D)[h, :, cols] = nn(hidden_t[h], flat_up[:, cols]).astype(LOW)
+        return carry
+
+    lax.fori_loop(0, 6, down_grads, 0)
+    d_c, d_x, d_home, d_y = net.slots(5), net.slots(2), net.slots(2), net.slots(2)
+    kept = (x + y + z) % 2
+    net.send(d_dn.at[1 - c], n0, d_c, cp)
     four.group(1)
     three.cross()
     four.fold(0)
-
-    def down_grads(i, carry):
-        h, cols = i // 3, pl.ds(pl.multiple_of(i % 3 * step, 128), step)
-        w_dn[h, :, cols] = nn(hidden_t[h], flat_up[:, cols]).astype(LOW)
-        return carry
-
-    lax.fori_loop(0, 6, down_grads, 0)
-    d_c, d_x, d_home = net.slots(5), net.slots(4), net.slots(3)
-    net.send(all_dn.at[1 - c], n0, d_c, cp)
-    four.fold(1)
-    three.done()
 
     def gate_up_grads(t, h, slopes):
         hidden_t[h] = slopes[h].reshape(8 * MINE, WIDE).T
@@ -905,21 +946,23 @@
 
     for h in range(2):
         gate_up_grads(0, h, slope_gate)
-    net.send(all_gu.at[0, :, 1 - c], g0.at[0], d_c + 1, cp)
+    net.send(all_gu.at[0, 1 - c], g0.at[0], d_c + 1, cp)
     net.got(n0, d_c)
     for q in range(2):
-        all_dn[c, q] = added(all_dn[c, q], n0[q])
-    net.send(all_dn.at[c, 1 - x], n1, d_x, xp)
+        d_dn[c, q] = added(d_dn[c, q], n0[q])
+    net.send(d_dn.at[c, 1 - kept], n1, d_y, xp)
+    four.fold(1)
+    three.done()
     four.cross()
     for h in range(2):
         gate_up_grads(1, h, slope_up)
-    net.send(all_gu.at[1, :, 1 - c], g0.at[1], d_c + 2, cp)
+    net.send(all_gu.at[1, 1 - c], g0.at[1], d_c + 2, cp)
 
     def share(t):
         net.got(g0.at[t], d_c + 1 + t)
-        for h in range(2):
-            all_gu[t, h, c] = added(all_gu[t, h, c], g0[t, h])
-        net.send(all_gu.at[t, 1 - x, c], g1.at[t], d_x + 1 + t, xp)
+        for q in range(2):
+            all_gu[t, c, q] = added(all_gu[t, c, q], g0[t, q])
+        net.send(all_gu.at[t, c, 1 - x], g1.at[t], d_x + t, xp)
 
     share(0)
     share(1)
@@ -947,28 +990,28 @@
     net.send(d_out.at[:, :, :, 1 - c], b0, d_c + 3, cp)
 
     def home_down():
-        net.got(n1, d_x)
-        all_dn[c, x] = added(all_dn[c, x], n1[...])
+        net.got(n1, d_y)
+        d_dn[c, kept] = added(d_dn[c, kept], n1[...])
         net.move(
-            z % 2 == y,
-            all_dn.at[c, x],
+            jnp.logical_and(z % 2 == y, x == y),
+            d_dn.at[c, kept],
             n2,
-            d_home + 2,
-            d_home + 2,
-            at(2 * (z // 2) + y, z % 2, x, c),
+            d_y + 1,
+            d_y + 1,
+            at(2 * (z // 2) + y, kept, z % 2, c),
         )
 
     def home_gate_up(t):
-        net.got(g1.at[t], d_x + 1 + t)
-        all_gu[t, x, c] = added(all_gu[t, x, c], g1[t])
+        net.got(g1.at[t], d_x + t)
+        all_gu[t, c, x] = added(all_gu[t, c, x], g1[t])
         source = z // 2 + 2 * t
         net.move(
-            jnp.logical_and(source == z, z % 2 == x),
-            all_gu.at[t, x, c],
-            g2.at[x],
+            jnp.logical_and(source == z, z % 2 == c),
+            all_gu.at[t, c, x],
+            g2.at[c],
             d_home + t,
-            d_home + x,
-            at(source, y, z % 2, c),
+            d_home + c,
+            at(source, y, x, z % 2),
         )
 
     class Collect:
@@ -1131,7 +1174,7 @@
         net.send(small.at[6], small.at[6 + k], r_s + 2 + k, z_peers[k])
     ins.cross(r_z + 1)
     outs.done(r_z, o_out)
-    net.got(n2, d_home + 2)
+    net.got(n2, d_y + 1)
     o_dn[...] = n2[...].astype(F32)[:BLOCK]
     for k in (1, 2, 3):
         net.got(small.at[6 + k], r_s + 2 + k)
@@ -1199,7 +1242,7 @@
     for count in (48, 32):
         scratch += [vm(2, 2, 2, count, D), vm(2, 2, count, D), vm(3, count, D)]
     scratch += [vm(2, 2, PADDED, D), vm(2, PADDED, D), vm(2, PADDED, D)]
-    scratch += [vm(2, PADDED, D), vm(PADDED, D), vm(PADDED, D)]
+    scratch += [vm(2, 2, PADDED, D), vm(2, PADDED, D), vm(PADDED, D), vm(PADDED, D)]
     scratch += [vf(10, 8, D)]
     scratch += [pltpu.SemaphoreType.DMA((2,))] + [pltpu.SemaphoreType.DMA((144,))] * 2
     return pl.pallas_call(

time: 310 us -> 277 us (0.89); the launches traced: 304 us -> 276 us
  Pallas kernels: 303 us -> 275 us
    pallas_call x1, Pallas kernels: 299 us -> 271 us  [whole_layer(): pl.pallas_call(layer_kernel, out_shape=(jax.ShapeDtypeStruct((2, 1, PART,...]
where the time goes in v4:
time: 277 us; the launch traced here: 276 us
  Pallas kernels  275 us (99%)
    pallas_call x1, Pallas kernels, whole_layer(): pl.pallas_call(layer_kernel, out_shape=(jax.ShapeDtypeStruct((2, 1, PART,...  271 us

profile of v4, /device:TPU:22, one launch (start us, length us, event | category | flops | bytes accessed | tf_op | source)
XLA Modules:
  0.0 276.2 jit_solution(7820418795667575683)
XLA Ops:
  0.6 271.3 %layer.1 = (bf16[2,1,64,1152]{3,2,1,0:T(8,128)(2,1)}, f32[2,1,64,1152]{3,2,1,0:T(8,128)}, f32[48,1152]{1,0:T(8,128)}, f32[32,1152]{1,0:T(8,128)}, f32[432,1152]{...) custom-call(bf16[2,1,64,1152]{3,2,1,0:T(8,128)(2,1)} %refs_0_.1, ...), custom_call_target="tpu_custom_call" | custom-call | tf_op jit(solution)/shard_map/layer/pallas_call | solution.py:1248
  271.9 0.0 copy-start
  271.9 3.7 %results.1 = (bf16[2,1,64,1152]{3,2,1,0:T(8,128)(2,1)}, f32[2,1,64,1152]{3,2,1,0:T(8,128)}, f32[48,1152]{1,0:T(8,128)}, f32[32,1152]{1,0:T(8,128)}, f32[432,1152...) custom-call(bf16[2,1,64,1152]{3,2,1,0:T(8,128)(2,1)} %get-tuple-element.26.refs_0_, ...), custom_call_target="tpu_custom_call" | custom-call | tf_op jit(solution)/shard_map/results/pallas_call | solution.py:1287
  275.7 0.0 copy-done
  275.7 0.5 copy.20
Async XLA Ops:
  271.9 3.8 %copy-start = (f32[4]{0:T(128)S(1)}, f32[4]{0:T(128)}, u32[]{:S(2)}) copy-start(f32[4]{0:T(128)} %get-tuple-element.60) | copy-start | bytes 52

commit v5 on v4

--- a/solution.py
+++ b/solution.py
@@ -605,8 +605,12 @@
             net.got(all_gu.at[t, 1 - c, 1 - x], w_d + which)
         net.got(all_dn.at[1 - c], v_c)
 
-    net.send(n0.at[0], n0.at[1], v_x, xp)
-    across_x = net.sent[-1]
+    across_x = []
+
+    def down_x():
+        net.send(n0.at[0], n0.at[1], v_x, xp)
+        across_x.append(net.sent[-1])
+
 
     def down_out():
         net.got(n0.at[1], v_x)
@@ -626,7 +630,6 @@
             net.got(all_dn.at[c, q], v_one + q)
         net.send(all_dn.at[c], all_dn.at[c], v_c, cp)
 
-    rows_out()
     into.hop(1)
     into.hop(2)
     outof.start()
@@ -658,23 +661,23 @@
     stream = stream_of(x_ref)
     normed_in[...] = norm_rows(stream, gains[0:1, :]).astype(LOW)
 
+    rows_out()
+    down_x()
     into.turn(2)
     outof.hop(1)
     outof.hop(2)
     into.turn(3)
-    down_out()
     into.near()
     outof.turn(0)
     outof.turn(1)
     outof.hop(3)
-    rows_on(0)
     into.far()
     outof.turn(2)
     outof.turn(3)
     outof.near()
-    rows_on(1)
     into.whole()
 
+    down_out()
     flat_in = all_in.reshape(HEADS * HD + 2 * HD, D)
     flat_out = all_out.reshape(HEADS * HD, D)
     half = HD // 2
@@ -700,7 +703,6 @@
         return carry
 
     lax.fori_loop(0, HEADS + 2, project, 0)
-    down_on()
     outof.far()
 
     def attend_head(j, carry):
@@ -715,7 +717,7 @@
         return carry
 
     lax.fori_loop(0, HEADS, attend_head, 0)
-    rows_across(0)
+    rows_on(0)
     outof.whole()
 
     attn_proj[...] = jnp.zeros((MINE, D), F32)
@@ -848,7 +850,7 @@
 
     def weights_here():
         net.settle_moves()
-        net.flush([across_x])
+        net.flush(across_x)
         rows_across(1)
         rows_whole()
 
@@ -878,17 +880,20 @@
 
     one, two = Half(0, 0, got_mid, forward_pairs), Half(0, 1, got_mid, forward_pairs)
     one.start()
+    rows_on(1)
+    rows_across(0)
+    down_on()
+    two.start()
     one.hop(1)
-    two.start()
+    two.hop(1)
     one.hop(2)
+    two.hop(2)
+    one.hop(3)
+    two.hop(3)
     weights_here()
     one.group(0)
-    two.hop(1)
-    one.hop(3)
-    two.hop(2)
     one.group(1)
     one.fold(0)
-    two.hop(3)
     two.group(0)
     one.fold(1)
     two.group(1)

time: 277 us -> 259 us (0.935)
  Pallas kernels: 275 us -> 255 us
    pallas_call x1, Pallas kernels: 271 us -> 251 us  [whole_layer(): pl.pallas_call(layer_kernel, out_shape=(jax.ShapeDtypeStruct((2, 1, PART,...]
where the time goes in v5:
time: 259 us; the launch traced here: 256 us
  Pallas kernels  255 us (98%)
    pallas_call x1, Pallas kernels, whole_layer(): pl.pallas_call(layer_kernel, out_shape=(jax.ShapeDtypeStruct((2, 1, PART,...  251 us

profile of v5, /device:TPU:22, one launch (start us, length us, event | category | flops | bytes accessed | tf_op | source)
XLA Modules:
  0.0 256.2 jit_solution(4360363522626344772)
XLA Ops:
  0.6 251.2 %layer.1 = (bf16[2,1,64,1152]{3,2,1,0:T(8,128)(2,1)}, f32[2,1,64,1152]{3,2,1,0:T(8,128)}, f32[48,1152]{1,0:T(8,128)}, f32[32,1152]{1,0:T(8,128)}, f32[432,1152]{...) custom-call(bf16[2,1,64,1152]{3,2,1,0:T(8,128)(2,1)} %refs_0_.1, ...), custom_call_target="tpu_custom_call" | custom-call | tf_op jit(solution)/shard_map/layer/pallas_call | solution.py:1253
  251.9 0.0 copy-start
  251.9 3.7 %results.1 = (bf16[2,1,64,1152]{3,2,1,0:T(8,128)(2,1)}, f32[2,1,64,1152]{3,2,1,0:T(8,128)}, f32[48,1152]{1,0:T(8,128)}, f32[32,1152]{1,0:T(8,128)}, f32[432,1152...) custom-call(bf16[2,1,64,1152]{3,2,1,0:T(8,128)(2,1)} %get-tuple-element.26.refs_0_, ...), custom_call_target="tpu_custom_call" | custom-call | tf_op jit(solution)/shard_map/results/pallas_call | solution.py:1292
  255.6 0.0 copy-done
  255.6 0.5 copy.20
Async XLA Ops:
  251.9 3.8 %copy-start = (f32[4]{0:T(128)S(1)}, f32[4]{0:T(128)}, u32[]{:S(2)}) copy-start(f32[4]{0:T(128)} %get-tuple-element.60) | copy-start | bytes 52

commit v6 on v5

--- a/solution.py
+++ b/solution.py
@@ -331,15 +331,16 @@
     return 3 - z
 
 
-def greet_all(me):
+def greet(z, y, x, c):
     barrier = pltpu.get_barrier_semaphore()
-
-    def one(step, carry):
-        pl.semaphore_signal(barrier, inc=1, device_id=((me + step) % 32,), device_id_type=MESH)
-        return carry
-
-    lax.fori_loop(1, 32, one, 0)
-    pl.semaphore_wait(barrier, 31)
+    others = [at(z_peer(z, k), y, x, core) for k in (1, 2, 3) for core in (c, 1 - c)]
+    others.append(at(z, y, x, 1 - c))
+    for k in range(2):
+        for there_y, there_x in ((1 - y, x), (y, 1 - x), (1 - y, 1 - x)):
+            others.append(at(z_peer(z, k), there_y, there_x, c))
+    for device in others:
+        pl.semaphore_signal(barrier, inc=1, device_id=(device,), device_id_type=MESH)
+    pl.semaphore_wait(barrier, len(others))
 
 
 def nt(left, right):
@@ -513,7 +514,7 @@
     keep_out = pltpu.make_async_copy(aout, all_out.at[z, y, x, c], local.at[1])
     keep_in.start()
     keep_out.start()
-    greet_all(me)
+    greet(z, y, x, c)
 
     class Spread:
         def __init__(self, own, full, x_first):
@@ -969,10 +970,36 @@
             all_gu[t, c, q] = added(all_gu[t, c, q], g0[t, q])
         net.send(all_gu.at[t, c, 1 - x], g1.at[t], d_x + t, xp)
 
+    def home_down():
+        net.got(n1, d_y)
+        d_dn[c, kept] = added(d_dn[c, kept], n1[...])
+        net.move(
+            jnp.logical_and(z % 2 == y, x == y),
+            d_dn.at[c, kept],
+            n2,
+            d_y + 1,
+            d_y + 1,
+            at(2 * (z // 2) + y, kept, z % 2, c),
+        )
+
+    def home_gate_up(t):
+        net.got(g1.at[t], d_x + t)
+        all_gu[t, c, x] = added(all_gu[t, c, x], g1[t])
+        source = z // 2 + 2 * t
+        net.move(
+            jnp.logical_and(source == z, z % 2 == c),
+            all_gu.at[t, c, x],
+            g2.at[c],
+            d_home + t,
+            d_home + c,
+            at(source, y, x, z % 2),
+        )
+
     share(0)
     share(1)
     four.done()
 
+    home_down()
     mid = middle[...]
     grad, gain_grad = norm_back(mid, gains[2:3, :], total[...].reshape(MINE, D))
     small[0, 2:3, :] = gain_grad
@@ -994,33 +1021,9 @@
     lax.fori_loop(0, HEADS, out_grads, 0)
     net.send(d_out.at[:, :, :, 1 - c], b0, d_c + 3, cp)
 
-    def home_down():
-        net.got(n1, d_y)
-        d_dn[c, kept] = added(d_dn[c, kept], n1[...])
-        net.move(
-            jnp.logical_and(z % 2 == y, x == y),
-            d_dn.at[c, kept],
-            n2,
-            d_y + 1,
-            d_y + 1,
-            at(2 * (z // 2) + y, kept, z % 2, c),
-        )
-
-    def home_gate_up(t):
-        net.got(g1.at[t], d_x + t)
-        all_gu[t, c, x] = added(all_gu[t, c, x], g1[t])
-        source = z // 2 + 2 * t
-        net.move(
-            jnp.logical_and(source == z, z % 2 == c),
-            all_gu.at[t, c, x],
-            g2.at[c],
-            d_home + t,
-            d_home + c,
-            at(source, y, x, z % 2),
-        )
-
     class Collect:
-        def __init__(self, grads, core_in, y_in, x_in, z_in, core_slot):
+        def __init__(self, grads, core_in, y_in, x_in, z_in, core_slot, y_first):
+            self.y_first = y_first
             self.grads, self.core_in, self.y_in, self.x_in, self.z_in = (
                 grads,
                 core_in,
@@ -1041,9 +1044,11 @@
 
                 lax.fori_loop(0, 8, one, 0)
                 both = pl.ds(2 * pair, 2)
-                net.send(
-                    self.grads.at[both, 1 - y, :, c], self.y_in.at[part], self.ys + part, yp
-                )
+                if self.y_first:
+                    away, device = self.grads.at[both, 1 - y, :, c], yp
+                else:
+                    away, device = self.grads.at[both, :, 1 - x, c], xp
+                net.send(away, self.y_in.at[part], self.ys + part, device)
 
         def ys_in(self, part):
             pair = (1 - zh, zh)[part]
@@ -1052,18 +1057,23 @@
             def one(i, carry):
                 p, q = i // 2, i % 2
                 there = 2 * pair + p
-                self.grads[there, y, q, c] = added(
-                    self.grads[there, y, q, c], self.y_in[part, p, q]
-                )
+                if self.y_first:
+                    self.grads[there, y, q, c] = added(
+                        self.grads[there, y, q, c], self.y_in[part, p, q]
+                    )
+                else:
+                    self.grads[there, q, x, c] = added(
+                        self.grads[there, q, x, c], self.y_in[part, p, q]
+                    )
                 return carry
 
             lax.fori_loop(0, 4, one, 0)
-            net.send(
-                self.grads.at[pl.ds(2 * pair, 2), y, 1 - x, c],
-                self.x_in.at[part],
-                self.xs + part,
-                xp,
-            )
+            both = pl.ds(2 * pair, 2)
+            if self.y_first:
+                away, device = self.grads.at[both, y, 1 - x, c], xp
+            else:
+                away, device = self.grads.at[both, 1 - y, x, c], yp
+            net.send(away, self.x_in.at[part], self.xs + part, device)
 
         def xs_in(self, part):
             pair = (1 - zh, zh)[part]
@@ -1096,8 +1106,8 @@
             )
 
     r_s, r_z = net.slots(8), net.slots(2)
-    outs = Collect(d_out, b0, b1, b2, b3, d_c + 3)
-    ins = Collect(d_in, a0, a1, a2, a3, d_c + 4)
+    outs = Collect(d_out, b0, b1, b2, b3, d_c + 3, False)
+    ins = Collect(d_in, a0, a1, a2, a3, d_c + 4, True)
 
     grad_heads[...] = jnp.zeros((6, MINE, HD), F32)
 
@@ -1143,27 +1153,26 @@
 
     lax.fori_loop(0, HEADS + 2, in_grads, 0)
     net.send(d_in.at[:, :, :, 1 - c], a0, d_c + 4, cp)
-    home_down()
     total[...] = jnp.zeros((2, PART, D), F32)
 
     def in_back(j, carry):
         total[...] += nn(grad_proj[j], flat_in[rows_of(j), :]).reshape(2, PART, D)
         return carry
 
+    home_gate_up(0)
     lax.fori_loop(0, HEADS + 2, in_back, 0)
     ins.cores()
     grad, gain_grad = norm_back(stream_of(x_ref), gains[0:1, :], total[...].reshape(MINE, D))
     small[0, 0:1, :] = gain_grad
     input_grad[...] = (grad_middle[...] + grad).reshape(2, 1, PART, D)
     net.send(small.at[0], small.at[1], r_s, cp)
-    home_gate_up(0)
+    home_gate_up(1)
     outs.ys_in(0)
     outs.ys_in(1)
     net.got(small.at[1], r_s)
     small[2] = small[0] + small[1]
     net.send(small.at[2], small.at[3], r_s + 1, xp)
     ins.ys_in(0)
-    home_gate_up(1)
     outs.xs_in(0)
     outs.xs_in(1)
     net.got(small.at[3], r_s + 1)

time: 259 us -> 254 us (0.981)
  Pallas kernels: 255 us -> 249 us
    pallas_call x1, Pallas kernels: 251 us -> 245 us  [whole_layer(): pl.pallas_call(layer_kernel, out_shape=(jax.ShapeDtypeStruct((2, 1, PART,...]
where the time goes in v6:
time: 254 us; the launch traced here: 250 us
  Pallas kernels  249 us (98%)
    pallas_call x1, Pallas kernels, whole_layer(): pl.pallas_call(layer_kernel, out_shape=(jax.ShapeDtypeStruct((2, 1, PART,...  245 us

profile of v6, /device:TPU:22, one launch (start us, length us, event | category | flops | bytes accessed | tf_op | source)
XLA Modules:
  0.0 250.1 jit_solution(4621644972724623356)
XLA Ops:
  0.6 245.1 %layer.1 = (bf16[2,1,64,1152]{3,2,1,0:T(8,128)(2,1)}, f32[2,1,64,1152]{3,2,1,0:T(8,128)}, f32[48,1152]{1,0:T(8,128)}, f32[32,1152]{1,0:T(8,128)}, f32[432,1152]{...) custom-call(bf16[2,1,64,1152]{3,2,1,0:T(8,128)(2,1)} %refs_0_.1, ...), custom_call_target="tpu_custom_call" | custom-call | tf_op jit(solution)/shard_map/layer/pallas_call | solution.py:1262
  245.8 0.0 copy-start
  245.8 3.7 %results.1 = (bf16[2,1,64,1152]{3,2,1,0:T(8,128)(2,1)}, f32[2,1,64,1152]{3,2,1,0:T(8,128)}, f32[48,1152]{1,0:T(8,128)}, f32[32,1152]{1,0:T(8,128)}, f32[432,1152...) custom-call(bf16[2,1,64,1152]{3,2,1,0:T(8,128)(2,1)} %get-tuple-element.26.refs_0_, ...), custom_call_target="tpu_custom_call" | custom-call | tf_op jit(solution)/shard_map/results/pallas_call | solution.py:1301
  249.5 0.0 copy-done
  249.5 0.5 copy.20
Async XLA Ops:
  245.8 3.8 %copy-start = (f32[4]{0:T(128)S(1)}, f32[4]{0:T(128)}, u32[]{:S(2)}) copy-start(f32[4]{0:T(128)} %get-tuple-element.60) | copy-start | bytes 52

commit v7 on v6

--- a/solution.py
+++ b/solution.py
@@ -1106,7 +1106,7 @@
             )
 
     r_s, r_z = net.slots(8), net.slots(2)
-    outs = Collect(d_out, b0, b1, b2, b3, d_c + 3, False)
+    outs = Collect(d_out, b0, b1, b2, b3, d_c + 3, True)
     ins = Collect(d_in, a0, a1, a2, a3, d_c + 4, True)
 
     grad_heads[...] = jnp.zeros((6, MINE, HD), F32)
@@ -1122,6 +1122,7 @@
         grad_heads[HEADS] += tn(grad_score, heads[j]) * SCALE_FACTOR
         return carry
 
+    outs.cores()
     lax.fori_loop(0, HEADS, head_back, 0)
     key_acc[...] = jnp.zeros((2, HD), F32)
 
@@ -1145,7 +1146,6 @@
     small[0, 4:5, 0:HD] = key_acc[0:1, :]
     small[0, 4:5, HD : 2 * HD] = key_acc[1:2, :]
 
-    outs.cores()
 
     def in_grads(j, carry):
         flat_d_in[rows_of(j), :] = tn(grad_proj[j], normed_in[...]).astype(LOW)

time: 254 us -> 252 us (level); the launches traced: 250 us -> 252 us
  no operation moved by 1% of the time
where the time goes in v7:
time: 252 us
  Pallas kernels  251 us (100%)
    pallas_call x1, Pallas kernels, whole_layer(): pl.pallas_call(layer_kernel, out_shape=(jax.ShapeDtypeStruct((2, 1, PART,...  247 us

profile of v7, /device:TPU:22, one launch (start us, length us, event | category | flops | bytes accessed | tf_op | source)
XLA Modules:
  0.0 251.8 jit_solution(8804042598848896795)
XLA Ops:
  0.6 246.9 %layer.1 = (bf16[2,1,64,1152]{3,2,1,0:T(8,128)(2,1)}, f32[2,1,64,1152]{3,2,1,0:T(8,128)}, f32[48,1152]{1,0:T(8,128)}, f32[32,1152]{1,0:T(8,128)}, f32[432,1152]{...) custom-call(bf16[2,1,64,1152]{3,2,1,0:T(8,128)(2,1)} %refs_0_.1, ...), custom_call_target="tpu_custom_call" | custom-call | tf_op jit(solution)/shard_map/layer/pallas_call | solution.py:1262
  247.5 0.0 copy-start
  247.5 3.7 %results.1 = (bf16[2,1,64,1152]{3,2,1,0:T(8,128)(2,1)}, f32[2,1,64,1152]{3,2,1,0:T(8,128)}, f32[48,1152]{1,0:T(8,128)}, f32[32,1152]{1,0:T(8,128)}, f32[432,1152...) custom-call(bf16[2,1,64,1152]{3,2,1,0:T(8,128)(2,1)} %get-tuple-element.26.refs_0_, ...), custom_call_target="tpu_custom_call" | custom-call | tf_op jit(solution)/shard_map/results/pallas_call | solution.py:1301
  251.3 0.0 copy-done
  251.3 0.5 copy.20
Async XLA Ops:
  247.5 3.8 %copy-start = (f32[4]{0:T(128)S(1)}, f32[4]{0:T(128)}, u32[]{:S(2)}) copy-start(f32[4]{0:T(128)} %get-tuple-element.60) | copy-start | bytes 52

commit v8 on v7

--- a/solution.py
+++ b/solution.py
@@ -571,8 +571,9 @@
     v_x, v_one, v_c = net.slots(1), net.slots(2), net.slots(1)
     kind, goal = z // 2, 2 * (z % 2) + c
     blank = jnp.zeros((PADDED - BLOCK, D), F32)
+    both_parts = gu[...].astype(F32)
     for h in range(2):
-        part = gu[pl.ds(h * BLOCK, BLOCK), :].astype(F32)
+        part = both_parts[h * BLOCK : (h + 1) * BLOCK]
         g0[0, h] = jnp.concatenate([part, blank], 0).astype(LOW)
     n0[0] = jnp.concatenate([dn[...].astype(F32), blank], 0).astype(LOW)
 

time: 252 us -> 252 us (level)
  no operation moved by 1% of the time
where the time goes in v8:
time: 252 us
  Pallas kernels  251 us (100%)
    pallas_call x1, Pallas kernels, whole_layer(): pl.pallas_call(layer_kernel, out_shape=(jax.ShapeDtypeStruct((2, 1, PART,...  247 us

profile of v8, /device:TPU:22, one launch (start us, length us, event | category | flops | bytes accessed | tf_op | source)
XLA Modules:
  0.0 251.8 jit_solution(8804042598848896795)
XLA Ops:
  0.6 246.9 %layer.1 = (bf16[2,1,64,1152]{3,2,1,0:T(8,128)(2,1)}, f32[2,1,64,1152]{3,2,1,0:T(8,128)}, f32[48,1152]{1,0:T(8,128)}, f32[32,1152]{1,0:T(8,128)}, f32[432,1152]{...) custom-call(bf16[2,1,64,1152]{3,2,1,0:T(8,128)(2,1)} %refs_0_.1, ...), custom_call_target="tpu_custom_call" | custom-call | tf_op jit(solution)/shard_map/layer/pallas_call | solution.py:1263
  247.5 0.0 copy-start
  247.5 3.7 %results.1 = (bf16[2,1,64,1152]{3,2,1,0:T(8,128)(2,1)}, f32[2,1,64,1152]{3,2,1,0:T(8,128)}, f32[48,1152]{1,0:T(8,128)}, f32[32,1152]{1,0:T(8,128)}, f32[432,1152...) custom-call(bf16[2,1,64,1152]{3,2,1,0:T(8,128)(2,1)} %get-tuple-element.26.refs_0_, ...), custom_call_target="tpu_custom_call" | custom-call | tf_op jit(solution)/shard_map/results/pallas_call | solution.py:1302
  251.3 0.0 copy-done
  251.3 0.5 copy.20
Async XLA Ops:
  247.5 3.8 %copy-start = (f32[4]{0:T(128)S(1)}, f32[4]{0:T(128)}, u32[]{:S(2)}) copy-start(f32[4]{0:T(128)} %get-tuple-element.60) | copy-start | bytes 52

commit v9 on v8

--- a/solution.py
+++ b/solution.py
@@ -895,8 +895,8 @@
     weights_here()
     one.group(0)
     one.group(1)
+    two.group(0)
     one.fold(0)
-    two.group(0)
     one.fold(1)
     two.group(1)
     one.cross()

time: 252 us -> 252 us (level)
  no operation moved by 1% of the time
where the time goes in v9:
time: 252 us
  Pallas kernels  251 us (100%)
    pallas_call x1, Pallas kernels, whole_layer(): pl.pallas_call(layer_kernel, out_shape=(jax.ShapeDtypeStruct((2, 1, PART,...  247 us

profile of v9, /device:TPU:22, one launch (start us, length us, event | category | flops | bytes accessed | tf_op | source)
XLA Modules:
  0.0 251.8 jit_solution(16334759136396228545)
XLA Ops:
  0.6 246.9 %layer.1 = (bf16[2,1,64,1152]{3,2,1,0:T(8,128)(2,1)}, f32[2,1,64,1152]{3,2,1,0:T(8,128)}, f32[48,1152]{1,0:T(8,128)}, f32[32,1152]{1,0:T(8,128)}, f32[432,1152]{...) custom-call(bf16[2,1,64,1152]{3,2,1,0:T(8,128)(2,1)} %refs_0_.1, ...), custom_call_target="tpu_custom_call" | custom-call | tf_op jit(solution)/shard_map/layer/pallas_call | solution.py:1263
  247.6 0.0 copy-start
  247.6 3.7 %results.1 = (bf16[2,1,64,1152]{3,2,1,0:T(8,128)(2,1)}, f32[2,1,64,1152]{3,2,1,0:T(8,128)}, f32[48,1152]{1,0:T(8,128)}, f32[32,1152]{1,0:T(8,128)}, f32[432,1152...) custom-call(bf16[2,1,64,1152]{3,2,1,0:T(8,128)(2,1)} %get-tuple-element.26.refs_0_, ...), custom_call_target="tpu_custom_call" | custom-call | tf_op jit(solution)/shard_map/results/pallas_call | solution.py:1302
  251.3 0.0 copy-done
  251.3 0.5 copy.20
Async XLA Ops:
  247.6 3.8 %copy-start = (f32[4]{0:T(128)S(1)}, f32[4]{0:T(128)}, u32[]{:S(2)}) copy-start(f32[4]{0:T(128)} %get-tuple-element.60) | copy-start | bytes 52
